TPU v7x, 256 devices: a whole 4x4x8 slice. The times are simulated.
256 devices in a mesh: ctx: 16 (over x, z_lo), tp: 16 (over z_hi, y, core).
Axes of the slice: x: 4, y: 4, z: 8 (z_hi: 2, z_lo: 4; z = z_hi * 4 + z_lo), core: 2. Of those that a mesh axis runs over, the one named last changes fastest.
Arguments:
- tokens: bfloat16 [16384, 2048], P('ctx', 'tp'), may hold values from -600 to 600
- gain: bfloat16 [2048], P('tp'), may hold values from 0.25 to 1.75
- w_inputs: bfloat16 [2048, 2048], P(None, 'tp'), may hold values from -0.125 to 0.125
- filters: float32 [24, 16384], P(None, 'ctx'), may hold values from -0.078125 to 0.078125
- w_plus: bfloat16 [24, 2048], P(None, 'tp'), may hold values from -1.25 to 1.25
- w_minus: bfloat16 [24, 2048], P(None, 'tp'), may hold values from -1.25 to 1.25
Outputs:
- mixed: bfloat16 [16384, 2048], P('ctx', 'tp')
All inputs are finite; a program needn't handle non-finite values.
Results may differ from a plain program's by a relative error of at most 0.0049.
Values may be sent and summed in bfloat16 or wider, within the bound.
No kernel may reach another device: no remote copies, remote signals or barrier semaphores. Data moves between devices by JAX's collectives and lax.ppermute only.
A program may use at most 64 MiB of HBM per device.

v0:
```python
import math

import jax
import jax.numpy as jnp
from jax import lax
from jax.sharding import PartitionSpec as P

EPS = 1e-05
TWO_PI = 2.0 * math.pi
HIGHEST = lax.Precision.HIGHEST


def phases(lead_ids, other_ids, period):
    return (lead_ids[:, None] * other_ids[None, :] % period).astype(jnp.float32) * (TWO_PI / period)


def transform_rows(real_part, imag_part, direction):
    row_count = real_part.shape[0]
    flat_width = real_part.shape[1] * real_part.shape[2]
    stacked = jnp.concatenate(
        [real_part.reshape(row_count, flat_width), imag_part.reshape(row_count, flat_width)], axis=1
    )
    segment = min(256, row_count)
    columns = lax.iota(jnp.int32, row_count)

    def one_segment(offset):
        outputs = offset + lax.iota(jnp.int32, segment)
        table = phases(outputs, columns, row_count)
        cosine = jnp.dot(jnp.cos(table), stacked, precision=HIGHEST)
        sine = jnp.dot(jnp.sin(table), stacked, precision=HIGHEST)
        out_real = cosine[:, :flat_width] + direction * sine[:, flat_width:]
        out_imag = cosine[:, flat_width:] - direction * sine[:, :flat_width]
        return (out_real, out_imag)

    offsets = lax.iota(jnp.int32, row_count // segment) * segment
    out_real, out_imag = lax.map(one_segment, offsets)
    return (out_real.reshape(real_part.shape), out_imag.reshape(real_part.shape))


def forward(lead_block, other_block):
    devices = lax.axis_size("ctx")
    position = lax.axis_index("ctx")
    row_count = lead_block.shape[0]
    share_rows = row_count // devices
    period = 2 * row_count * devices
    lead_cols, other_cols = (
        lax.all_to_all(
            lead_block.reshape(1, row_count, lead_block.shape[1]),
            "ctx",
            split_axis=1,
            concat_axis=0,
            tiled=True,
        ),
        lax.all_to_all(
            other_block.reshape(1, row_count, other_block.shape[1]),
            "ctx",
            split_axis=1,
            concat_axis=0,
            tiled=True,
        ),
    )
    frequency = lax.iota(jnp.int32, 2 * devices)
    block_ids = lax.iota(jnp.int32, devices)
    outer = phases(frequency, block_ids, 2 * devices)
    outer_cos = jnp.cos(outer)
    outer_sin = jnp.sin(outer)
    local_ids = position * share_rows + lax.iota(jnp.int32, share_rows)
    twiddle = phases(local_ids, frequency, period)
    twiddle_cos = jnp.cos(twiddle)[:, :, None]
    twiddle_sin = jnp.sin(twiddle)[:, :, None]

    def mix_blocks(gathered):
        sum_real = jnp.einsum("kn,nrc->rkc", outer_cos, gathered, precision=HIGHEST)
        sum_imag = -jnp.einsum("kn,nrc->rkc", outer_sin, gathered, precision=HIGHEST)
        return (
            sum_real * twiddle_cos + sum_imag * twiddle_sin,
            sum_imag * twiddle_cos - sum_real * twiddle_sin,
        )

    lead_real, lead_imag = mix_blocks(lead_cols)
    other_real, other_imag = mix_blocks(other_cols)
    lead_real, lead_imag, other_real, other_imag = (
        lax.all_to_all(lead_real, "ctx", split_axis=1, concat_axis=0, tiled=True),
        lax.all_to_all(lead_imag, "ctx", split_axis=1, concat_axis=0, tiled=True),
        lax.all_to_all(other_real, "ctx", split_axis=1, concat_axis=0, tiled=True),
        lax.all_to_all(other_imag, "ctx", split_axis=1, concat_axis=0, tiled=True),
    )
    return (transform_rows(lead_real, lead_imag, 1.0), transform_rows(other_real, other_imag, 1.0))


def inverse(real_part, imag_part):
    devices = lax.axis_size("ctx")
    position = lax.axis_index("ctx")
    row_count = real_part.shape[0]
    share_rows = row_count // devices
    period = 2 * row_count * devices
    back_real, back_imag = transform_rows(real_part, imag_part, -1.0)
    back_real, back_imag = (
        lax.all_to_all(back_real, "ctx", split_axis=0, concat_axis=1, tiled=True),
        lax.all_to_all(back_imag, "ctx", split_axis=0, concat_axis=1, tiled=True),
    )
    frequency = lax.iota(jnp.int32, 2 * devices)
    block_ids = lax.iota(jnp.int32, devices)
    local_ids = position * share_rows + lax.iota(jnp.int32, share_rows)
    twiddle = phases(local_ids, frequency, period)
    twiddle_cos = jnp.cos(twiddle)[:, :, None]
    twiddle_sin = jnp.sin(twiddle)[:, :, None]
    turned_real = back_real * twiddle_cos - back_imag * twiddle_sin
    turned_imag = back_imag * twiddle_cos + back_real * twiddle_sin
    inverse_phase = phases(block_ids, frequency, 2 * devices)
    result = jnp.einsum("nk,rkc->nrc", jnp.cos(inverse_phase), turned_real, precision=HIGHEST)
    result = result - jnp.einsum(
        "nk,rkc->nrc", jnp.sin(inverse_phase), turned_imag, precision=HIGHEST
    )
    result = result / period
    result = lax.all_to_all(
        result.astype(jnp.bfloat16), "ctx", split_axis=0, concat_axis=1, tiled=True
    ).astype(result.dtype)
    return result.reshape(row_count, result.shape[2])


def on_device(tokens, gain, w_inputs, filters, w_plus, w_minus):
    row_count = tokens.shape[0]
    full_width = tokens.shape[1] * lax.axis_size("tp")
    tok_values = tokens.astype(jnp.float32)
    row_power = lax.psum(jnp.sum(tok_values * tok_values, axis=1), "tp")
    scaled = (tok_values * gain.astype(jnp.float32)).astype(jnp.bfloat16)
    product = jnp.dot(
        lax.all_gather(scaled, "tp", axis=1, tiled=True),
        w_inputs,
        preferred_element_type=jnp.float32,
    )
    scale = lax.rsqrt(row_power / full_width + EPS)
    projected = product * scale[:, None]
    plus_weights = w_plus.astype(jnp.float32)
    minus_weights = w_minus.astype(jnp.float32)
    lag_sign = 1.0 - 2.0 * (lax.iota(jnp.int32, row_count) % 2).astype(jnp.float32)
    response = jnp.einsum("kt,kc->tc", filters, plus_weights, precision=HIGHEST)
    response = response + lag_sign[:, None] * jnp.einsum(
        "kt,kc->tc", filters, minus_weights, precision=HIGHEST
    )
    signal, spectrum = forward(projected, response)
    filt_real, filt_imag = spectrum
    sig_real, sig_imag = signal
    prod_real = sig_real * filt_real - sig_imag * filt_imag
    prod_imag = sig_real * filt_imag + sig_imag * filt_real
    mixed = inverse(prod_real, prod_imag)
    return mixed.astype(jnp.bfloat16)


def solution(mesh):
    in_specs = (
        P("ctx", "tp"),
        P("tp"),
        P(None, "tp"),
        P(None, "ctx"),
        P(None, "tp"),
        P(None, "tp"),
    )
    out_specs = P("ctx", "tp")
    return jax.shard_map(
        on_device, mesh=mesh, in_specs=in_specs, out_specs=out_specs, check_vma=False
    )
```

profile of v0, /device:TPU:8, one launch (start us, length us, event | category | flops | bytes accessed | tf_op | source)
XLA Modules:
  0.0 522.0 jit_solution(14017675002344416610)
XLA Ops:
  12.9 8.5 %all-to-all-start.3 = ((f32[1,1024,128]{2,0,1:T(1,128)}), f32[1,1024,128]{2,0,1:T(1,128)S(1)}, u32[]{:S(2)}, u32[]{:S(2)}) async-start(f32[1,1024,128]{2,0,1:T(1,128)} %bitcast.13), calls=%async_computation.3 | async-start | bytes 1048576 | tf_op jit(solution)/shard_map/all_to_all | solution.py:54
  21.4 44.6 %psum.7 = f32[1024]{0:T(1024)S(1)} all-reduce(f32[1024]{0:T(1024)S(1)} %get-tuple-element.326), channel_id=1, replica_groups=mesh['ctx'=16,'tp'=16] {'tp'}, use_global_device_ids=true, to_apply=%region_1.0 | all-reduce | flops 1024 | bytes 8192 | tf_op jit(solution)/shard_map/psum | solution.py:126
  66.0 28.4 %all-gather.2.cloned.1.call-done = bf16[1024,2048]{1,0:T(8,128)(2,1)} async-done(((bf16[1024,128]{1,0:T(8,128)(2,1)}), bf16[1024,2048]{1,0:T(8,128)(2,1)}) %all-gather.2.cloned.1.call-update) | async-done | bytes 4194320 | tf_op jit(solution)/shard_map/all_gather | solution.py:129
  107.3 13.2 %all-to-all-done = f32[1,1024,128]{2,0,1:T(1,128)S(1)} async-done(((f32[1,1024,128]{2,0,1:T(1,128)}), f32[1,1024,128]{2,0,1:T(1,128)S(1)}, u32[]{:S(2)}, u32[]{:S(2)}) %all-to-all-start) | async-done | bytes 524320 | tf_op jit(solution)/shard_map/all_to_all | solution.py:47
  133.7 24.1 %all-to-all-done.4 = f32[64,32,128]{2,0,1:T(8,128)} async-done(((f32[64,32,128]{2,0,1:T(8,128)}), f32[64,32,128]{2,0,1:T(8,128)}, u32[]{:S(2)}, u32[]{:S(2)}) %all-to-all-start.4) | async-done | bytes 1048608 | tf_op jit(solution)/shard_map/all_to_all | solution.py:85
  163.8 25.6 %all-to-all-done.5 = f32[64,32,128]{2,0,1:T(8,128)} async-done(((f32[64,32,128]{2,0,1:T(8,128)}), f32[64,32,128]{2,0,1:T(8,128)}, u32[]{:S(2)}, u32[]{:S(2)}) %all-to-all-start.5) | async-done | bytes 1048608 | tf_op jit(solution)/shard_map/all_to_all | solution.py:86
  201.0 20.0 %all-to-all-done.1 = f32[64,32,128]{2,0,1:T(8,128)S(1)} async-done(((f32[64,32,128]{2,0,1:T(8,128)}), f32[64,32,128]{2,0,1:T(8,128)S(1)}, u32[]{:S(2)}, u32[]{:S(2)}) %all-to-all-start.1) | async-done | bytes 1048608 | tf_op jit(solution)/shard_map/all_to_all | solution.py:83
  230.4 62.2 %while.46 = (s32[]{:T(128)}, f32[4,256,256]{2,1,0:T(8,128)}, f32[4,256,256]{2,1,0:T(8,128)}, s32[4]{0:T(128)S(1)}, f32[1024,512]{1,0:T(8,128)}, /*index=5*/s32[]{:T(128)}) while((s32[]{:T(128)}, f32[4,256,256]{2,1,0:T(8,128)}, f32[4,256,256]{2,1,0:T(8,128)}, s32[4]{0:T(128)S(1)}, f32[1024,512]{1,0:T(8,128)}, ...), condition=%wide.region_5.6_spmd.clone, body=%wide.region_4.5_spmd.clone.sunk | while | flops 3228696832 | bytes 15208049 | solution.py:36
  231.7 7.6 %fusion.217 = f32[256,512]{1,0:T(8,128)S(1)} fusion(f32[1024,512]{1,0:T(8,128)} %get-tuple-element.475, s32[256]{0:T(256)S(1)} %iota_add_fusion.8), kind=kOutput, calls=%fused_computation.41.clone.1 | convolution fusion | flops 1614282752 | bytes 2622464 | tf_op jit(solution)/shard_map/while/body/eval_jaxpr/dot_general | solution.py:30
  262.7 7.6 %fusion.217 = f32[256,512]{1,0:T(8,128)S(1)} fusion(f32[1024,512]{1,0:T(8,128)} %get-tuple-element.475, s32[256]{0:T(256)S(1)} %iota_add_fusion.8), kind=kOutput, calls=%fused_computation.41.clone.1 | convolution fusion | flops 1614282752 | bytes 2622464 | tf_op jit(solution)/shard_map/while/body/eval_jaxpr/dot_general | solution.py:30
  278.3 7.6 %fusion.217 = f32[256,512]{1,0:T(8,128)S(1)} fusion(f32[1024,512]{1,0:T(8,128)} %get-tuple-element.475, s32[256]{0:T(256)S(1)} %iota_add_fusion.8), kind=kOutput, calls=%fused_computation.41.clone.1 | convolution fusion | flops 1614282752 | bytes 2622464 | tf_op jit(solution)/shard_map/while/body/eval_jaxpr/dot_general | solution.py:30
  295.8 68.2 %while.45 = (s32[]{:T(128)}, f32[4,256,256]{2,1,0:T(8,128)S(1)}, f32[4,256,256]{2,1,0:T(8,128)S(1)}, s32[4]{0:T(128)S(1)}, f32[1024,512]{1,0:T(8,128)}, /*index=5*/s32[]{:T(128)}) while((s32[]{:T(128)}, f32[4,256,256]{2,1,0:T(8,128)S(1)}, f32[4,256,256]{2,1,0:T(8,128)S(1)}, s32[4]{0:T(128)S(1)}, f32[1024,512]{1,0:T(8,128)}, ...), condition=%wide.region_3.4_spmd.clone, body=%wide.region_2.3_spmd.clone.sunk | while | flops 3228696832 | bytes 15207541 | solution.py:36
  306.0 7.6 %fusion.210 = f32[256,512]{1,0:T(8,128)S(1)} fusion(f32[1024,512]{1,0:T(8,128)} %get-tuple-element.457, s32[256]{0:T(256)S(1)} %iota_add_fusion.7), kind=kOutput, calls=%fused_computation.12.clone.1 | convolution fusion | flops 1614282752 | bytes 2622464 | tf_op jit(solution)/shard_map/while/body/eval_jaxpr/dot_general | solution.py:30
  320.8 7.6 %fusion.210 = f32[256,512]{1,0:T(8,128)S(1)} fusion(f32[1024,512]{1,0:T(8,128)} %get-tuple-element.457, s32[256]{0:T(256)S(1)} %iota_add_fusion.7), kind=kOutput, calls=%fused_computation.12.clone.1 | convolution fusion | flops 1614282752 | bytes 2622464 | tf_op jit(solution)/shard_map/while/body/eval_jaxpr/dot_general | solution.py:30
  335.7 7.6 %fusion.210 = f32[256,512]{1,0:T(8,128)S(1)} fusion(f32[1024,512]{1,0:T(8,128)} %get-tuple-element.457, s32[256]{0:T(256)S(1)} %iota_add_fusion.7), kind=kOutput, calls=%fused_computation.12.clone.1 | convolution fusion | flops 1614282752 | bytes 2622464 | tf_op jit(solution)/shard_map/while/body/eval_jaxpr/dot_general | solution.py:30
  350.6 7.6 %fusion.210 = f32[256,512]{1,0:T(8,128)S(1)} fusion(f32[1024,512]{1,0:T(8,128)} %get-tuple-element.457, s32[256]{0:T(256)S(1)} %iota_add_fusion.7), kind=kOutput, calls=%fused_computation.12.clone.1 | convolution fusion | flops 1614282752 | bytes 2622464 | tf_op jit(solution)/shard_map/while/body/eval_jaxpr/dot_general | solution.py:30
  367.7 59.9 %while.47 = (s32[]{:T(128)}, f32[4,256,256]{2,1,0:T(8,128)S(1)}, f32[4,256,256]{2,1,0:T(8,128)S(1)}, s32[4]{0:T(128)S(1)}, f32[1024,512]{1,0:T(8,128)}, /*index=5*/s32[]{:T(128)}) while((s32[]{:T(128)}, f32[4,256,256]{2,1,0:T(8,128)S(1)}, f32[4,256,256]{2,1,0:T(8,128)S(1)}, s32[4]{0:T(128)S(1)}, f32[1024,512]{1,0:T(8,128)}, ...), condition=%wide.region_7.8_spmd.clone, body=%wide.region_6.7_spmd.clone.sunk | while | flops 3228827904 | bytes 15207541 | solution.py:36
  369.3 7.6 %fusion.224 = f32[256,512]{1,0:T(8,128)S(1)} fusion(f32[1024,512]{1,0:T(8,128)} %get-tuple-element.493, s32[256]{0:T(256)S(1)} %iota_add_fusion.9), kind=kOutput, calls=%fused_computation.70.clone.1 | convolution fusion | flops 1614282752 | bytes 2622464 | tf_op jit(solution)/shard_map/while/body/eval_jaxpr/dot_general | solution.py:30
  384.2 7.6 %fusion.224 = f32[256,512]{1,0:T(8,128)S(1)} fusion(f32[1024,512]{1,0:T(8,128)} %get-tuple-element.493, s32[256]{0:T(256)S(1)} %iota_add_fusion.9), kind=kOutput, calls=%fused_computation.70.clone.1 | convolution fusion | flops 1614282752 | bytes 2622464 | tf_op jit(solution)/shard_map/while/body/eval_jaxpr/dot_general | solution.py:30
  399.0 7.6 %fusion.224 = f32[256,512]{1,0:T(8,128)S(1)} fusion(f32[1024,512]{1,0:T(8,128)} %get-tuple-element.493, s32[256]{0:T(256)S(1)} %iota_add_fusion.9), kind=kOutput, calls=%fused_computation.70.clone.1 | convolution fusion | flops 1614282752 | bytes 2622464 | tf_op jit(solution)/shard_map/while/body/eval_jaxpr/dot_general | solution.py:30
  413.9 7.6 %fusion.224 = f32[256,512]{1,0:T(8,128)S(1)} fusion(f32[1024,512]{1,0:T(8,128)} %get-tuple-element.493, s32[256]{0:T(256)S(1)} %iota_add_fusion.9), kind=kOutput, calls=%fused_computation.70.clone.1 | convolution fusion | flops 1614282752 | bytes 2622464 | tf_op jit(solution)/shard_map/while/body/eval_jaxpr/dot_general | solution.py:30
  438.1 25.7 %all-to-all-done.6 = f32[1024,2,128]{2,1,0:T(2,128)S(1)} async-done(((f32[1024,2,128]{2,1,0:T(2,128)}), f32[1024,2,128]{2,1,0:T(2,128)S(1)}, u32[]{:S(2)}, u32[]{:S(2)}) %all-to-all-start.6) | async-done | bytes 1048608 | tf_op jit(solution)/shard_map/all_to_all | solution.py:99
  468.8 26.6 %all-to-all-done.7 = f32[1024,2,128]{2,1,0:T(2,128)} async-done(((f32[1024,2,128]{2,1,0:T(2,128)}), f32[1024,2,128]{2,1,0:T(2,128)}, u32[]{:S(2)}, u32[]{:S(2)}) %all-to-all-start.7) | async-done | bytes 1048608 | tf_op jit(solution)/shard_map/all_to_all | solution.py:100
  499.7 14.3 %all_to_all.132 = bf16[16,64,128]{2,1,0:T(8,128)(2,1)S(1)} all-to-all(bf16[16,64,128]{2,1,0:T(8,128)(2,1)S(1)} %copy.57), channel_id=1, replica_groups=mesh['ctx'=16,'tp'=16] {'ctx'}, dimensions={0} | all-to-all | bytes 524288 | tf_op jit(solution)/shard_map/all_to_all | solution.py:116
  (138 shorter events, 183.6 us)
Async XLA Ops:
  6.5 87.9 %copy-start = (bf16[2048,128]{1,0:T(8,128)(2,1)S(1)}, bf16[2048,128]{1,0:T(8,128)(2,1)}, u32[]{:S(2)}) copy-start(bf16[2048,128]{1,0:T(8,128)(2,1)} %param.14) | copy-start | bytes 1572868
  6.5 87.9 %all-gather.2.cloned.1.call-start = ((), (), s32[]{:S(2)}) async-start(), calls=%async_computation.9 | async-start | bytes 4456448 | tf_op jit(solution)/shard_map/all_gather | solution.py:129
  12.9 85.8 %all-to-all-start.3 = ((f32[1,1024,128]{2,0,1:T(1,128)}), f32[1,1024,128]{2,0,1:T(1,128)S(1)}, u32[]{:S(2)}, u32[]{:S(2)}) async-start(f32[1,1024,128]{2,0,1:T(1,128)} %bitcast.13), calls=%async_computation.3 | async-start | bytes 1048576 | tf_op jit(solution)/shard_map/all_to_all | solution.py:54
  98.7 21.8 %all-to-all-start = ((f32[1,1024,128]{2,0,1:T(1,128)}), f32[1,1024,128]{2,0,1:T(1,128)S(1)}, u32[]{:S(2)}, u32[]{:S(2)}) async-start(f32[1,1024,128]{2,0,1:T(1,128)} %bitcast.2), calls=%async_computation | async-start | bytes 1048576 | tf_op jit(solution)/shard_map/all_to_all | solution.py:47
  126.4 31.4 %all-to-all-start.4 = ((f32[64,32,128]{2,0,1:T(8,128)}), f32[64,32,128]{2,0,1:T(8,128)}, u32[]{:S(2)}, u32[]{:S(2)}) async-start(f32[64,32,128]{2,0,1:T(8,128)} %copy.51), calls=%async_computation.4 | async-start | bytes 2097152 | tf_op jit(solution)/shard_map/all_to_all | solution.py:85
  130.8 31.4 %copy-start.1 = (f32[64,32,128]{2,1,0:T(8,128)S(1)}, f32[64,32,128]{2,1,0:T(8,128)}, u32[]{:S(2)}) copy-start(f32[64,32,128]{2,1,0:T(8,128)} %get-tuple-element.329) | copy-start | bytes 3145732
  157.8 31.5 %all-to-all-start.5 = ((f32[64,32,128]{2,0,1:T(8,128)}), f32[64,32,128]{2,0,1:T(8,128)}, u32[]{:S(2)}, u32[]{:S(2)}) async-start(f32[64,32,128]{2,0,1:T(8,128)} %copy.53), calls=%async_computation.5 | async-start | bytes 2097152 | tf_op jit(solution)/shard_map/all_to_all | solution.py:86
  189.3 31.7 %all-to-all-start.1 = ((f32[64,32,128]{2,0,1:T(8,128)}), f32[64,32,128]{2,0,1:T(8,128)S(1)}, u32[]{:S(2)}, u32[]{:S(2)}) async-start(f32[64,32,128]{2,0,1:T(8,128)} %copy.44), calls=%async_computation.1 | async-start | bytes 2097152 | tf_op jit(solution)/shard_map/all_to_all | solution.py:83
  221.0 71.6 %all-to-all-start.2 = ((f32[64,32,128]{2,0,1:T(8,128)}), f32[64,32,128]{2,0,1:T(8,128)S(1)}, u32[]{:S(2)}, u32[]{:S(2)}) async-start(f32[64,32,128]{2,0,1:T(8,128)} %copy.46), calls=%async_computation.2 | async-start | bytes 2097152 | tf_op jit(solution)/shard_map/all_to_all | solution.py:84
  224.6 1.8 copy-start.4
  231.7 7.6 %copy-start.7 = (f32[1024,512]{1,0:T(8,128)S(1)}, f32[1024,512]{1,0:T(8,128)}, u32[]{:S(2)}) copy-start(f32[1024,512]{1,0:T(8,128)} %get-tuple-element.475) | copy-start | bytes 6291460 | tf_op jit(solution)/shard_map/while
  247.2 7.6 %copy-start.7 = (f32[1024,512]{1,0:T(8,128)S(1)}, f32[1024,512]{1,0:T(8,128)}, u32[]{:S(2)}) copy-start(f32[1024,512]{1,0:T(8,128)} %get-tuple-element.475) | copy-start | bytes 6291460 | tf_op jit(solution)/shard_map/while
  262.7 7.6 %copy-start.7 = (f32[1024,512]{1,0:T(8,128)S(1)}, f32[1024,512]{1,0:T(8,128)}, u32[]{:S(2)}) copy-start(f32[1024,512]{1,0:T(8,128)} %get-tuple-element.475) | copy-start | bytes 6291460 | tf_op jit(solution)/shard_map/while
  278.2 7.6 %copy-start.7 = (f32[1024,512]{1,0:T(8,128)S(1)}, f32[1024,512]{1,0:T(8,128)}, u32[]{:S(2)}) copy-start(f32[1024,512]{1,0:T(8,128)} %get-tuple-element.475) | copy-start | bytes 6291460 | tf_op jit(solution)/shard_map/while
  306.0 7.6 %copy-start.8 = (f32[1024,512]{1,0:T(8,128)S(1)}, f32[1024,512]{1,0:T(8,128)}, u32[]{:S(2)}) copy-start(f32[1024,512]{1,0:T(8,128)} %get-tuple-element.457) | copy-start | bytes 6291460 | tf_op jit(solution)/shard_map/while
  320.8 7.6 %copy-start.8 = (f32[1024,512]{1,0:T(8,128)S(1)}, f32[1024,512]{1,0:T(8,128)}, u32[]{:S(2)}) copy-start(f32[1024,512]{1,0:T(8,128)} %get-tuple-element.457) | copy-start | bytes 6291460 | tf_op jit(solution)/shard_map/while
  335.7 7.6 %copy-start.8 = (f32[1024,512]{1,0:T(8,128)S(1)}, f32[1024,512]{1,0:T(8,128)}, u32[]{:S(2)}) copy-start(f32[1024,512]{1,0:T(8,128)} %get-tuple-element.457) | copy-start | bytes 6291460 | tf_op jit(solution)/shard_map/while
  350.5 7.6 %copy-start.8 = (f32[1024,512]{1,0:T(8,128)S(1)}, f32[1024,512]{1,0:T(8,128)}, u32[]{:S(2)}) copy-start(f32[1024,512]{1,0:T(8,128)} %get-tuple-element.457) | copy-start | bytes 6291460 | tf_op jit(solution)/shard_map/while
  369.3 7.6 %copy-start.6 = (f32[1024,512]{1,0:T(8,128)S(1)}, f32[1024,512]{1,0:T(8,128)}, u32[]{:S(2)}) copy-start(f32[1024,512]{1,0:T(8,128)} %get-tuple-element.493) | copy-start | bytes 6291460 | tf_op jit(solution)/shard_map/while
  384.1 7.6 %copy-start.6 = (f32[1024,512]{1,0:T(8,128)S(1)}, f32[1024,512]{1,0:T(8,128)}, u32[]{:S(2)}) copy-start(f32[1024,512]{1,0:T(8,128)} %get-tuple-element.493) | copy-start | bytes 6291460 | tf_op jit(solution)/shard_map/while
  399.0 7.6 %copy-start.6 = (f32[1024,512]{1,0:T(8,128)S(1)}, f32[1024,512]{1,0:T(8,128)}, u32[]{:S(2)}) copy-start(f32[1024,512]{1,0:T(8,128)} %get-tuple-element.493) | copy-start | bytes 6291460 | tf_op jit(solution)/shard_map/while
  413.9 7.6 %copy-start.6 = (f32[1024,512]{1,0:T(8,128)S(1)}, f32[1024,512]{1,0:T(8,128)}, u32[]{:S(2)}) copy-start(f32[1024,512]{1,0:T(8,128)} %get-tuple-element.493) | copy-start | bytes 6291460 | tf_op jit(solution)/shard_map/while
  429.1 34.7 %all-to-all-start.6 = ((f32[1024,2,128]{2,1,0:T(2,128)}), f32[1024,2,128]{2,1,0:T(2,128)S(1)}, u32[]{:S(2)}, u32[]{:S(2)}) async-start(f32[1024,2,128]{2,1,0:T(2,128)} %reshape.154), calls=%async_computation.6 | async-start | bytes 2097152 | tf_op jit(solution)/shard_map/all_to_all | solution.py:99
  463.8 31.5 %all-to-all-start.7 = ((f32[1024,2,128]{2,1,0:T(2,128)}), f32[1024,2,128]{2,1,0:T(2,128)}, u32[]{:S(2)}, u32[]{:S(2)}) async-start(f32[1024,2,128]{2,1,0:T(2,128)} %reshape.155), calls=%async_computation.7 | async-start | bytes 2097152 | tf_op jit(solution)/shard_map/all_to_all | solution.py:100
  (3 other events, 4.3 us)
Sparse Core Ops, SparseCore 0:
  9.9 84.4 all-gather.1
where the time goes:
time: 531 us; the launch traced here: 522 us
  matrix products  179 us (34%)
  waiting for transfers between devices  164 us (31%)
  blocking collectives  58.9 us (11%)
  starting transfers between devices  41.4 us (8%)
  local copies, waits for them, and re-layouts  33.4 us (6%)
  other arithmetic  21.4 us (4%)
  between operations  14.1 us (3%)
  loops' own time  9.95 us (2%)
    dot_general x12, matrix products, one_segment(): sine = jnp.dot(jnp.sin(table), stacked, precision=HIGHEST)  91 us
    dot_general x12, matrix products, one_segment(): cosine = jnp.dot(jnp.cos(table), stacked, precision=HIGHEST)  69.8 us
    psum x1, blocking collectives, on_device(): row_power = lax.psum(jnp.sum(tok_values * tok_values, axis=1), 'tp')  44.6 us
    all_gather x1, waiting for transfers between devices, on_device(): lax.all_gather(scaled, 'tp', axis=1, tiled=True)  28.4 us
    all_to_all x1, waiting for transfers between devices, inverse(): lax.all_to_all(back_imag, 'ctx', split_axis=0, concat_axis=1, tiled=True)  26.6 us
    all_to_all x1, waiting for transfers between devices, inverse(): lax.all_to_all(back_real, 'ctx', split_axis=0, concat_axis=1, tiled=True)  25.7 us
    all_to_all x1, waiting for transfers between devices, forward(): lax.all_to_all(other_imag, 'ctx', split_axis=1, concat_axis=0, tiled=True)  25.6 us
    all_to_all x1, waiting for transfers between devices, forward(): lax.all_to_all(other_real, 'ctx', split_axis=1, concat_axis=0, tiled=True)  24.1 us
  transfers between devices with their start and end apart: 9, of which 7 were waited for; matrix products, arithmetic and copies ran while one was open for 18% of the time, Pallas kernels for 0%

commit v1 on v0

v1 whole, which is shorter than its diff:
```python
import math

import jax
import jax.numpy as jnp
import ml_dtypes
import numpy as np
from jax import lax
from jax.experimental import pallas as pl
from jax.experimental.pallas import tpu as pltpu
from jax.sharding import PartitionSpec as P

EPS = 1e-05
HIGHEST = lax.Precision.HIGHEST
CTX, HI, YS, CORES = 16, 2, 4, 2
LANES = 128
FEATURES = 2048
SHARE = 8
ROWS = 1024
HALF = ROWS // CORES
BLOCKS = ROWS // LANES
PAD = 16
BF16, F32 = jnp.bfloat16, jnp.float32


def split_high_low(table):
    high = table.astype(ml_dtypes.bfloat16)
    low = (table - high.astype(np.float64)).astype(ml_dtypes.bfloat16)
    return high, low


def tables():
    ids = np.arange(LANES)
    quarter = ids + 0.25
    outer = np.exp(-2j * np.pi * np.outer(quarter, ids) / LANES)
    first = np.concatenate([outer.real, outer.imag], axis=0)
    twiddle = np.exp(-2j * np.pi * np.outer(quarter, ids) / LANES**2)
    inner = np.exp(-2j * np.pi * np.outer(ids, ids) / LANES)
    second = np.block([[inner.real, inner.imag], [-inner.imag, inner.real]])
    other = (ids // BLOCKS) * BLOCKS + (ids % BLOCKS + BLOCKS // 2) % BLOCKS
    natural = np.concatenate(split_high_low(first), axis=1)
    swapped = np.concatenate(split_high_low(first[:, other]), axis=1)
    last = split_high_low(first.T / LANES**2)
    return dict(
        first=np.stack([natural, swapped]),
        turn=np.stack([twiddle.real, twiddle.imag]).astype(np.float32),
        second=np.stack(split_high_low(second)),
        second_back=np.stack(split_high_low(second.T)),
        last=np.stack(last),
    )


def mm(left, right):
    return jnp.dot(left, right, preferred_element_type=F32)


def high_low(value):
    high = value.astype(BF16)
    return high, (value - high.astype(F32)).astype(BF16)


def mm3_right(value, table):
    high, low = high_low(value)
    return mm(high, table[0]) + mm(low, table[0]) + mm(high, table[1])


def mm3_left(table, value):
    high, low = high_low(value)
    return mm(table[0], high) + mm(table[0], low) + mm(table[1], high)


def spectrum_of_pair(pair, first, turn_real, turn_imag, second):
    mixed = mm(first, jnp.concatenate([pair, pair], axis=0))
    rows = []
    for at in range(2):
        real = mixed[:LANES, at * LANES : (at + 1) * LANES]
        imag = mixed[LANES:, at * LANES : (at + 1) * LANES]
        rows.append(
            jnp.concatenate(
                [real * turn_real - imag * turn_imag, real * turn_imag + imag * turn_real], axis=1
            )
        )
    return mm3_right(jnp.concatenate(rows, axis=0), second)


def load_pair(unpacked, at):
    return jnp.concatenate(
        [unpacked[pl.ds(2 * at + k, LANES, stride=SHARE), :] for k in range(2)], axis=1
    ).astype(BF16)


def filter_kernel(blocks_ref, first_ref, turn_ref, second_ref, out_ref, unpacked):
    unpacked[...] = blocks_ref[...].astype(F32).reshape(CTX * BLOCKS * SHARE, LANES)
    for at in range(SHARE // 2):
        out_ref[pl.ds(at * 2 * LANES, 2 * LANES), :] = spectrum_of_pair(
            load_pair(unpacked, at), first_ref[...], turn_ref[0], turn_ref[1], second_ref
        )


def mix_kernel(
    own_ref, other_ref, response_ref, first_ref, turn_ref, second_ref, back_ref, last_ref,
    out_ref, unpacked, gathered,
):
    half = BLOCKS * SHARE // 2
    both = jnp.concatenate([own_ref[:, :half, :], other_ref[...]], axis=1)
    unpacked[...] = both.astype(F32).reshape(CTX * BLOCKS * SHARE, LANES)
    turn_real, turn_imag = turn_ref[0], turn_ref[1]
    for at in range(SHARE // 2):
        signal = spectrum_of_pair(
            load_pair(unpacked, at), first_ref[...], turn_real, turn_imag, second_ref
        )
        response = response_ref[pl.ds(at * 2 * LANES, 2 * LANES), :]
        sig_real, sig_imag = signal[:, :LANES], signal[:, LANES:]
        res_real, res_imag = response[:, :LANES], response[:, LANES:]
        product = jnp.concatenate(
            [sig_real * res_real - sig_imag * res_imag, sig_real * res_imag + sig_imag * res_real],
            axis=1,
        )
        back = mm3_right(product, back_ref)
        reals, imags = [], []
        for k in range(2):
            real = back[k * LANES : (k + 1) * LANES, :LANES]
            imag = back[k * LANES : (k + 1) * LANES, LANES:]
            reals.append(real * turn_real + imag * turn_imag)
            imags.append(imag * turn_real - real * turn_imag)
        turned = jnp.concatenate(
            [jnp.concatenate(reals, axis=1), jnp.concatenate(imags, axis=1)], axis=0
        )
        result = mm3_left(last_ref, turned)
        for k in range(2):
            gathered[pl.ds(2 * at + k, LANES, stride=SHARE), :] = result[
                :, k * LANES : (k + 1) * LANES
            ]
    out_ref[...] = gathered[...].reshape(CTX, BLOCKS * SHARE, LANES).astype(BF16)


def project_kernel(
    place_ref, own_ref, left_ref, right_ref, mid_a_ref, mid_b_ref,
    far_ref, far_left_ref, far_right_ref, far_mid_a_ref, far_mid_b_ref,
    w_own_ref, w_other_ref, out_ref,
):
    high, along, core = place_ref[0], place_ref[1], place_ref[2]
    pieces = [
        (0, 0, own_ref, 0, own_ref, 1),
        (0, YS - 1, left_ref, 0, left_ref, 1),
        (0, 1, right_ref, 0, right_ref, 1),
        (0, 2, mid_a_ref, 0, mid_b_ref, 0),
        (1, 0, far_ref, 0, far_ref, 1),
        (1, YS - 1, far_left_ref, 0, far_left_ref, 1),
        (1, 1, far_right_ref, 0, far_right_ref, 1),
        (1, 2, far_mid_a_ref, 0, far_mid_b_ref, 0),
    ]
    total = jnp.zeros((HALF, 2 * LANES), F32)
    squares = jnp.zeros((HALF, LANES), F32)
    for d_high, d_along, ref_a, at_a, ref_b, at_b in pieces:
        chip = lax.rem(high + d_high, HI) * YS + lax.rem(along + d_along, YS)
        scaled, weights = [], []
        for slot, (ref, at) in enumerate(((ref_a, at_a), (ref_b, at_b))):
            values = ref[at, :HALF, :].astype(F32)
            squares = squares + values * values
            gain = ref[at, HALF : HALF + PAD, :].astype(F32)[:1]
            scaled.append((values * gain).astype(BF16))
            owner = chip * CORES + (core if slot == 0 else 1 - core)
            start = pl.multiple_of(owner * LANES, LANES)
            weights.append(
                jnp.concatenate(
                    [w_own_ref[pl.ds(start, LANES), :], w_other_ref[pl.ds(start, LANES), :]],
                    axis=1,
                )
            )
        total = total + mm(jnp.concatenate(scaled, axis=1), jnp.concatenate(weights, axis=0))
    power = jnp.sum(squares, axis=1, keepdims=True) * (1.0 / FEATURES)
    total = total * lax.rsqrt(power + EPS)
    for slot in range(CORES):
        for pair in range(BLOCKS // CORES // 2):
            parts = []
            for k in range(2):
                block = 2 * pair + k
                part = total[
                    block * LANES : (block + 1) * LANES, slot * LANES : (slot + 1) * LANES
                ]
                parts.append(part.T.reshape(CTX, SHARE, LANES))
            start = slot * (BLOCKS * SHARE // 2) + pair * 2 * SHARE
            out_ref[:, start : start + 2 * SHARE, :] = jnp.concatenate(parts, axis=1).astype(BF16)


def turn_kernel(blocks_ref, out_ref):
    for pair in range(BLOCKS // 2):
        values = blocks_ref[:, pair * 2 * SHARE : (pair + 1) * 2 * SHARE, :].astype(F32)
        for k in range(2):
            part = values[:, k * SHARE : (k + 1) * SHARE, :].reshape(LANES, LANES)
            start = (2 * pair + k) * LANES
            out_ref[start : start + LANES, :] = part.T.astype(BF16)


VMEM = pl.BlockSpec(memory_space=pltpu.VMEM)
SMEM = pl.BlockSpec(memory_space=pltpu.SMEM)
PARAMS = pltpu.CompilerParams(vmem_limit_bytes=48 * 1024 * 1024)


def call(kernel, shape, dtype, operands, scratch=(), first_spec=VMEM, flops=0):
    moved = sum(x.size * x.dtype.itemsize for x in operands)
    return pl.pallas_call(
        kernel,
        out_shape=jax.ShapeDtypeStruct(shape, dtype),
        in_specs=[first_spec] + [VMEM] * (len(operands) - 1),
        out_specs=VMEM,
        scratch_shapes=list(scratch),
        compiler_params=PARAMS,
        cost_estimate=pl.CostEstimate(flops=flops, bytes_accessed=moved, transcendentals=0),
    )(*operands)


def tp_shift(value, d_high, d_along, d_core):
    pairs = []
    for high in range(HI):
        for along in range(YS):
            for core in range(CORES):
                source = (high * YS + along) * CORES + core
                target = (
                    (high + d_high) % HI * YS + (along + d_along) % YS
                ) * CORES + (core + d_core) % CORES
                pairs.append((source, target))
    return lax.ppermute(value, "tp", pairs)


def rings(piece):
    left = tp_shift(piece, 0, 1, 0)
    right = tp_shift(piece, 0, YS - 1, 0)
    mid_a = tp_shift(left[:1], 0, 1, 0)
    mid_b = tp_shift(right[1:], 0, YS - 1, 0)
    return left, right, mid_a, mid_b


def on_device(tokens, gain, w_inputs, filters, w_plus, w_minus):
    table = tables()
    position = lax.axis_index("tp")
    core = lax.rem(position, CORES)
    place = jnp.stack(
        [position // (YS * CORES), lax.rem(position // CORES, YS), core, core]
    ).astype(jnp.int32)

    gain_rows = jnp.broadcast_to(gain[None, :], (PAD, LANES))
    mine = lax.dynamic_slice_in_dim(tokens, core * HALF, HALF, axis=0)
    theirs = lax.dynamic_slice_in_dim(tokens, (1 - core) * HALF, HALF, axis=0)
    arrived = tp_shift(jnp.concatenate([theirs, gain_rows], axis=0), 0, 0, 1)
    own = jnp.stack([jnp.concatenate([mine, gain_rows], axis=0), arrived])
    far = tp_shift(own, 1, 0, 0)
    near_parts = rings(own)
    far_parts = rings(far)
    w_other = tp_shift(w_inputs, 0, 0, 1)

    lag_sign = 1.0 - 2.0 * (lax.iota(jnp.int32, ROWS) % 2).astype(F32)
    response = jnp.einsum("kt,kc->ct", filters, w_plus.astype(F32), precision=HIGHEST)
    response = response + lag_sign[None, :] * jnp.einsum(
        "kt,kc->ct", filters, w_minus.astype(F32), precision=HIGHEST
    )
    response = (
        response.reshape(CTX, SHARE, BLOCKS, LANES)
        .transpose(0, 2, 1, 3)
        .astype(BF16)
        .reshape(CTX, BLOCKS * SHARE, LANES)
    )
    response = lax.all_to_all(response, "ctx", split_axis=0, concat_axis=0, tiled=True)
    unpacked = pltpu.VMEM((CTX * BLOCKS * SHARE, LANES), F32)
    turn, second = jnp.asarray(table["turn"]), jnp.asarray(table["second"])
    first = jnp.asarray(table["first"])
    response = call(
        filter_kernel,
        (SHARE * LANES, 2 * LANES),
        F32,
        [response, first[0], turn, second],
        [unpacked],
        flops=10**9,
    )

    operands = [place, own, *near_parts, far, *far_parts, w_inputs, w_other]
    blocks = call(
        project_kernel,
        (CTX, BLOCKS * SHARE, LANES),
        BF16,
        operands,
        first_spec=SMEM,
        flops=2 * HALF * 2 * LANES * FEATURES,
    )
    blocks = lax.all_to_all(blocks, "ctx", split_axis=0, concat_axis=0, tiled=True)
    other = tp_shift(blocks[:, BLOCKS * SHARE // 2 :, :], 0, 0, 1)
    mixed = call(
        mix_kernel,
        (CTX, BLOCKS * SHARE, LANES),
        BF16,
        [
            blocks,
            other,
            response,
            lax.dynamic_index_in_dim(first, core, axis=0, keepdims=False),
            turn,
            second,
            jnp.asarray(table["second_back"]),
            jnp.asarray(table["last"]),
        ],
        [unpacked, unpacked],
        flops=2 * 10**9,
    )
    mixed = lax.all_to_all(mixed, "ctx", split_axis=0, concat_axis=0, tiled=True)
    return call(turn_kernel, (ROWS, LANES), BF16, [mixed])


def solution(mesh):
    in_specs = (
        P("ctx", "tp"),
        P("tp"),
        P(None, "tp"),
        P(None, "ctx"),
        P(None, "tp"),
        P(None, "tp"),
    )
    return jax.shard_map(
        on_device, mesh=mesh, in_specs=in_specs, out_specs=P("ctx", "tp"), check_vma=False
    )
```

time: 531 us -> 89.2 us (0.17); the launches traced: 522 us -> 87.7 us
  matrix products: 179 us -> 1.56 us
  waiting for transfers between devices: 164 us -> 32.4 us
  blocking collectives: 58.9 us -> 12.4 us
  local copies, waits for them, and re-layouts: 33.4 us -> 4.03 us
  other arithmetic: 21.4 us -> 0.13 us
  between operations: 14.1 us -> 0.23 us
  starting transfers between devices: 41.4 us -> 29.8 us
  loops' own time: 9.95 us -> 0 us
  Pallas kernels: 0 us -> 7.12 us
    dot_general x33 -> x2, matrix products: 179 us -> 1.56 us  [the longest x1 1.15 us: on_device(): jnp.einsum('kt,kc->ct', filters, w_minus.astype(F32), precision=HIGHEST)]
    all_to_all x8 -> x2, waiting for transfers between devices: 135 us -> 16 us  [the longest x1 8.7 us: on_device(): lax.all_to_all(response, 'ctx', split_axis=0, concat_axis=0, tiled=True)]
    psum x1 -> x0, blocking collectives: 44.6 us -> none  [on_device(): row_power = lax.psum(jnp.sum(tok_values * tok_values, axis=1), 'tp')]
    all_gather x1 -> x0, waiting for transfers between devices: 28.4 us -> none  [on_device(): lax.all_gather(scaled, 'tp', axis=1, tiled=True)]
    all_to_all x8 -> x2, starting transfers between devices: 41.4 us -> 13.9 us  [the longest x1 10.3 us: on_device(): lax.all_to_all(blocks, 'ctx', split_axis=0, concat_axis=0, tiled=True)]
    ppermute x0 -> x12, waiting for transfers between devices: none -> 16.4 us  [tp_shift(): return lax.ppermute(value, 'tp', pairs)]
    ppermute x0 -> x12, starting transfers between devices: none -> 15.8 us  [tp_shift(): return lax.ppermute(value, 'tp', pairs)]
    all_to_all x6 -> x0, local copies, waits for them, and re-layouts: 11.1 us -> none  [the longest x1 3.08 us: forward(): lax.all_to_all(other_real, 'ctx', split_axis=1, concat_axis=0, tiled=True)]
  transfers between devices with their start and end apart: 9 -> 14, of which waited for: 7 -> 7; matrix products, arithmetic and copies ran while one was open for 18% -> 4% of each run, Pallas kernels for 0% -> 1%
where the time goes in v1:
time: 89.2 us; the launch traced here: 87.7 us
  waiting for transfers between devices  32.4 us (36%)
  starting transfers between devices  29.8 us (33%)
  blocking collectives  12.4 us (14%)
  Pallas kernels  7.12 us (8%)
  local copies, waits for them, and re-layouts  4.03 us (5%)
  matrix products  1.56 us (2%)
    ppermute x12, waiting for transfers between devices, tp_shift(): return lax.ppermute(value, 'tp', pairs)  16.4 us
    ppermute x12, starting transfers between devices, tp_shift(): return lax.ppermute(value, 'tp', pairs)  15.8 us
    all_to_all x1, blocking collectives, on_device(): lax.all_to_all(mixed, 'ctx', split_axis=0, concat_axis=0, tiled=True)  12.4 us
    all_to_all x1, starting transfers between devices, on_device(): lax.all_to_all(blocks, 'ctx', split_axis=0, concat_axis=0, tiled=True)  10.3 us
    all_to_all x1, waiting for transfers between devices, on_device(): lax.all_to_all(response, 'ctx', split_axis=0, concat_axis=0, tiled=True)  8.7 us
    all_to_all x1, waiting for transfers between devices, on_device(): lax.all_to_all(blocks, 'ctx', split_axis=0, concat_axis=0, tiled=True)  7.26 us
    pallas_call x4, Pallas kernels, call(): pl.pallas_call(kernel, out_shape=jax.ShapeDtypeStruct(shape, dtype), in_s...  7.12 us
    all_to_all x1, starting transfers between devices, on_device(): lax.all_to_all(response, 'ctx', split_axis=0, concat_axis=0, tiled=True)  3.66 us
  transfers between devices with their start and end apart: 14, of which 7 were waited for; matrix products, arithmetic and copies ran while one was open for 4% of the time, Pallas kernels for 1%

profile of v1, /device:TPU:8, one launch (start us, length us, event | category | flops | bytes accessed | tf_op | source)
XLA Modules:
  0.0 87.7 jit_solution(17841209201208383670)
XLA Ops:
  0.0 1.0 %constant_dynamic-slice_fusion.1 = (bf16[512,128]{1,0:T(8,128)(2,1)S(1)}, bf16[512,128]{1,0:T(8,128)(2,1)S(1)}) fusion(bf16[1024,128]{1,0:T(8,128)(2,1)} %param.11, s32[]{:T(128)S(6)} %select_n.30, s32[]{:T(128)S(6)} %select_n.31), kind=kLoop, calls=%fused_computation.18 | loop fusion | bytes 524296 | tf_op jit(solution)/shard_map/dynamic_slice | solution.py:243
  1.8 1.3 %collective-permute-done = bf16[528,128]{1,0:T(8,128)(2,1)S(1)} collective-permute-done((bf16[528,128]{1,0:T(8,128)(2,1)S(1)}, bf16[528,128]{1,0:T(8,128)(2,1)S(1)}, u32[]{:S(2)}, u32[]{:S(2)}) %collective-permute-start) | collective-permute-done | bytes 135200 | tf_op jit(solution)/shard_map/ppermute | solution.py:223
  3.2 7.3 %collective-permute-start.5 = (bf16[2,528,128]{2,1,0:T(8,128)(2,1)S(1)}, bf16[2,528,128]{2,1,0:T(8,128)(2,1)S(1)}, u32[]{:S(2)}, u32[]{:S(2)}) collective-permute-start(bf16[2,528,128]{2,1,0:T(8,128)(2,1)S(1)} %pad_maximum_fusion.own_ref), channel_id=1, source_target_pairs={{0,8},{1,9},{2,10},{3,11},{4,12},{5,13},{6,14},{7,15},{8,0},{9,1},... | collective-permute-start | bytes 811016 | tf_op jit(solution)/shard_map/ppermute | solution.py:223
  10.5 1.6 %collective-permute-start.1 = (bf16[2,528,128]{2,1,0:T(8,128)(2,1)S(1)}, bf16[2,528,128]{2,1,0:T(8,128)(2,1)S(1)}, u32[]{:S(2)}, u32[]{:S(2)}) collective-permute-start(bf16[2,528,128]{2,1,0:T(8,128)(2,1)S(1)} %pad_maximum_fusion.own_ref), channel_id=1, source_target_pairs={{0,2},{1,3},{2,4},{3,5},{4,6},{5,7},{6,0},{7,1},{8,10},{9,11},{10,... | collective-permute-start | bytes 811016 | tf_op jit(solution)/shard_map/ppermute | solution.py:223
  12.5 5.9 %collective-permute-done.5.far_ref = bf16[2,528,128]{2,1,0:T(8,128)(2,1)S(1)} collective-permute-done((bf16[2,528,128]{2,1,0:T(8,128)(2,1)S(1)}, bf16[2,528,128]{2,1,0:T(8,128)(2,1)S(1)}, u32[]{:S(2)}, u32[]{:S(2)}) %collective-permute-start.5) | collective-permute-done | bytes 270368 | tf_op jit(solution)/shard_map/ppermute | solution.py:223
  18.4 1.6 %collective-permute-start.6 = (bf16[2,528,128]{2,1,0:T(8,128)(2,1)S(1)}, bf16[2,528,128]{2,1,0:T(8,128)(2,1)S(1)}, u32[]{:S(2)}, u32[]{:S(2)}) collective-permute-start(bf16[2,528,128]{2,1,0:T(8,128)(2,1)S(1)} %collective-permute-done.5.far_ref), channel_id=1, source_target_pairs={{0,2},{1,3},{2,4},{3,5},{4,6},{5,7},{6,0},{7,1},{8,10},{9,11},{10,... | collective-permute-start | bytes 811016 | tf_op jit(solution)/shard_map/ppermute | solution.py:223
  20.4 1.7 %collective-permute-start.3 = (bf16[1,528,128]{2,1,0:T(8,128)(2,1)S(1)}, bf16[1,528,128]{2,1,0:T(8,128)(2,1)S(1)}, u32[]{:S(2)}, u32[]{:S(2)}) collective-permute-start(bf16[1,528,128]{2,1,0:T(8,128)(2,1)S(1)} %slice.24), channel_id=1, source_target_pairs={{0,2},{1,3},{2,4},{3,5},{4,6},{5,7},{6,0},{7,1},{8,10},{9,11},{10,... | collective-permute-start | bytes 405512 | tf_op jit(solution)/shard_map/ppermute | solution.py:223
  22.1 0.7 slice.25
  23.2 4.5 %collective-permute-done.6.far_left_ref = bf16[2,528,128]{2,1,0:T(8,128)(2,1)S(1)} collective-permute-done((bf16[2,528,128]{2,1,0:T(8,128)(2,1)S(1)}, bf16[2,528,128]{2,1,0:T(8,128)(2,1)S(1)}, u32[]{:S(2)}, u32[]{:S(2)}) %collective-permute-start.6) | collective-permute-done | bytes 270368 | tf_op jit(solution)/shard_map/ppermute | solution.py:223
  27.7 0.7 slice.26
  28.4 1.6 %collective-permute-start.8 = (bf16[1,528,128]{2,1,0:T(8,128)(2,1)}, bf16[1,528,128]{2,1,0:T(8,128)(2,1)S(1)}, u32[]{:S(2)}, u32[]{:S(2)}) collective-permute-start(bf16[1,528,128]{2,1,0:T(8,128)(2,1)} %slice.26), channel_id=1, source_target_pairs={{0,2},{1,3},{2,4},{3,5},{4,6},{5,7},{6,0},{7,1},{8,10},{9,11},{10,... | collective-permute-start | bytes 405512 | tf_op jit(solution)/shard_map/ppermute | solution.py:223
  30.0 0.7 slice.27
  31.2 2.4 %collective-permute-done.8.far_mid_a_ref = bf16[1,528,128]{2,1,0:T(8,128)(2,1)S(1)} collective-permute-done((bf16[1,528,128]{2,1,0:T(8,128)(2,1)}, bf16[1,528,128]{2,1,0:T(8,128)(2,1)S(1)}, u32[]{:S(2)}, u32[]{:S(2)}) %collective-permute-start.8) | collective-permute-done | bytes 135200 | tf_op jit(solution)/shard_map/ppermute | solution.py:223
  33.6 2.2 %collective-permute-done.9.far_mid_b_ref = bf16[1,528,128]{2,1,0:T(8,128)(2,1)S(1)} collective-permute-done((bf16[1,528,128]{2,1,0:T(8,128)(2,1)}, bf16[1,528,128]{2,1,0:T(8,128)(2,1)S(1)}, u32[]{:S(2)}, u32[]{:S(2)}) %collective-permute-start.9) | collective-permute-done | bytes 135200 | tf_op jit(solution)/shard_map/ppermute | solution.py:223
  35.9 2.2 %shard_map.109 = bf16[16,64,128]{2,1,0:T(8,128)(2,1)} custom-call(s32[4]{0:T(128)S(1)} %pad_add_fusion.place_ref, bf16[2,528,128]{2,1,0:T(8,128)(2,1)S(1)} %pad_maximum_fusion.own_ref, bf16[2,528,128]{2,1,0:T(8,128)(2,1)S(1)} %collective-permute-done.1.left_ref, bf16[2,528,128]{2,1,0:T(8,128)(2,1)S(1)} %collective-permute-done.2.right_ref, ...), custom_call_target="tpu_custom_call" | custom-call | flops 536870912 | bytes 3211280 | tf_op jit(solution)/shard_map/pallas_call | solution.py:202
  38.1 10.3 %all-to-all-start = ((bf16[16,64,128]{2,1,0:T(8,128)(2,1)}), bf16[16,64,128]{2,1,0:T(8,128)(2,1)S(1)}, u32[]{:S(2)}, u32[]{:S(2)}) async-start(bf16[16,64,128]{2,1,0:T(8,128)(2,1)} %shard_map.109), calls=%async_computation | async-start | bytes 524288 | tf_op jit(solution)/shard_map/all_to_all | solution.py:285
  49.1 1.1 %fusion.2 = bf16[16,64,128]{2,1,0:T(8,128)(2,1)} fusion(f32[128,1024]{1,0:T(8,128)S(1)} %fusion.10, bf16[24,128]{1,0:T(8,128)(2,1)S(1)} %copy-done.9, f32[24,1024]{1,0:T(8,128)S(1)} %copy-done, f32[1024]{0:T(1024)S(1)} %fusion.6), kind=kOutput, calls=%fused_computation.3 | convolution fusion | flops 38141952 | bytes 894976 | tf_op jit(solution)/shard_map/kt,kc->ct/dot_general | solution.py:254
  50.2 7.3 %all-to-all-done.own_ref = bf16[16,64,128]{2,1,0:T(8,128)(2,1)S(1)} async-done(((bf16[16,64,128]{2,1,0:T(8,128)(2,1)}), bf16[16,64,128]{2,1,0:T(8,128)(2,1)S(1)}, u32[]{:S(2)}, u32[]{:S(2)}) %all-to-all-start) | async-done | bytes 262176 | tf_op jit(solution)/shard_map/all_to_all | solution.py:285
  57.5 3.7 %all-to-all-start.1 = ((bf16[16,64,128]{2,1,0:T(8,128)(2,1)}), bf16[16,64,128]{2,1,0:T(8,128)(2,1)S(1)}, u32[]{:S(2)}, u32[]{:S(2)}) async-start(bf16[16,64,128]{2,1,0:T(8,128)(2,1)} %fusion.2), calls=%async_computation.1 | async-start | bytes 524288 | tf_op jit(solution)/shard_map/all_to_all | solution.py:263
  61.6 8.7 %all-to-all-done.1.blocks_ref = bf16[16,64,128]{2,1,0:T(8,128)(2,1)S(1)} async-done(((bf16[16,64,128]{2,1,0:T(8,128)(2,1)}), bf16[16,64,128]{2,1,0:T(8,128)(2,1)S(1)}, u32[]{:S(2)}, u32[]{:S(2)}) %all-to-all-start.1) | async-done | bytes 262176 | tf_op jit(solution)/shard_map/all_to_all | solution.py:263
  70.3 1.0 %shard_map.110.response_ref = f32[1024,256]{1,0:T(8,128)S(1)} custom-call(bf16[16,64,128]{2,1,0:T(8,128)(2,1)S(1)} %all-to-all-done.1.blocks_ref, bf16[256,256]{1,0:T(8,128)(2,1)S(1)} %copy-done.6, f32[2,128,128]{2,1,0:T(8,128)S(1)} %copy-done.4, bf16[2,256,256]{2,1,0:T(8,128)(2,1)S(1)} %copy-done.2), custom_call_target="tpu_custom_call" | custom-call | flops 1000000000 | bytes 786432 | tf_op jit(solution)/shard_map/pallas_call | solution.py:202
  71.3 3.0 %shard_map.111 = bf16[16,64,128]{2,1,0:T(8,128)(2,1)S(1)} custom-call(bf16[16,64,128]{2,1,0:T(8,128)(2,1)S(1)} %all-to-all-done.own_ref, bf16[16,32,128]{2,1,0:T(8,128)(2,1)S(1)} %collective-permute-done.11.other_ref, f32[1024,256]{1,0:T(8,128)S(1)} %shard_map.110.response_ref, bf16[256,256]{1,0:T(8,128)(2,1)S(1)} %dynamic-slice_bitcast_fusion.first_ref, ...), custom_call_target="tpu_custom_call" | custom-call | flops 2000000000 | bytes 2359296 | tf_op jit(solution)/shard_map/pallas_call | solution.py:202
  74.4 12.4 %all_to_all.15.blocks_ref = bf16[16,64,128]{2,1,0:T(8,128)(2,1)S(1)} all-to-all(bf16[16,64,128]{2,1,0:T(8,128)(2,1)S(1)} %shard_map.111), channel_id=1, replica_groups=mesh['ctx'=16,'tp'=16] {'ctx'}, dimensions={0} | all-to-all | bytes 524288 | tf_op jit(solution)/shard_map/all_to_all | solution.py:304
  86.8 0.8 shard_map.112
  (45 shorter events, 3.7 us)
Async XLA Ops:
  0.0 48.4 %copy-start = (f32[24,1024]{1,0:T(8,128)S(1)}, f32[24,1024]{1,0:T(8,128)}, u32[]{:S(2)}) copy-start(f32[24,1024]{1,0:T(8,128)} %param.14) | copy-start | bytes 294916
  1.7 8.8 %copy-start.1 = (bf16[2048,128]{1,0:T(8,128)(2,1)S(1)}, bf16[2048,128]{1,0:T(8,128)(2,1)}, u32[]{:S(2)}) copy-start(bf16[2048,128]{1,0:T(8,128)(2,1)} %w_own_ref.1) | copy-start | bytes 1572868
  1.7 1.4 %collective-permute-start = (bf16[528,128]{1,0:T(8,128)(2,1)S(1)}, bf16[528,128]{1,0:T(8,128)(2,1)S(1)}, u32[]{:S(2)}, u32[]{:S(2)}) collective-permute-start(bf16[528,128]{1,0:T(8,128)(2,1)S(1)} %get-tuple-element.8), channel_id=1, source_target_pairs={{0,1},{1,0},{2,3},{3,2},{4,5},{5,4},{6,7},{7,6},{8,9},{9,8},{10,11... | collective-permute-start | bytes 405512 | tf_op jit(solution)/shard_map/ppermute | solution.py:223
  3.2 15.2 %collective-permute-start.5 = (bf16[2,528,128]{2,1,0:T(8,128)(2,1)S(1)}, bf16[2,528,128]{2,1,0:T(8,128)(2,1)S(1)}, u32[]{:S(2)}, u32[]{:S(2)}) collective-permute-start(bf16[2,528,128]{2,1,0:T(8,128)(2,1)S(1)} %pad_maximum_fusion.own_ref), channel_id=1, source_target_pairs={{0,8},{1,9},{2,10},{3,11},{4,12},{5,13},{6,14},{7,15},{8,0},{9,1},... | collective-permute-start | bytes 811016 | tf_op jit(solution)/shard_map/ppermute | solution.py:223
  10.5 20.7 %collective-permute-start.10 = (bf16[2048,128]{1,0:T(8,128)(2,1)S(1)}, bf16[2048,128]{1,0:T(8,128)(2,1)S(1)}, u32[]{:S(2)}, u32[]{:S(2)}) collective-permute-start(bf16[2048,128]{1,0:T(8,128)(2,1)S(1)} %copy-done.1), channel_id=1, source_target_pairs={{0,1},{1,0},{2,3},{3,2},{4,5},{5,4},{6,7},{7,6},{8,9},{9,8},{10,11... | collective-permute-start | bytes 1572872 | tf_op jit(solution)/shard_map/ppermute | solution.py:223
  10.5 10.0 %collective-permute-start.1 = (bf16[2,528,128]{2,1,0:T(8,128)(2,1)S(1)}, bf16[2,528,128]{2,1,0:T(8,128)(2,1)S(1)}, u32[]{:S(2)}, u32[]{:S(2)}) collective-permute-start(bf16[2,528,128]{2,1,0:T(8,128)(2,1)S(1)} %pad_maximum_fusion.own_ref), channel_id=1, source_target_pairs={{0,2},{1,3},{2,4},{3,5},{4,6},{5,7},{6,0},{7,1},{8,10},{9,11},{10,... | collective-permute-start | bytes 811016 | tf_op jit(solution)/shard_map/ppermute | solution.py:223
  12.0 10.1 %collective-permute-start.2 = (bf16[2,528,128]{2,1,0:T(8,128)(2,1)S(1)}, bf16[2,528,128]{2,1,0:T(8,128)(2,1)S(1)}, u32[]{:S(2)}, u32[]{:S(2)}) collective-permute-start(bf16[2,528,128]{2,1,0:T(8,128)(2,1)S(1)} %pad_maximum_fusion.own_ref), channel_id=1, source_target_pairs={{0,6},{1,7},{2,0},{3,1},{4,2},{5,3},{6,4},{7,5},{8,14},{9,15},{10,... | collective-permute-start | bytes 811016 | tf_op jit(solution)/shard_map/ppermute | solution.py:223
  18.4 9.3 %collective-permute-start.6 = (bf16[2,528,128]{2,1,0:T(8,128)(2,1)S(1)}, bf16[2,528,128]{2,1,0:T(8,128)(2,1)S(1)}, u32[]{:S(2)}, u32[]{:S(2)}) collective-permute-start(bf16[2,528,128]{2,1,0:T(8,128)(2,1)S(1)} %collective-permute-done.5.far_ref), channel_id=1, source_target_pairs={{0,2},{1,3},{2,4},{3,5},{4,6},{5,7},{6,0},{7,1},{8,10},{9,11},{10,... | collective-permute-start | bytes 811016 | tf_op jit(solution)/shard_map/ppermute | solution.py:223
  20.0 10.0 %collective-permute-start.7 = (bf16[2,528,128]{2,1,0:T(8,128)(2,1)S(1)}, bf16[2,528,128]{2,1,0:T(8,128)(2,1)S(1)}, u32[]{:S(2)}, u32[]{:S(2)}) collective-permute-start(bf16[2,528,128]{2,1,0:T(8,128)(2,1)S(1)} %collective-permute-done.5.far_ref), channel_id=1, source_target_pairs={{0,6},{1,7},{2,0},{3,1},{4,2},{5,3},{6,4},{7,5},{8,14},{9,15},{10,... | collective-permute-start | bytes 811016 | tf_op jit(solution)/shard_map/ppermute | solution.py:223
  20.4 10.7 %collective-permute-start.3 = (bf16[1,528,128]{2,1,0:T(8,128)(2,1)S(1)}, bf16[1,528,128]{2,1,0:T(8,128)(2,1)S(1)}, u32[]{:S(2)}, u32[]{:S(2)}) collective-permute-start(bf16[1,528,128]{2,1,0:T(8,128)(2,1)S(1)} %slice.24), channel_id=1, source_target_pairs={{0,2},{1,3},{2,4},{3,5},{4,6},{5,7},{6,0},{7,1},{8,10},{9,11},{10,... | collective-permute-start | bytes 405512 | tf_op jit(solution)/shard_map/ppermute | solution.py:223
  22.8 8.4 %collective-permute-start.4 = (bf16[1,528,128]{2,1,0:T(8,128)(2,1)}, bf16[1,528,128]{2,1,0:T(8,128)(2,1)S(1)}, u32[]{:S(2)}, u32[]{:S(2)}) collective-permute-start(bf16[1,528,128]{2,1,0:T(8,128)(2,1)} %slice.25), channel_id=1, source_target_pairs={{0,6},{1,7},{2,0},{3,1},{4,2},{5,3},{6,4},{7,5},{8,14},{9,15},{10,... | collective-permute-start | bytes 405512 | tf_op jit(solution)/shard_map/ppermute | solution.py:223
  28.4 5.2 %collective-permute-start.8 = (bf16[1,528,128]{2,1,0:T(8,128)(2,1)}, bf16[1,528,128]{2,1,0:T(8,128)(2,1)S(1)}, u32[]{:S(2)}, u32[]{:S(2)}) collective-permute-start(bf16[1,528,128]{2,1,0:T(8,128)(2,1)} %slice.26), channel_id=1, source_target_pairs={{0,2},{1,3},{2,4},{3,5},{4,6},{5,7},{6,0},{7,1},{8,10},{9,11},{10,... | collective-permute-start | bytes 405512 | tf_op jit(solution)/shard_map/ppermute | solution.py:223
  30.6 5.2 %collective-permute-start.9 = (bf16[1,528,128]{2,1,0:T(8,128)(2,1)}, bf16[1,528,128]{2,1,0:T(8,128)(2,1)S(1)}, u32[]{:S(2)}, u32[]{:S(2)}) collective-permute-start(bf16[1,528,128]{2,1,0:T(8,128)(2,1)} %slice.27), channel_id=1, source_target_pairs={{0,6},{1,7},{2,0},{3,1},{4,2},{5,3},{6,4},{7,5},{8,14},{9,15},{10,... | collective-permute-start | bytes 405512 | tf_op jit(solution)/shard_map/ppermute | solution.py:223
  38.1 10.3 %copy-start.8 = (bf16[24,128]{1,0:T(8,128)(2,1)S(1)}, bf16[24,128]{1,0:T(8,128)(2,1)}, u32[]{:S(2)}) copy-start(bf16[24,128]{1,0:T(8,128)(2,1)} %param.15) | copy-start | bytes 18436
  38.1 19.4 %all-to-all-start = ((bf16[16,64,128]{2,1,0:T(8,128)(2,1)}), bf16[16,64,128]{2,1,0:T(8,128)(2,1)S(1)}, u32[]{:S(2)}, u32[]{:S(2)}) async-start(bf16[16,64,128]{2,1,0:T(8,128)(2,1)} %shard_map.109), calls=%async_computation | async-start | bytes 524288 | tf_op jit(solution)/shard_map/all_to_all | solution.py:285
  48.4 0.7 copy-start.9
  57.5 4.0 %copy-start.7 = (bf16[2,256,256]{2,1,0:T(8,128)(2,1)S(1)}, bf16[2,256,256]{2,1,0:T(8,128)(2,1)}, u32[]{:S(2)}) copy-start(bf16[2,256,256]{2,1,0:T(8,128)(2,1)} %constant.71.clone) | copy-start | bytes 786436
  57.5 12.8 %all-to-all-start.1 = ((bf16[16,64,128]{2,1,0:T(8,128)(2,1)}), bf16[16,64,128]{2,1,0:T(8,128)(2,1)S(1)}, u32[]{:S(2)}, u32[]{:S(2)}) async-start(bf16[16,64,128]{2,1,0:T(8,128)(2,1)} %fusion.2), calls=%async_computation.1 | async-start | bytes 524288 | tf_op jit(solution)/shard_map/all_to_all | solution.py:263
  61.2 9.1 %copy-start.2 = (bf16[2,256,256]{2,1,0:T(8,128)(2,1)S(1)}, bf16[2,256,256]{2,1,0:T(8,128)(2,1)}, u32[]{:S(2)}) copy-start(bf16[2,256,256]{2,1,0:T(8,128)(2,1)} %constant.70.clone.second_ref) | copy-start | bytes 786436
  61.2 9.1 %copy-start.4 = (f32[2,128,128]{2,1,0:T(8,128)S(1)}, f32[2,128,128]{2,1,0:T(8,128)}, u32[]{:S(2)}) copy-start(f32[2,128,128]{2,1,0:T(8,128)} %constant.69.clone.turn_ref) | copy-start | bytes 393220
  61.2 9.1 %copy-start.6 = (bf16[256,256]{1,0:T(8,128)(2,1)S(1)}, bf16[256,256]{1,0:T(8,128)(2,1)}, u32[]{:S(2)}) copy-start(bf16[256,256]{1,0:T(8,128)(2,1)} %constant.75.first_ref) | copy-start | bytes 393220
  61.2 10.1 %collective-permute-start.11 = (bf16[16,32,128]{2,1,0:T(8,128)(2,1)S(1)}, bf16[16,32,128]{2,1,0:T(8,128)(2,1)S(1)}, u32[]{:S(2)}, u32[]{:S(2)}) collective-permute-start(bf16[16,32,128]{2,1,0:T(8,128)(2,1)S(1)} %slice.28), channel_id=1, source_target_pairs={{0,1},{1,0},{2,3},{3,2},{4,5},{5,4},{6,7},{7,6},{8,9},{9,8},{10,11... | collective-permute-start | bytes 393224 | tf_op jit(solution)/shard_map/ppermute | solution.py:223
  61.5 9.8 %copy-start.3 = (bf16[2,256,256]{2,1,0:T(8,128)(2,1)S(1)}, bf16[2,256,256]{2,1,0:T(8,128)(2,1)}, u32[]{:S(2)}) copy-start(bf16[2,256,256]{2,1,0:T(8,128)(2,1)} %constant.72.clone.back_ref) | copy-start | bytes 786436
  61.5 9.8 %copy-start.5 = (bf16[2,128,256]{2,1,0:T(8,128)(2,1)S(1)}, bf16[2,128,256]{2,1,0:T(8,128)(2,1)}, u32[]{:S(2)}) copy-start(bf16[2,128,256]{2,1,0:T(8,128)(2,1)} %constant.73.clone.last_ref) | copy-start | bytes 393220
  (1 other events, 0.7 us)

commit v2 on v1

--- a/solution.py
+++ b/solution.py
@@ -1,3 +1,4 @@
+import functools
 import math
 
 import jax
@@ -88,27 +89,28 @@
     ).astype(BF16)
 
 
-def filter_kernel(blocks_ref, first_ref, turn_ref, second_ref, out_ref, unpacked):
-    unpacked[...] = blocks_ref[...].astype(F32).reshape(CTX * BLOCKS * SHARE, LANES)
-    for at in range(SHARE // 2):
-        out_ref[pl.ds(at * 2 * LANES, 2 * LANES), :] = spectrum_of_pair(
-            load_pair(unpacked, at), first_ref[...], turn_ref[0], turn_ref[1], second_ref
-        )
+def unpack(ref, values):
+    ref[...] = values.astype(F32).reshape(CTX * BLOCKS * SHARE, LANES)
 
 
 def mix_kernel(
-    own_ref, other_ref, response_ref, first_ref, turn_ref, second_ref, back_ref, last_ref,
-    out_ref, unpacked, gathered,
+    place_ref, own_ref, other_ref, first_ref, turn_ref, second_ref, back_ref, last_ref,
+    out_ref, signals, responses, gathered,
 ):
-    half = BLOCKS * SHARE // 2
-    both = jnp.concatenate([own_ref[:, :half, :], other_ref[...]], axis=1)
-    unpacked[...] = both.astype(F32).reshape(CTX * BLOCKS * SHARE, LANES)
+    full = BLOCKS * SHARE
+    half = full // 2
+    unpack(signals, jnp.concatenate([own_ref[:, :half, :], other_ref[...]], axis=1))
+    unpack(responses, own_ref[:, full:, :])
     turn_real, turn_imag = turn_ref[0], turn_ref[1]
+    first_here = first_ref[place_ref[2]]
+    first = first_ref[0]
     for at in range(SHARE // 2):
         signal = spectrum_of_pair(
-            load_pair(unpacked, at), first_ref[...], turn_real, turn_imag, second_ref
-        )
-        response = response_ref[pl.ds(at * 2 * LANES, 2 * LANES), :]
+            load_pair(signals, at), first_here, turn_real, turn_imag, second_ref
+        )
+        response = spectrum_of_pair(
+            load_pair(responses, at), first, turn_real, turn_imag, second_ref
+        )
         sig_real, sig_imag = signal[:, :LANES], signal[:, LANES:]
         res_real, res_imag = response[:, :LANES], response[:, LANES:]
         product = jnp.concatenate(
@@ -130,35 +132,24 @@
             gathered[pl.ds(2 * at + k, LANES, stride=SHARE), :] = result[
                 :, k * LANES : (k + 1) * LANES
             ]
-    out_ref[...] = gathered[...].reshape(CTX, BLOCKS * SHARE, LANES).astype(BF16)
-
-
-def project_kernel(
-    place_ref, own_ref, left_ref, right_ref, mid_a_ref, mid_b_ref,
-    far_ref, far_left_ref, far_right_ref, far_mid_a_ref, far_mid_b_ref,
-    w_own_ref, w_other_ref, out_ref,
-):
+    out_ref[...] = gathered[...].reshape(CTX, full, LANES).astype(BF16)
+
+
+def project_kernel(pieces, place_ref, *refs):
     high, along, core = place_ref[0], place_ref[1], place_ref[2]
-    pieces = [
-        (0, 0, own_ref, 0, own_ref, 1),
-        (0, YS - 1, left_ref, 0, left_ref, 1),
-        (0, 1, right_ref, 0, right_ref, 1),
-        (0, 2, mid_a_ref, 0, mid_b_ref, 0),
-        (1, 0, far_ref, 0, far_ref, 1),
-        (1, YS - 1, far_left_ref, 0, far_left_ref, 1),
-        (1, 1, far_right_ref, 0, far_right_ref, 1),
-        (1, 2, far_mid_a_ref, 0, far_mid_b_ref, 0),
-    ]
+    *piece_refs, w_own_ref, w_other_ref, response_ref, out_ref = refs
+    count = HALF // LANES
     total = jnp.zeros((HALF, 2 * LANES), F32)
     squares = jnp.zeros((HALF, LANES), F32)
-    for d_high, d_along, ref_a, at_a, ref_b, at_b in pieces:
+    for d_high, d_along, *slots in pieces:
         chip = lax.rem(high + d_high, HI) * YS + lax.rem(along + d_along, YS)
         scaled, weights = [], []
-        for slot, (ref, at) in enumerate(((ref_a, at_a), (ref_b, at_b))):
-            values = ref[at, :HALF, :].astype(F32)
+        for slot, (at, lead) in enumerate(slots):
+            ref = piece_refs[at]
+            block = ref[...] if lead is None else ref[lead]
+            values = block[:HALF].astype(F32)
             squares = squares + values * values
-            gain = ref[at, HALF : HALF + PAD, :].astype(F32)[:1]
-            scaled.append((values * gain).astype(BF16))
+            scaled.append((values * block[HALF:].astype(F32)[:1]).astype(BF16))
             owner = chip * CORES + (core if slot == 0 else 1 - core)
             start = pl.multiple_of(owner * LANES, LANES)
             weights.append(
@@ -171,16 +162,16 @@
     power = jnp.sum(squares, axis=1, keepdims=True) * (1.0 / FEATURES)
     total = total * lax.rsqrt(power + EPS)
     for slot in range(CORES):
-        for pair in range(BLOCKS // CORES // 2):
+        for pair in range(count // 2):
             parts = []
-            for k in range(2):
-                block = 2 * pair + k
+            for block in (2 * pair, 2 * pair + 1):
                 part = total[
                     block * LANES : (block + 1) * LANES, slot * LANES : (slot + 1) * LANES
                 ]
                 parts.append(part.T.reshape(CTX, SHARE, LANES))
-            start = slot * (BLOCKS * SHARE // 2) + pair * 2 * SHARE
+            start = (slot * count + 2 * pair) * SHARE
             out_ref[:, start : start + 2 * SHARE, :] = jnp.concatenate(parts, axis=1).astype(BF16)
+    out_ref[:, BLOCKS * SHARE :, :] = response_ref[...]
 
 
 def turn_kernel(blocks_ref, out_ref):
@@ -197,17 +188,21 @@
 PARAMS = pltpu.CompilerParams(vmem_limit_bytes=48 * 1024 * 1024)
 
 
-def call(kernel, shape, dtype, operands, scratch=(), first_spec=VMEM, flops=0):
+def call(kernel, outs, operands, scratch=(), first_spec=VMEM, flops=0):
     moved = sum(x.size * x.dtype.itemsize for x in operands)
     return pl.pallas_call(
         kernel,
-        out_shape=jax.ShapeDtypeStruct(shape, dtype),
+        out_shape=outs,
         in_specs=[first_spec] + [VMEM] * (len(operands) - 1),
-        out_specs=VMEM,
+        out_specs=jax.tree.map(lambda _: VMEM, outs),
         scratch_shapes=list(scratch),
         compiler_params=PARAMS,
         cost_estimate=pl.CostEstimate(flops=flops, bytes_accessed=moved, transcendentals=0),
     )(*operands)
+
+
+def bf16(*shape):
+    return jax.ShapeDtypeStruct(shape, BF16)
 
 
 def tp_shift(value, d_high, d_along, d_core):
@@ -223,12 +218,79 @@
     return lax.ppermute(value, "tp", pairs)
 
 
-def rings(piece):
-    left = tp_shift(piece, 0, 1, 0)
-    right = tp_shift(piece, 0, YS - 1, 0)
-    mid_a = tp_shift(left[:1], 0, 1, 0)
-    mid_b = tp_shift(right[1:], 0, YS - 1, 0)
-    return left, right, mid_a, mid_b
+AG = "G6"
+
+
+def gather(mine, theirs):
+    def left(x, swap=0):
+        return tp_shift(x, 0, 1, swap)
+
+    def right(x, swap=0):
+        return tp_shift(x, 0, YS - 1, swap)
+
+    arrived = tp_shift(theirs, 0, 0, 1)
+    out, pieces = [], []
+
+    def add(d_high, d_along, *slots):
+        entry = [d_high, d_along]
+        for value, lead in slots:
+            for at, known in enumerate(out):
+                if known is value:
+                    break
+            else:
+                at = len(out)
+                out.append(value)
+            entry.append((at, lead))
+        pieces.append(tuple(entry))
+
+    def add_whole(d_high, d_along, value):
+        add(d_high, d_along, (value, 0), (value, 1))
+
+    def ring_whole(d_high, value):
+        l, r = left(value), right(value)
+        ma, mb = left(l[0]), right(r[1])
+        add_whole(d_high, 0, value)
+        add_whole(d_high, YS - 1, l)
+        add_whole(d_high, 1, r)
+        add(d_high, 2, (ma, None), (mb, None))
+
+    def ring_slots(d_high, a, b, src=None, swap=0):
+        src = b if src is None else src
+        la, rb = left(a), right(src, swap)
+        ra, lb = right(a), left(src, swap)
+        ma, mb = left(la), right(rb)
+        add(d_high, 0, (a, None), (b, None))
+        add(d_high, YS - 1, (la, None), (lb, None))
+        add(d_high, 1, (ra, None), (rb, None))
+        add(d_high, 2, (ma, None), (mb, None))
+
+    own = jnp.stack([mine, arrived])
+    if AG == "G1":
+        far = tp_shift(own, 1, 0, 0)
+        ring_whole(0, own)
+        ring_whole(1, far)
+    elif AG == "G2":
+        za, zb = tp_shift(mine, 1, 0, 0), tp_shift(arrived, 1, 0, 0)
+        ring_whole(0, own)
+        ring_slots(1, za, zb)
+    elif AG == "G3":
+        za, zb = tp_shift(mine, 1, 0, 0), tp_shift(arrived, 1, 0, 0)
+        ring_slots(0, mine, arrived)
+        ring_slots(1, za, zb)
+    elif AG == "G4":
+        za, zb = tp_shift(mine, 1, 0, 0), tp_shift(theirs, 1, 0, 1)
+        ring_slots(0, mine, arrived, theirs, 1)
+        ring_slots(1, za, zb)
+    elif AG == "G5":
+        za, zb = tp_shift(mine, 1, 0, 0), tp_shift(theirs, 1, 0, 1)
+        ring_whole(0, own)
+        ring_slots(1, za, zb)
+    elif AG == "G6":
+        za, zb = tp_shift(mine, 1, 0, 0), tp_shift(theirs, 1, 0, 1)
+        far = jnp.stack([za, zb])
+        ring_whole(0, own)
+        ring_whole(1, far)
+    return out, tuple(pieces)
 
 
 def on_device(tokens, gain, w_inputs, filters, w_plus, w_minus):
@@ -240,13 +302,13 @@
     ).astype(jnp.int32)
 
     gain_rows = jnp.broadcast_to(gain[None, :], (PAD, LANES))
-    mine = lax.dynamic_slice_in_dim(tokens, core * HALF, HALF, axis=0)
-    theirs = lax.dynamic_slice_in_dim(tokens, (1 - core) * HALF, HALF, axis=0)
-    arrived = tp_shift(jnp.concatenate([theirs, gain_rows], axis=0), 0, 0, 1)
-    own = jnp.stack([jnp.concatenate([mine, gain_rows], axis=0), arrived])
-    far = tp_shift(own, 1, 0, 0)
-    near_parts = rings(own)
-    far_parts = rings(far)
+    mine, theirs = (
+        jnp.concatenate(
+            [lax.dynamic_slice_in_dim(tokens, half * HALF, HALF, axis=0), gain_rows], axis=0
+        )
+        for half in (core, 1 - core)
+    )
+    gathered, pieces = gather(mine, theirs)
     w_other = tp_shift(w_inputs, 0, 0, 1)
 
     lag_sign = 1.0 - 2.0 * (lax.iota(jnp.int32, ROWS) % 2).astype(F32)
@@ -260,49 +322,28 @@
         .astype(BF16)
         .reshape(CTX, BLOCKS * SHARE, LANES)
     )
-    response = lax.all_to_all(response, "ctx", split_axis=0, concat_axis=0, tiled=True)
-    unpacked = pltpu.VMEM((CTX * BLOCKS * SHARE, LANES), F32)
-    turn, second = jnp.asarray(table["turn"]), jnp.asarray(table["second"])
-    first = jnp.asarray(table["first"])
-    response = call(
-        filter_kernel,
-        (SHARE * LANES, 2 * LANES),
-        F32,
-        [response, first[0], turn, second],
-        [unpacked],
-        flops=10**9,
-    )
-
-    operands = [place, own, *near_parts, far, *far_parts, w_inputs, w_other]
+
     blocks = call(
-        project_kernel,
-        (CTX, BLOCKS * SHARE, LANES),
-        BF16,
-        operands,
+        functools.partial(project_kernel, pieces),
+        bf16(CTX, 2 * BLOCKS * SHARE, LANES),
+        [place, *gathered, w_inputs, w_other, response],
         first_spec=SMEM,
         flops=2 * HALF * 2 * LANES * FEATURES,
     )
     blocks = lax.all_to_all(blocks, "ctx", split_axis=0, concat_axis=0, tiled=True)
-    other = tp_shift(blocks[:, BLOCKS * SHARE // 2 :, :], 0, 0, 1)
+    other = tp_shift(blocks[:, BLOCKS * SHARE // 2 : BLOCKS * SHARE, :], 0, 0, 1)
+    consts = [jnp.asarray(table[k]) for k in ("first", "turn", "second", "second_back", "last")]
+    unpacked = pltpu.VMEM((CTX * BLOCKS * SHARE, LANES), F32)
     mixed = call(
         mix_kernel,
-        (CTX, BLOCKS * SHARE, LANES),
-        BF16,
-        [
-            blocks,
-            other,
-            response,
-            lax.dynamic_index_in_dim(first, core, axis=0, keepdims=False),
-            turn,
-            second,
-            jnp.asarray(table["second_back"]),
-            jnp.asarray(table["last"]),
-        ],
-        [unpacked, unpacked],
-        flops=2 * 10**9,
+        bf16(CTX, BLOCKS * SHARE, LANES),
+        [place, blocks, other, *consts],
+        [unpacked, unpacked, unpacked],
+        first_spec=SMEM,
+        flops=3 * 10**9,
     )
     mixed = lax.all_to_all(mixed, "ctx", split_axis=0, concat_axis=0, tiled=True)
-    return call(turn_kernel, (ROWS, LANES), BF16, [mixed])
+    return call(turn_kernel, bf16(ROWS, LANES), [mixed])
 
 
 def solution(mesh):

time: 89.2 us -> 81.1 us (0.909)
  the two profiles are of different devices: /device:TPU:8 before, /device:TPU:1 now
where the time goes in v2:
time: 81.1 us; the launch traced here: 80.9 us
  starting transfers between devices  30.3 us (37%)
  blocking collectives  29.5 us (36%)
  waiting for transfers between devices  11.8 us (15%)
  Pallas kernels  6.27 us (8%)
  local copies, waits for them, and re-layouts  1.84 us (2%)
  matrix products  0.84 us (1%)
    ppermute x13, starting transfers between devices, tp_shift(): return lax.ppermute(value, 'tp', pairs)  30.3 us
    all_to_all x1, blocking collectives, on_device(): lax.all_to_all(blocks, 'ctx', split_axis=0, concat_axis=0, tiled=True)  16.8 us
    all_to_all x1, blocking collectives, on_device(): lax.all_to_all(mixed, 'ctx', split_axis=0, concat_axis=0, tiled=True)  12.6 us
    ppermute x13, waiting for transfers between devices, tp_shift(): return lax.ppermute(value, 'tp', pairs)  11.8 us
    pallas_call x3, Pallas kernels, call(): pl.pallas_call(kernel, out_shape=outs, in_specs=[first_spec] + [VMEM] * (...  6.27 us
  transfers between devices with their start and end apart: 13, of which 5 were waited for; matrix products, arithmetic and copies ran while one was open for 1% of the time, Pallas kernels for 0%

profile of v2, /device:TPU:1, one launch (start us, length us, event | category | flops | bytes accessed | tf_op | source)
XLA Modules:
  0.0 80.9 jit_solution(13579476086785782711)
XLA Ops:
  0.0 1.1 %constant_dynamic-slice_fusion.1 = (bf16[512,128]{1,0:T(8,128)(2,1)S(1)}, bf16[512,128]{1,0:T(8,128)(2,1)S(1)}) fusion(bf16[1024,128]{1,0:T(8,128)(2,1)} %param.11, s32[]{:T(128)S(6)} %select_n.26, s32[]{:T(128)S(6)} %select_n.27), kind=kLoop, calls=%fused_computation.22 | loop fusion | bytes 524296 | tf_op jit(solution)/shard_map/dynamic_slice | solution.py:307
  1.1 8.4 %collective-permute-start.6 = (bf16[528,128]{1,0:T(8,128)(2,1)S(1)}, bf16[528,128]{1,0:T(8,128)(2,1)S(1)}, u32[]{:S(2)}, u32[]{:S(2)}) collective-permute-start(bf16[528,128]{1,0:T(8,128)(2,1)S(1)} %get-tuple-element.9), channel_id=1, source_target_pairs={{0,9},{1,8},{2,11},{3,10},{4,13},{5,12},{6,15},{7,14},{8,1},{9,0},... | collective-permute-start | bytes 405512 | tf_op jit(solution)/shard_map/ppermute | solution.py:218
  9.5 0.2 collective-permute-start.5
  9.7 0.8 collective-permute-start.11
  10.5 0.7 copy-done.7
  11.2 0.4 fusion.10
  11.7 2.4 %collective-permute-start.2 = (bf16[2,528,128]{2,1,0:T(8,128)(2,1)S(1)}, bf16[2,528,128]{2,1,0:T(8,128)(2,1)S(1)}, u32[]{:S(2)}, u32[]{:S(2)}) collective-permute-start(bf16[2,528,128]{2,1,0:T(8,128)(2,1)S(1)} %pad_maximum_fusion.refs_0_), channel_id=1, source_target_pairs={{0,6},{1,7},{2,0},{3,1},{4,2},{5,3},{6,4},{7,5},{8,14},{9,15},{10,... | collective-permute-start | bytes 811016 | tf_op jit(solution)/shard_map/ppermute | solution.py:218
  14.2 4.0 %collective-permute-done.5 = bf16[528,128]{1,0:T(8,128)(2,1)S(1)} collective-permute-done((bf16[528,128]{1,0:T(8,128)(2,1)S(1)}, bf16[528,128]{1,0:T(8,128)(2,1)S(1)}, u32[]{:S(2)}, u32[]{:S(2)}) %collective-permute-start.5) | collective-permute-done | bytes 135200 | tf_op jit(solution)/shard_map/ppermute | solution.py:218
  18.2 6.1 %collective-permute-start.8 = (bf16[2,528,128]{2,1,0:T(8,128)(2,1)S(1)}, bf16[2,528,128]{2,1,0:T(8,128)(2,1)S(1)}, u32[]{:S(2)}, u32[]{:S(2)}) collective-permute-start(bf16[2,528,128]{2,1,0:T(8,128)(2,1)S(1)} %pad_maximum_fusion.1.refs_5_), channel_id=1, source_target_pairs={{0,6},{1,7},{2,0},{3,1},{4,2},{5,3},{6,4},{7,5},{8,14},{9,15},{10,... | collective-permute-start | bytes 811016 | tf_op jit(solution)/shard_map/ppermute | solution.py:218
  24.3 2.8 %collective-permute-start.4 = (bf16[528,128]{1,0:T(8,128)(2,1)S(1)}, bf16[528,128]{1,0:T(8,128)(2,1)S(1)}, u32[]{:S(2)}, u32[]{:S(2)}) collective-permute-start(bf16[528,128]{1,0:T(8,128)(2,1)S(1)} %slice_bitcast_fusion.2), channel_id=1, source_target_pairs={{0,6},{1,7},{2,0},{3,1},{4,2},{5,3},{6,4},{7,5},{8,14},{9,15},{10,... | collective-permute-start | bytes 405512 | tf_op jit(solution)/shard_map/ppermute | solution.py:218
  27.1 0.1 collective-permute-start.3
  27.2 1.8 %collective-permute-done.8.refs_7_ = bf16[2,528,128]{2,1,0:T(8,128)(2,1)S(1)} collective-permute-done((bf16[2,528,128]{2,1,0:T(8,128)(2,1)S(1)}, bf16[2,528,128]{2,1,0:T(8,128)(2,1)S(1)}, u32[]{:S(2)}, u32[]{:S(2)}) %collective-permute-start.8) | collective-permute-done | bytes 270368 | tf_op jit(solution)/shard_map/ppermute | solution.py:218
  29.0 3.5 %collective-permute-start.10 = (bf16[528,128]{1,0:T(8,128)(2,1)S(1)}, bf16[528,128]{1,0:T(8,128)(2,1)S(1)}, u32[]{:S(2)}, u32[]{:S(2)}) collective-permute-start(bf16[528,128]{1,0:T(8,128)(2,1)S(1)} %slice_bitcast_fusion), channel_id=1, source_target_pairs={{0,6},{1,7},{2,0},{3,1},{4,2},{5,3},{6,4},{7,5},{8,14},{9,15},{10,... | collective-permute-start | bytes 405512 | tf_op jit(solution)/shard_map/ppermute | solution.py:218
  32.5 0.1 collective-permute-start.9
  32.6 0.4 fusion.2.refs_12_
  33.1 1.9 %collective-permute-done.3.refs_3_ = bf16[528,128]{1,0:T(8,128)(2,1)S(1)} collective-permute-done((bf16[528,128]{1,0:T(8,128)(2,1)S(1)}, bf16[528,128]{1,0:T(8,128)(2,1)S(1)}, u32[]{:S(2)}, u32[]{:S(2)}) %collective-permute-start.3) | collective-permute-done | bytes 135200 | tf_op jit(solution)/shard_map/ppermute | solution.py:218
  35.0 3.1 %collective-permute-done.9.refs_8_ = bf16[528,128]{1,0:T(8,128)(2,1)S(1)} collective-permute-done((bf16[528,128]{1,0:T(8,128)(2,1)S(1)}, bf16[528,128]{1,0:T(8,128)(2,1)S(1)}, u32[]{:S(2)}, u32[]{:S(2)}) %collective-permute-start.9) | collective-permute-done | bytes 135200 | tf_op jit(solution)/shard_map/ppermute | solution.py:218
  38.1 1.5 %shard_map.109 = bf16[16,128,128]{2,1,0:T(8,128)(2,1)S(1)} custom-call(s32[4]{0:T(128)S(1)} %pad_add_fusion.place_ref, bf16[2,528,128]{2,1,0:T(8,128)(2,1)S(1)} %pad_maximum_fusion.refs_0_, bf16[2,528,128]{2,1,0:T(8,128)(2,1)S(1)} %collective-permute-done.1.refs_1_, bf16[2,528,128]{2,1,0:T(8,128)(2,1)S(1)} %collective-permute-done.2.refs_2_, ...), custom_call_target="tpu_custom_call" | custom-call | flops 536870912 | bytes 3473424 | tf_op jit(solution)/shard_map/pallas_call | solution.py:193
  39.6 16.8 %all_to_all.10.own_ref = bf16[16,128,128]{2,1,0:T(8,128)(2,1)S(1)} all-to-all(bf16[16,128,128]{2,1,0:T(8,128)(2,1)S(1)} %shard_map.109), channel_id=1, replica_groups=mesh['ctx'=16,'tp'=16] {'ctx'}, dimensions={0} | all-to-all | bytes 1048576 | tf_op jit(solution)/shard_map/all_to_all | solution.py:333
  56.5 6.0 %collective-permute-start.12 = (bf16[16,32,128]{2,1,0:T(8,128)(2,1)S(1)}, bf16[16,32,128]{2,1,0:T(8,128)(2,1)S(1)}, u32[]{:S(2)}, u32[]{:S(2)}) collective-permute-start(bf16[16,32,128]{2,1,0:T(8,128)(2,1)S(1)} %slice.24), channel_id=1, source_target_pairs={{0,1},{1,0},{2,3},{3,2},{4,5},{5,4},{6,7},{7,6},{8,9},{9,8},{10,11... | collective-permute-start | bytes 393224 | tf_op jit(solution)/shard_map/ppermute | solution.py:218
  62.4 1.0 %collective-permute-done.12.other_ref = bf16[16,32,128]{2,1,0:T(8,128)(2,1)S(1)} collective-permute-done((bf16[16,32,128]{2,1,0:T(8,128)(2,1)S(1)}, bf16[16,32,128]{2,1,0:T(8,128)(2,1)S(1)}, u32[]{:S(2)}, u32[]{:S(2)}) %collective-permute-start.12) | collective-permute-done | bytes 131104 | tf_op jit(solution)/shard_map/ppermute | solution.py:218
  63.4 3.9 %shard_map.110 = bf16[16,64,128]{2,1,0:T(8,128)(2,1)S(1)} custom-call(s32[4]{0:T(128)S(1)} %pad_add_fusion.place_ref, bf16[16,128,128]{2,1,0:T(8,128)(2,1)S(1)} %all_to_all.10.own_ref, bf16[16,32,128]{2,1,0:T(8,128)(2,1)S(1)} %collective-permute-done.12.other_ref, bf16[2,256,256]{2,1,0:T(8,128)(2,1)S(1)} %copy-done.4, f32[2,128,128]{2,1,0:T(8,128)S(1)} %copy-done.6, ...), custom_call_target="tpu_custom_call" | custom-call | flops 3000000000 | bytes 1703952 | tf_op jit(solution)/shard_map/pallas_call | solution.py:193
  67.4 12.6 %all_to_all.11.blocks_ref = bf16[16,64,128]{2,1,0:T(8,128)(2,1)S(1)} all-to-all(bf16[16,64,128]{2,1,0:T(8,128)(2,1)S(1)} %shard_map.110), channel_id=1, replica_groups=mesh['ctx'=16,'tp'=16] {'ctx'}, dimensions={0} | all-to-all | bytes 524288 | tf_op jit(solution)/shard_map/all_to_all | solution.py:345
  80.0 0.8 %shard_map.111 = bf16[1024,128]{1,0:T(8,128)(2,1)} custom-call(bf16[16,64,128]{2,1,0:T(8,128)(2,1)S(1)} %all_to_all.11.blocks_ref), custom_call_target="tpu_custom_call" | custom-call | bytes 262144 | tf_op jit(solution)/shard_map/pallas_call | solution.py:193
  (41 shorter events, 0.3 us)
Async XLA Ops:
  0.0 10.5 %copy-start = (f32[24,1024]{1,0:T(8,128)S(1)}, f32[24,1024]{1,0:T(8,128)}, u32[]{:S(2)}) copy-start(f32[24,1024]{1,0:T(8,128)} %param.14) | copy-start | bytes 294916
  0.0 1.1 %copy-start.9 = (bf16[128]{0:T(256)(128)(2,1)S(1)}, bf16[128]{0:T(256)(128)(2,1)}, u32[]{:S(2)}) copy-start(bf16[128]{0:T(256)(128)(2,1)} %param.12) | copy-start | bytes 772
  0.0 9.7 %copy-start.1 = (bf16[2048,128]{1,0:T(8,128)(2,1)S(1)}, bf16[2048,128]{1,0:T(8,128)(2,1)}, u32[]{:S(2)}) copy-start(bf16[2048,128]{1,0:T(8,128)(2,1)} %refs_10_.1) | copy-start | bytes 1572868
  1.1 17.0 %collective-permute-start.6 = (bf16[528,128]{1,0:T(8,128)(2,1)S(1)}, bf16[528,128]{1,0:T(8,128)(2,1)S(1)}, u32[]{:S(2)}, u32[]{:S(2)}) collective-permute-start(bf16[528,128]{1,0:T(8,128)(2,1)S(1)} %get-tuple-element.9), channel_id=1, source_target_pairs={{0,9},{1,8},{2,11},{3,10},{4,13},{5,12},{6,15},{7,14},{8,1},{9,0},... | collective-permute-start | bytes 405512 | tf_op jit(solution)/shard_map/ppermute | solution.py:218
  9.5 2.1 %collective-permute-start = (bf16[528,128]{1,0:T(8,128)(2,1)S(1)}, bf16[528,128]{1,0:T(8,128)(2,1)S(1)}, u32[]{:S(2)}, u32[]{:S(2)}) collective-permute-start(bf16[528,128]{1,0:T(8,128)(2,1)S(1)} %get-tuple-element.9), channel_id=1, source_target_pairs={{0,1},{1,0},{2,3},{3,2},{4,5},{5,4},{6,7},{7,6},{8,9},{9,8},{10,11... | collective-permute-start | bytes 405512 | tf_op jit(solution)/shard_map/ppermute | solution.py:218
  9.5 8.6 %collective-permute-start.5 = (bf16[528,128]{1,0:T(8,128)(2,1)S(1)}, bf16[528,128]{1,0:T(8,128)(2,1)S(1)}, u32[]{:S(2)}, u32[]{:S(2)}) collective-permute-start(bf16[528,128]{1,0:T(8,128)(2,1)S(1)} %get-tuple-element.7), channel_id=1, source_target_pairs={{0,8},{1,9},{2,10},{3,11},{4,12},{5,13},{6,14},{7,15},{8,0},{9,1},... | collective-permute-start | bytes 405512 | tf_op jit(solution)/shard_map/ppermute | solution.py:218
  9.7 23.3 %collective-permute-start.11 = (bf16[2048,128]{1,0:T(8,128)(2,1)S(1)}, bf16[2048,128]{1,0:T(8,128)(2,1)S(1)}, u32[]{:S(2)}, u32[]{:S(2)}) collective-permute-start(bf16[2048,128]{1,0:T(8,128)(2,1)S(1)} %copy-done.1), channel_id=1, source_target_pairs={{0,1},{1,0},{2,3},{3,2},{4,5},{5,4},{6,7},{7,6},{8,9},{9,8},{10,11... | collective-permute-start | bytes 1572872 | tf_op jit(solution)/shard_map/ppermute | solution.py:218
  10.5 0.7 copy-start.7
  11.7 12.6 %collective-permute-start.2 = (bf16[2,528,128]{2,1,0:T(8,128)(2,1)S(1)}, bf16[2,528,128]{2,1,0:T(8,128)(2,1)S(1)}, u32[]{:S(2)}, u32[]{:S(2)}) collective-permute-start(bf16[2,528,128]{2,1,0:T(8,128)(2,1)S(1)} %pad_maximum_fusion.refs_0_), channel_id=1, source_target_pairs={{0,6},{1,7},{2,0},{3,1},{4,2},{5,3},{6,4},{7,5},{8,14},{9,15},{10,... | collective-permute-start | bytes 811016 | tf_op jit(solution)/shard_map/ppermute | solution.py:218
  14.2 12.9 %collective-permute-start.1 = (bf16[2,528,128]{2,1,0:T(8,128)(2,1)S(1)}, bf16[2,528,128]{2,1,0:T(8,128)(2,1)S(1)}, u32[]{:S(2)}, u32[]{:S(2)}) collective-permute-start(bf16[2,528,128]{2,1,0:T(8,128)(2,1)S(1)} %pad_maximum_fusion.refs_0_), channel_id=1, source_target_pairs={{0,2},{1,3},{2,4},{3,5},{4,6},{5,7},{6,0},{7,1},{8,10},{9,11},{10,... | collective-permute-start | bytes 811016 | tf_op jit(solution)/shard_map/ppermute | solution.py:218
  18.2 10.8 %collective-permute-start.8 = (bf16[2,528,128]{2,1,0:T(8,128)(2,1)S(1)}, bf16[2,528,128]{2,1,0:T(8,128)(2,1)S(1)}, u32[]{:S(2)}, u32[]{:S(2)}) collective-permute-start(bf16[2,528,128]{2,1,0:T(8,128)(2,1)S(1)} %pad_maximum_fusion.1.refs_5_), channel_id=1, source_target_pairs={{0,6},{1,7},{2,0},{3,1},{4,2},{5,3},{6,4},{7,5},{8,14},{9,15},{10,... | collective-permute-start | bytes 811016 | tf_op jit(solution)/shard_map/ppermute | solution.py:218
  24.3 8.2 %collective-permute-start.7 = (bf16[2,528,128]{2,1,0:T(8,128)(2,1)S(1)}, bf16[2,528,128]{2,1,0:T(8,128)(2,1)S(1)}, u32[]{:S(2)}, u32[]{:S(2)}) collective-permute-start(bf16[2,528,128]{2,1,0:T(8,128)(2,1)S(1)} %pad_maximum_fusion.1.refs_5_), channel_id=1, source_target_pairs={{0,2},{1,3},{2,4},{3,5},{4,6},{5,7},{6,0},{7,1},{8,10},{9,11},{10,... | collective-permute-start | bytes 811016 | tf_op jit(solution)/shard_map/ppermute | solution.py:218
  24.3 8.7 %collective-permute-start.4 = (bf16[528,128]{1,0:T(8,128)(2,1)S(1)}, bf16[528,128]{1,0:T(8,128)(2,1)S(1)}, u32[]{:S(2)}, u32[]{:S(2)}) collective-permute-start(bf16[528,128]{1,0:T(8,128)(2,1)S(1)} %slice_bitcast_fusion.2), channel_id=1, source_target_pairs={{0,6},{1,7},{2,0},{3,1},{4,2},{5,3},{6,4},{7,5},{8,14},{9,15},{10,... | collective-permute-start | bytes 405512 | tf_op jit(solution)/shard_map/ppermute | solution.py:218
  27.1 7.9 %collective-permute-start.3 = (bf16[528,128]{1,0:T(8,128)(2,1)S(1)}, bf16[528,128]{1,0:T(8,128)(2,1)S(1)}, u32[]{:S(2)}, u32[]{:S(2)}) collective-permute-start(bf16[528,128]{1,0:T(8,128)(2,1)S(1)} %slice_bitcast_fusion.3), channel_id=1, source_target_pairs={{0,2},{1,3},{2,4},{3,5},{4,6},{5,7},{6,0},{7,1},{8,10},{9,11},{10,... | collective-permute-start | bytes 405512 | tf_op jit(solution)/shard_map/ppermute | solution.py:218
  29.0 3.6 %copy-start.8 = (bf16[24,128]{1,0:T(8,128)(2,1)S(1)}, bf16[24,128]{1,0:T(8,128)(2,1)}, u32[]{:S(2)}) copy-start(bf16[24,128]{1,0:T(8,128)(2,1)} %param.16) | copy-start | bytes 18436
  29.0 6.0 %collective-permute-start.10 = (bf16[528,128]{1,0:T(8,128)(2,1)S(1)}, bf16[528,128]{1,0:T(8,128)(2,1)S(1)}, u32[]{:S(2)}, u32[]{:S(2)}) collective-permute-start(bf16[528,128]{1,0:T(8,128)(2,1)S(1)} %slice_bitcast_fusion), channel_id=1, source_target_pairs={{0,6},{1,7},{2,0},{3,1},{4,2},{5,3},{6,4},{7,5},{8,14},{9,15},{10,... | collective-permute-start | bytes 405512 | tf_op jit(solution)/shard_map/ppermute | solution.py:218
  32.5 5.6 %collective-permute-start.9 = (bf16[528,128]{1,0:T(8,128)(2,1)S(1)}, bf16[528,128]{1,0:T(8,128)(2,1)S(1)}, u32[]{:S(2)}, u32[]{:S(2)}) collective-permute-start(bf16[528,128]{1,0:T(8,128)(2,1)S(1)} %slice_bitcast_fusion.1), channel_id=1, source_target_pairs={{0,2},{1,3},{2,4},{3,5},{4,6},{5,7},{6,0},{7,1},{8,10},{9,11},{10,... | collective-permute-start | bytes 405512 | tf_op jit(solution)/shard_map/ppermute | solution.py:218
  39.6 23.8 %copy-start.3 = (bf16[2,256,256]{2,1,0:T(8,128)(2,1)S(1)}, bf16[2,256,256]{2,1,0:T(8,128)(2,1)}, u32[]{:S(2)}) copy-start(bf16[2,256,256]{2,1,0:T(8,128)(2,1)} %constant.67.clone.second_ref) | copy-start | bytes 786436
  39.6 23.8 %copy-start.4 = (bf16[2,256,256]{2,1,0:T(8,128)(2,1)S(1)}, bf16[2,256,256]{2,1,0:T(8,128)(2,1)}, u32[]{:S(2)}) copy-start(bf16[2,256,256]{2,1,0:T(8,128)(2,1)} %constant.65.clone.first_ref) | copy-start | bytes 786436
  39.6 23.8 %copy-start.5 = (bf16[2,128,256]{2,1,0:T(8,128)(2,1)S(1)}, bf16[2,128,256]{2,1,0:T(8,128)(2,1)}, u32[]{:S(2)}) copy-start(bf16[2,128,256]{2,1,0:T(8,128)(2,1)} %constant.69.clone.last_ref) | copy-start | bytes 393220
  39.6 23.8 %copy-start.6 = (f32[2,128,128]{2,1,0:T(8,128)S(1)}, f32[2,128,128]{2,1,0:T(8,128)}, u32[]{:S(2)}) copy-start(f32[2,128,128]{2,1,0:T(8,128)} %constant.66.clone.turn_ref) | copy-start | bytes 393220
  56.4 7.0 %copy-start.2 = (bf16[2,256,256]{2,1,0:T(8,128)(2,1)S(1)}, bf16[2,256,256]{2,1,0:T(8,128)(2,1)}, u32[]{:S(2)}) copy-start(bf16[2,256,256]{2,1,0:T(8,128)(2,1)} %constant.68.clone.back_ref) | copy-start | bytes 786436
  56.5 7.0 %collective-permute-start.12 = (bf16[16,32,128]{2,1,0:T(8,128)(2,1)S(1)}, bf16[16,32,128]{2,1,0:T(8,128)(2,1)S(1)}, u32[]{:S(2)}, u32[]{:S(2)}) collective-permute-start(bf16[16,32,128]{2,1,0:T(8,128)(2,1)S(1)} %slice.24), channel_id=1, source_target_pairs={{0,1},{1,0},{2,3},{3,2},{4,5},{5,4},{6,7},{7,6},{8,9},{9,8},{10,11... | collective-permute-start | bytes 393224 | tf_op jit(solution)/shard_map/ppermute | solution.py:218

commit v3 on v2

--- a/solution.py
+++ b/solution.py
@@ -1,4 +1,3 @@
-import functools
 import math
 
 import jax
@@ -61,18 +60,24 @@
 
 def mm3_right(value, table):
     high, low = high_low(value)
-    return mm(high, table[0]) + mm(low, table[0]) + mm(high, table[1])
+    return mm(
+        jnp.concatenate([high, low, high], axis=1),
+        jnp.concatenate([table[0], table[0], table[1]], axis=0),
+    )
 
 
 def mm3_left(table, value):
     high, low = high_low(value)
-    return mm(table[0], high) + mm(table[0], low) + mm(table[1], high)
-
-
-def spectrum_of_pair(pair, first, turn_real, turn_imag, second):
-    mixed = mm(first, jnp.concatenate([pair, pair], axis=0))
+    return mm(
+        jnp.concatenate([table[0], table[0], table[1]], axis=1),
+        jnp.concatenate([high, low, high], axis=0),
+    )
+
+
+def turned_blocks(values, first, turn_real, turn_imag):
+    mixed = mm(first, jnp.concatenate([values, values], axis=0))
     rows = []
-    for at in range(2):
+    for at in range(SHARE):
         real = mixed[:LANES, at * LANES : (at + 1) * LANES]
         imag = mixed[LANES:, at * LANES : (at + 1) * LANES]
         rows.append(
@@ -80,17 +85,14 @@
                 [real * turn_real - imag * turn_imag, real * turn_imag + imag * turn_real], axis=1
             )
         )
-    return mm3_right(jnp.concatenate(rows, axis=0), second)
-
-
-def load_pair(unpacked, at):
+    return jnp.concatenate(rows, axis=0)
+
+
+def load_all(unpacked, values):
+    unpacked[...] = values.astype(F32).reshape(CTX * BLOCKS * SHARE, LANES)
     return jnp.concatenate(
-        [unpacked[pl.ds(2 * at + k, LANES, stride=SHARE), :] for k in range(2)], axis=1
+        [unpacked[pl.ds(at, LANES, stride=SHARE), :] for at in range(SHARE)], axis=1
     ).astype(BF16)
-
-
-def unpack(ref, values):
-    ref[...] = values.astype(F32).reshape(CTX * BLOCKS * SHARE, LANES)
 
 
 def mix_kernel(
@@ -98,55 +100,45 @@
     out_ref, signals, responses, gathered,
 ):
     full = BLOCKS * SHARE
-    half = full // 2
-    unpack(signals, jnp.concatenate([own_ref[:, :half, :], other_ref[...]], axis=1))
-    unpack(responses, own_ref[:, full:, :])
     turn_real, turn_imag = turn_ref[0], turn_ref[1]
-    first_here = first_ref[place_ref[2]]
     first = first_ref[0]
-    for at in range(SHARE // 2):
-        signal = spectrum_of_pair(
-            load_pair(signals, at), first_here, turn_real, turn_imag, second_ref
-        )
-        response = spectrum_of_pair(
-            load_pair(responses, at), first, turn_real, turn_imag, second_ref
-        )
-        sig_real, sig_imag = signal[:, :LANES], signal[:, LANES:]
-        res_real, res_imag = response[:, :LANES], response[:, LANES:]
-        product = jnp.concatenate(
-            [sig_real * res_real - sig_imag * res_imag, sig_real * res_imag + sig_imag * res_real],
-            axis=1,
-        )
-        back = mm3_right(product, back_ref)
-        reals, imags = [], []
-        for k in range(2):
-            real = back[k * LANES : (k + 1) * LANES, :LANES]
-            imag = back[k * LANES : (k + 1) * LANES, LANES:]
-            reals.append(real * turn_real + imag * turn_imag)
-            imags.append(imag * turn_real - real * turn_imag)
-        turned = jnp.concatenate(
-            [jnp.concatenate(reals, axis=1), jnp.concatenate(imags, axis=1)], axis=0
-        )
-        result = mm3_left(last_ref, turned)
-        for k in range(2):
-            gathered[pl.ds(2 * at + k, LANES, stride=SHARE), :] = result[
-                :, k * LANES : (k + 1) * LANES
-            ]
-    out_ref[...] = gathered[...].reshape(CTX, full, LANES).astype(BF16)
-
-
-def project_kernel(pieces, place_ref, *refs):
+    signal = load_all(
+        signals, jnp.concatenate([own_ref[:, : full // 2, :], other_ref[...]], axis=1)
+    )
+    response = load_all(responses, own_ref[:, full:, :])
+    signal = turned_blocks(signal, first_ref[place_ref[2]], turn_real, turn_imag)
+    signal = mm3_right(signal, second_ref)
+    response = mm3_right(turned_blocks(response, first, turn_real, turn_imag), second_ref)
+    sig_real, sig_imag = signal[:, :LANES], signal[:, LANES:]
+    res_real, res_imag = response[:, :LANES], response[:, LANES:]
+    product = jnp.concatenate(
+        [sig_real * res_real - sig_imag * res_imag, sig_real * res_imag + sig_imag * res_real],
+        axis=1,
+    )
+    back = mm3_right(product, back_ref)
+    reals, imags = [], []
+    for at in range(SHARE):
+        real = back[at * LANES : (at + 1) * LANES, :LANES]
+        imag = back[at * LANES : (at + 1) * LANES, LANES:]
+        reals.append(real * turn_real + imag * turn_imag)
+        imags.append(imag * turn_real - real * turn_imag)
+    turned = jnp.concatenate(
+        [jnp.concatenate(reals, axis=1), jnp.concatenate(imags, axis=1)], axis=0
+    )
+    result = mm3_left(last_ref, turned)
+    for at in range(SHARE):
+        gathered[pl.ds(at, LANES, stride=SHARE), :] = result[:, at * LANES : (at + 1) * LANES]
+    out_ref[...] = gathered[...].reshape(CTX, BLOCKS * SHARE, LANES).astype(BF16)
+
+
+def add_products(d_high, place_ref, piece_refs, w_own_ref, w_other_ref, total, squares):
     high, along, core = place_ref[0], place_ref[1], place_ref[2]
-    *piece_refs, w_own_ref, w_other_ref, response_ref, out_ref = refs
-    count = HALF // LANES
-    total = jnp.zeros((HALF, 2 * LANES), F32)
-    squares = jnp.zeros((HALF, LANES), F32)
-    for d_high, d_along, *slots in pieces:
+    whole_refs, mid_refs = piece_refs[:3], piece_refs[3:]
+    for d_along, ref in (*zip((0, YS - 1, 1), whole_refs), (2, None)):
         chip = lax.rem(high + d_high, HI) * YS + lax.rem(along + d_along, YS)
         scaled, weights = [], []
-        for slot, (at, lead) in enumerate(slots):
-            ref = piece_refs[at]
-            block = ref[...] if lead is None else ref[lead]
+        for slot in range(CORES):
+            block = mid_refs[slot][...] if ref is None else ref[slot]
             values = block[:HALF].astype(F32)
             squares = squares + values * values
             scaled.append((values * block[HALF:].astype(F32)[:1]).astype(BF16))
@@ -159,6 +151,28 @@
                 )
             )
         total = total + mm(jnp.concatenate(scaled, axis=1), jnp.concatenate(weights, axis=0))
+    return total, squares
+
+
+def near_kernel(place_ref, *refs):
+    *piece_refs, w_own_ref, w_other_ref, total_ref, squares_ref = refs
+    total_ref[...], squares_ref[...] = add_products(
+        0,
+        place_ref,
+        piece_refs,
+        w_own_ref,
+        w_other_ref,
+        jnp.zeros((HALF, 2 * LANES), F32),
+        jnp.zeros((HALF, LANES), F32),
+    )
+
+
+def project_kernel(place_ref, *refs):
+    *piece_refs, w_own_ref, w_other_ref, response_ref, total_ref, squares_ref, out_ref = refs
+    count = HALF // LANES
+    total, squares = add_products(
+        1, place_ref, piece_refs, w_own_ref, w_other_ref, total_ref[...], squares_ref[...]
+    )
     power = jnp.sum(squares, axis=1, keepdims=True) * (1.0 / FEATURES)
     total = total * lax.rsqrt(power + EPS)
     for slot in range(CORES):
@@ -218,79 +232,20 @@
     return lax.ppermute(value, "tp", pairs)
 
 
-AG = "G6"
-
-
 def gather(mine, theirs):
-    def left(x, swap=0):
-        return tp_shift(x, 0, 1, swap)
-
-    def right(x, swap=0):
-        return tp_shift(x, 0, YS - 1, swap)
-
-    arrived = tp_shift(theirs, 0, 0, 1)
-    out, pieces = [], []
-
-    def add(d_high, d_along, *slots):
-        entry = [d_high, d_along]
-        for value, lead in slots:
-            for at, known in enumerate(out):
-                if known is value:
-                    break
-            else:
-                at = len(out)
-                out.append(value)
-            entry.append((at, lead))
-        pieces.append(tuple(entry))
-
-    def add_whole(d_high, d_along, value):
-        add(d_high, d_along, (value, 0), (value, 1))
-
-    def ring_whole(d_high, value):
-        l, r = left(value), right(value)
-        ma, mb = left(l[0]), right(r[1])
-        add_whole(d_high, 0, value)
-        add_whole(d_high, YS - 1, l)
-        add_whole(d_high, 1, r)
-        add(d_high, 2, (ma, None), (mb, None))
-
-    def ring_slots(d_high, a, b, src=None, swap=0):
-        src = b if src is None else src
-        la, rb = left(a), right(src, swap)
-        ra, lb = right(a), left(src, swap)
-        ma, mb = left(la), right(rb)
-        add(d_high, 0, (a, None), (b, None))
-        add(d_high, YS - 1, (la, None), (lb, None))
-        add(d_high, 1, (ra, None), (rb, None))
-        add(d_high, 2, (ma, None), (mb, None))
-
-    own = jnp.stack([mine, arrived])
-    if AG == "G1":
-        far = tp_shift(own, 1, 0, 0)
-        ring_whole(0, own)
-        ring_whole(1, far)
-    elif AG == "G2":
-        za, zb = tp_shift(mine, 1, 0, 0), tp_shift(arrived, 1, 0, 0)
-        ring_whole(0, own)
-        ring_slots(1, za, zb)
-    elif AG == "G3":
-        za, zb = tp_shift(mine, 1, 0, 0), tp_shift(arrived, 1, 0, 0)
-        ring_slots(0, mine, arrived)
-        ring_slots(1, za, zb)
-    elif AG == "G4":
-        za, zb = tp_shift(mine, 1, 0, 0), tp_shift(theirs, 1, 0, 1)
-        ring_slots(0, mine, arrived, theirs, 1)
-        ring_slots(1, za, zb)
-    elif AG == "G5":
-        za, zb = tp_shift(mine, 1, 0, 0), tp_shift(theirs, 1, 0, 1)
-        ring_whole(0, own)
-        ring_slots(1, za, zb)
-    elif AG == "G6":
-        za, zb = tp_shift(mine, 1, 0, 0), tp_shift(theirs, 1, 0, 1)
-        far = jnp.stack([za, zb])
-        ring_whole(0, own)
-        ring_whole(1, far)
-    return out, tuple(pieces)
+    def left(value):
+        return tp_shift(value, 0, 1, 0)
+
+    def right(value):
+        return tp_shift(value, 0, YS - 1, 0)
+
+    def ring(value):
+        from_left, from_right = left(value), right(value)
+        return [value, from_left, from_right, left(from_left[0]), right(from_right[1])]
+
+    across = [tp_shift(mine, 1, 0, 0), tp_shift(theirs, 1, 0, 1)]
+    own = jnp.stack([mine, tp_shift(theirs, 0, 0, 1)])
+    return ring(own), ring(jnp.stack(across))
 
 
 def on_device(tokens, gain, w_inputs, filters, w_plus, w_minus):
@@ -308,7 +263,7 @@
         )
         for half in (core, 1 - core)
     )
-    gathered, pieces = gather(mine, theirs)
+    near, far = gather(mine, theirs)
     w_other = tp_shift(w_inputs, 0, 0, 1)
 
     lag_sign = 1.0 - 2.0 * (lax.iota(jnp.int32, ROWS) % 2).astype(F32)
@@ -323,12 +278,23 @@
         .reshape(CTX, BLOCKS * SHARE, LANES)
     )
 
+    flops = HALF * 2 * LANES * FEATURES
+    total, squares = call(
+        near_kernel,
+        (
+            jax.ShapeDtypeStruct((HALF, 2 * LANES), F32),
+            jax.ShapeDtypeStruct((HALF, LANES), F32),
+        ),
+        [place, *near, w_inputs, w_other],
+        first_spec=SMEM,
+        flops=flops,
+    )
     blocks = call(
-        functools.partial(project_kernel, pieces),
+        project_kernel,
         bf16(CTX, 2 * BLOCKS * SHARE, LANES),
-        [place, *gathered, w_inputs, w_other, response],
+        [place, *far, w_inputs, w_other, response, total, squares],
         first_spec=SMEM,
-        flops=2 * HALF * 2 * LANES * FEATURES,
+        flops=flops,
     )
     blocks = lax.all_to_all(blocks, "ctx", split_axis=0, concat_axis=0, tiled=True)
     other = tp_shift(blocks[:, BLOCKS * SHARE // 2 : BLOCKS * SHARE, :], 0, 0, 1)

time: 81.1 us -> 79 us (0.974)
  the two profiles are of different devices: /device:TPU:1 before, /device:TPU:8 now
where the time goes in v3:
time: 79 us; the launch traced here: 78.8 us
  blocking collectives  33.4 us (42%)
  waiting for transfers between devices  18.7 us (24%)
  starting transfers between devices  16.7 us (21%)
  Pallas kernels  6.25 us (8%)
  local copies, waits for them, and re-layouts  2.49 us (3%)
  matrix products  0.83 us (1%)
    all_to_all x1, blocking collectives, on_device(): lax.all_to_all(blocks, 'ctx', split_axis=0, concat_axis=0, tiled=True)  19.2 us
    ppermute x13, waiting for transfers between devices, tp_shift(): return lax.ppermute(value, 'tp', pairs)  18.7 us
    ppermute x13, starting transfers between devices, tp_shift(): return lax.ppermute(value, 'tp', pairs)  16.7 us
    all_to_all x1, blocking collectives, on_device(): lax.all_to_all(mixed, 'ctx', split_axis=0, concat_axis=0, tiled=True)  14.2 us
    pallas_call x4, Pallas kernels, call(): pl.pallas_call(kernel, out_shape=outs, in_specs=[first_spec] + [VMEM] * (...  6.25 us
  transfers between devices with their start and end apart: 13, of which 6 were waited for; matrix products, arithmetic and copies ran while one was open for 1% of the time, Pallas kernels for 1%

profile of v3, /device:TPU:8, one launch (start us, length us, event | category | flops | bytes accessed | tf_op | source)
XLA Modules:
  0.0 78.8 jit_solution(1446703518407632349)
XLA Ops:
  0.0 1.0 %constant_dynamic-slice_fusion.1 = (bf16[512,128]{1,0:T(8,128)(2,1)S(1)}, bf16[512,128]{1,0:T(8,128)(2,1)S(1)}) fusion(bf16[1024,128]{1,0:T(8,128)(2,1)} %param.11, s32[]{:T(128)S(6)} %select_n.26, s32[]{:T(128)S(6)} %select_n.27), kind=kLoop, calls=%fused_computation.22 | loop fusion | bytes 524296 | tf_op jit(solution)/shard_map/dynamic_slice | solution.py:262
  1.1 0.6 copy-done.9
  1.9 7.3 %collective-permute-start.1 = (bf16[528,128]{1,0:T(8,128)(2,1)S(1)}, bf16[528,128]{1,0:T(8,128)(2,1)S(1)}, u32[]{:S(2)}, u32[]{:S(2)}) collective-permute-start(bf16[528,128]{1,0:T(8,128)(2,1)S(1)} %get-tuple-element.13), channel_id=1, source_target_pairs={{0,9},{1,8},{2,11},{3,10},{4,13},{5,12},{6,15},{7,14},{8,1},{9,0},... | collective-permute-start | bytes 405512 | tf_op jit(solution)/shard_map/ppermute | solution.py:232
  10.0 1.7 %collective-permute-start.8 = (bf16[2,528,128]{2,1,0:T(8,128)(2,1)S(1)}, bf16[2,528,128]{2,1,0:T(8,128)(2,1)S(1)}, u32[]{:S(2)}, u32[]{:S(2)}) collective-permute-start(bf16[2,528,128]{2,1,0:T(8,128)(2,1)S(1)} %pad_maximum_fusion.1.refs_0_), channel_id=1, source_target_pairs={{0,2},{1,3},{2,4},{3,5},{4,6},{5,7},{6,0},{7,1},{8,10},{9,11},{10,... | collective-permute-start | bytes 811016 | tf_op jit(solution)/shard_map/ppermute | solution.py:232
  11.7 0.7 copy-done.8
  12.4 0.4 fusion.2.refs_7_
  12.8 0.5 collective-permute-start.9
  13.3 8.8 %collective-permute-done = bf16[528,128]{1,0:T(8,128)(2,1)S(1)} collective-permute-done((bf16[528,128]{1,0:T(8,128)(2,1)S(1)}, bf16[528,128]{1,0:T(8,128)(2,1)S(1)}, u32[]{:S(2)}, u32[]{:S(2)}) %collective-permute-start) | collective-permute-done | bytes 135200 | tf_op jit(solution)/shard_map/ppermute | solution.py:232
  22.1 1.7 %collective-permute-start.2 = (bf16[2,528,128]{2,1,0:T(8,128)(2,1)S(1)}, bf16[2,528,128]{2,1,0:T(8,128)(2,1)S(1)}, u32[]{:S(2)}, u32[]{:S(2)}) collective-permute-start(bf16[2,528,128]{2,1,0:T(8,128)(2,1)S(1)} %pad_maximum_fusion.refs_0_), channel_id=1, source_target_pairs={{0,2},{1,3},{2,4},{3,5},{4,6},{5,7},{6,0},{7,1},{8,10},{9,11},{10,... | collective-permute-start | bytes 811016 | tf_op jit(solution)/shard_map/ppermute | solution.py:232
  23.8 0.4 collective-permute-start.3
  24.3 1.7 %collective-permute-start.10 = (bf16[528,128]{1,0:T(8,128)(2,1)S(1)}, bf16[528,128]{1,0:T(8,128)(2,1)S(1)}, u32[]{:S(2)}, u32[]{:S(2)}) collective-permute-start(bf16[528,128]{1,0:T(8,128)(2,1)S(1)} %slice_bitcast_fusion.1), channel_id=1, source_target_pairs={{0,2},{1,3},{2,4},{3,5},{4,6},{5,7},{6,0},{7,1},{8,10},{9,11},{10,... | collective-permute-start | bytes 405512 | tf_op jit(solution)/shard_map/ppermute | solution.py:232
  25.9 0.5 collective-permute-start.11
  26.5 5.2 %collective-permute-done.2.refs_1_ = bf16[2,528,128]{2,1,0:T(8,128)(2,1)S(1)} collective-permute-done((bf16[2,528,128]{2,1,0:T(8,128)(2,1)S(1)}, bf16[2,528,128]{2,1,0:T(8,128)(2,1)S(1)}, u32[]{:S(2)}, u32[]{:S(2)}) %collective-permute-start.2) | collective-permute-done | bytes 270368 | tf_op jit(solution)/shard_map/ppermute | solution.py:232
  31.6 1.7 %collective-permute-start.4 = (bf16[528,128]{1,0:T(8,128)(2,1)S(1)}, bf16[528,128]{1,0:T(8,128)(2,1)S(1)}, u32[]{:S(2)}, u32[]{:S(2)}) collective-permute-start(bf16[528,128]{1,0:T(8,128)(2,1)S(1)} %slice_bitcast_fusion.3), channel_id=1, source_target_pairs={{0,2},{1,3},{2,4},{3,5},{4,6},{5,7},{6,0},{7,1},{8,10},{9,11},{10,... | collective-permute-start | bytes 405512 | tf_op jit(solution)/shard_map/ppermute | solution.py:232
  33.3 0.5 collective-permute-start.5
  34.3 1.5 %collective-permute-done.11.refs_4_ = bf16[528,128]{1,0:T(8,128)(2,1)S(1)} collective-permute-done((bf16[528,128]{1,0:T(8,128)(2,1)S(1)}, bf16[528,128]{1,0:T(8,128)(2,1)S(1)}, u32[]{:S(2)}, u32[]{:S(2)}) %collective-permute-start.11) | collective-permute-done | bytes 135200 | tf_op jit(solution)/shard_map/ppermute | solution.py:232
  35.8 1.0 %shard_map.109 = (f32[512,256]{1,0:T(8,128)S(1)}, f32[512,128]{1,0:T(8,128)S(1)}) custom-call(s32[4]{0:T(128)S(1)} %pad_add_fusion.place_ref, bf16[2,528,128]{2,1,0:T(8,128)(2,1)S(1)} %pad_maximum_fusion.1.refs_0_, bf16[2,528,128]{2,1,0:T(8,128)(2,1)S(1)} %collective-permute-done.8.refs_1_, bf16[2,528,128]{2,1,0:T(8,128)(2,1)S(1)} %collective-permute-done.9.refs_2_, ...), custom_call_target="tpu_custom_call" | custom-call | flops 268435456 | bytes 2129936 | tf_op jit(solution)/shard_map/pallas_call | solution.py:207
  36.8 1.6 %collective-permute-done.5.refs_4_ = bf16[528,128]{1,0:T(8,128)(2,1)S(1)} collective-permute-done((bf16[528,128]{1,0:T(8,128)(2,1)S(1)}, bf16[528,128]{1,0:T(8,128)(2,1)S(1)}, u32[]{:S(2)}, u32[]{:S(2)}) %collective-permute-start.5) | collective-permute-done | bytes 135200 | tf_op jit(solution)/shard_map/ppermute | solution.py:232
  38.4 1.2 %shard_map.110 = bf16[16,128,128]{2,1,0:T(8,128)(2,1)S(1)} custom-call(s32[4]{0:T(128)S(1)} %pad_add_fusion.place_ref, bf16[2,528,128]{2,1,0:T(8,128)(2,1)S(1)} %pad_maximum_fusion.refs_0_, bf16[2,528,128]{2,1,0:T(8,128)(2,1)S(1)} %collective-permute-done.2.refs_1_, bf16[2,528,128]{2,1,0:T(8,128)(2,1)S(1)} %collective-permute-done.3.refs_2_, ...), custom_call_target="tpu_custom_call" | custom-call | flops 268435456 | bytes 3178512 | tf_op jit(solution)/shard_map/pallas_call | solution.py:207
  39.6 19.2 %all_to_all.10.own_ref = bf16[16,128,128]{2,1,0:T(8,128)(2,1)S(1)} all-to-all(bf16[16,128,128]{2,1,0:T(8,128)(2,1)S(1)} %shard_map.110), channel_id=1, replica_groups=mesh['ctx'=16,'tp'=16] {'ctx'}, dimensions={0} | all-to-all | bytes 1048576 | tf_op jit(solution)/shard_map/all_to_all | solution.py:299
  59.2 1.3 %collective-permute-done.12.other_ref = bf16[16,32,128]{2,1,0:T(8,128)(2,1)S(1)} collective-permute-done((bf16[16,32,128]{2,1,0:T(8,128)(2,1)S(1)}, bf16[16,32,128]{2,1,0:T(8,128)(2,1)S(1)}, u32[]{:S(2)}, u32[]{:S(2)}) %collective-permute-start.12) | collective-permute-done | bytes 131104 | tf_op jit(solution)/shard_map/ppermute | solution.py:232
  60.5 3.2 %shard_map.111 = bf16[16,64,128]{2,1,0:T(8,128)(2,1)S(1)} custom-call(s32[4]{0:T(128)S(1)} %pad_add_fusion.place_ref, bf16[16,128,128]{2,1,0:T(8,128)(2,1)S(1)} %all_to_all.10.own_ref, bf16[16,32,128]{2,1,0:T(8,128)(2,1)S(1)} %collective-permute-done.12.other_ref, bf16[2,256,256]{2,1,0:T(8,128)(2,1)S(1)} %copy-done.2, f32[2,128,128]{2,1,0:T(8,128)S(1)} %copy-done.5, ...), custom_call_target="tpu_custom_call" | custom-call | flops 3000000000 | bytes 1703952 | tf_op jit(solution)/shard_map/pallas_call | solution.py:207
  63.8 14.2 %all_to_all.11.blocks_ref = bf16[16,64,128]{2,1,0:T(8,128)(2,1)S(1)} all-to-all(bf16[16,64,128]{2,1,0:T(8,128)(2,1)S(1)} %shard_map.111), channel_id=1, replica_groups=mesh['ctx'=16,'tp'=16] {'ctx'}, dimensions={0} | all-to-all | bytes 524288 | tf_op jit(solution)/shard_map/all_to_all | solution.py:311
  77.9 0.8 %shard_map.112 = bf16[1024,128]{1,0:T(8,128)(2,1)} custom-call(bf16[16,64,128]{2,1,0:T(8,128)(2,1)S(1)} %all_to_all.11.blocks_ref), custom_call_target="tpu_custom_call" | custom-call | bytes 262144 | tf_op jit(solution)/shard_map/pallas_call | solution.py:207
  (42 shorter events, 1.8 us)
Async XLA Ops:
  0.0 9.6 %copy-start = (f32[24,1024]{1,0:T(8,128)S(1)}, f32[24,1024]{1,0:T(8,128)}, u32[]{:S(2)}) copy-start(f32[24,1024]{1,0:T(8,128)} %param.14) | copy-start | bytes 294916
  0.0 9.2 %copy-start.1 = (bf16[2048,128]{1,0:T(8,128)(2,1)S(1)}, bf16[2048,128]{1,0:T(8,128)(2,1)}, u32[]{:S(2)}) copy-start(bf16[2048,128]{1,0:T(8,128)(2,1)} %refs_5_.3) | copy-start | bytes 1572868
  1.1 0.7 copy-start.9
  1.7 7.8 %copy-start.7 = (bf16[24,128]{1,0:T(8,128)(2,1)S(1)}, bf16[24,128]{1,0:T(8,128)(2,1)}, u32[]{:S(2)}) copy-start(bf16[24,128]{1,0:T(8,128)(2,1)} %param.15) | copy-start | bytes 18436
  1.8 8.2 %collective-permute-start.7 = (bf16[528,128]{1,0:T(8,128)(2,1)S(1)}, bf16[528,128]{1,0:T(8,128)(2,1)S(1)}, u32[]{:S(2)}, u32[]{:S(2)}) collective-permute-start(bf16[528,128]{1,0:T(8,128)(2,1)S(1)} %get-tuple-element.13), channel_id=1, source_target_pairs={{0,1},{1,0},{2,3},{3,2},{4,5},{5,4},{6,7},{7,6},{8,9},{9,8},{10,11... | collective-permute-start | bytes 405512 | tf_op jit(solution)/shard_map/ppermute | solution.py:232
  1.9 20.2 %collective-permute-start.1 = (bf16[528,128]{1,0:T(8,128)(2,1)S(1)}, bf16[528,128]{1,0:T(8,128)(2,1)S(1)}, u32[]{:S(2)}, u32[]{:S(2)}) collective-permute-start(bf16[528,128]{1,0:T(8,128)(2,1)S(1)} %get-tuple-element.13), channel_id=1, source_target_pairs={{0,9},{1,8},{2,11},{3,10},{4,13},{5,12},{6,15},{7,14},{8,1},{9,0},... | collective-permute-start | bytes 405512 | tf_op jit(solution)/shard_map/ppermute | solution.py:232
  9.2 24.7 %collective-permute-start.6 = (bf16[2048,128]{1,0:T(8,128)(2,1)S(1)}, bf16[2048,128]{1,0:T(8,128)(2,1)S(1)}, u32[]{:S(2)}, u32[]{:S(2)}) collective-permute-start(bf16[2048,128]{1,0:T(8,128)(2,1)S(1)} %copy-done.1), channel_id=1, source_target_pairs={{0,1},{1,0},{2,3},{3,2},{4,5},{5,4},{6,7},{7,6},{8,9},{9,8},{10,11... | collective-permute-start | bytes 1572872 | tf_op jit(solution)/shard_map/ppermute | solution.py:232
  9.3 12.8 %collective-permute-start = (bf16[528,128]{1,0:T(8,128)(2,1)S(1)}, bf16[528,128]{1,0:T(8,128)(2,1)S(1)}, u32[]{:S(2)}, u32[]{:S(2)}) collective-permute-start(bf16[528,128]{1,0:T(8,128)(2,1)S(1)} %get-tuple-element.12), channel_id=1, source_target_pairs={{0,8},{1,9},{2,10},{3,11},{4,12},{5,13},{6,14},{7,15},{8,0},{9,1},... | collective-permute-start | bytes 405512 | tf_op jit(solution)/shard_map/ppermute | solution.py:232
  10.0 14.2 %collective-permute-start.8 = (bf16[2,528,128]{2,1,0:T(8,128)(2,1)S(1)}, bf16[2,528,128]{2,1,0:T(8,128)(2,1)S(1)}, u32[]{:S(2)}, u32[]{:S(2)}) collective-permute-start(bf16[2,528,128]{2,1,0:T(8,128)(2,1)S(1)} %pad_maximum_fusion.1.refs_0_), channel_id=1, source_target_pairs={{0,2},{1,3},{2,4},{3,5},{4,6},{5,7},{6,0},{7,1},{8,10},{9,11},{10,... | collective-permute-start | bytes 811016 | tf_op jit(solution)/shard_map/ppermute | solution.py:232
  11.7 0.7 copy-start.8
  12.8 13.1 %collective-permute-start.9 = (bf16[2,528,128]{2,1,0:T(8,128)(2,1)S(1)}, bf16[2,528,128]{2,1,0:T(8,128)(2,1)S(1)}, u32[]{:S(2)}, u32[]{:S(2)}) collective-permute-start(bf16[2,528,128]{2,1,0:T(8,128)(2,1)S(1)} %pad_maximum_fusion.1.refs_0_), channel_id=1, source_target_pairs={{0,6},{1,7},{2,0},{3,1},{4,2},{5,3},{6,4},{7,5},{8,14},{9,15},{10,... | collective-permute-start | bytes 811016 | tf_op jit(solution)/shard_map/ppermute | solution.py:232
  22.1 9.5 %collective-permute-start.2 = (bf16[2,528,128]{2,1,0:T(8,128)(2,1)S(1)}, bf16[2,528,128]{2,1,0:T(8,128)(2,1)S(1)}, u32[]{:S(2)}, u32[]{:S(2)}) collective-permute-start(bf16[2,528,128]{2,1,0:T(8,128)(2,1)S(1)} %pad_maximum_fusion.refs_0_), channel_id=1, source_target_pairs={{0,2},{1,3},{2,4},{3,5},{4,6},{5,7},{6,0},{7,1},{8,10},{9,11},{10,... | collective-permute-start | bytes 811016 | tf_op jit(solution)/shard_map/ppermute | solution.py:232
  23.8 9.5 %collective-permute-start.3 = (bf16[2,528,128]{2,1,0:T(8,128)(2,1)S(1)}, bf16[2,528,128]{2,1,0:T(8,128)(2,1)S(1)}, u32[]{:S(2)}, u32[]{:S(2)}) collective-permute-start(bf16[2,528,128]{2,1,0:T(8,128)(2,1)S(1)} %pad_maximum_fusion.refs_0_), channel_id=1, source_target_pairs={{0,6},{1,7},{2,0},{3,1},{4,2},{5,3},{6,4},{7,5},{8,14},{9,15},{10,... | collective-permute-start | bytes 811016 | tf_op jit(solution)/shard_map/ppermute | solution.py:232
  24.3 10.0 %collective-permute-start.10 = (bf16[528,128]{1,0:T(8,128)(2,1)S(1)}, bf16[528,128]{1,0:T(8,128)(2,1)S(1)}, u32[]{:S(2)}, u32[]{:S(2)}) collective-permute-start(bf16[528,128]{1,0:T(8,128)(2,1)S(1)} %slice_bitcast_fusion.1), channel_id=1, source_target_pairs={{0,2},{1,3},{2,4},{3,5},{4,6},{5,7},{6,0},{7,1},{8,10},{9,11},{10,... | collective-permute-start | bytes 405512 | tf_op jit(solution)/shard_map/ppermute | solution.py:232
  25.9 9.8 %collective-permute-start.11 = (bf16[528,128]{1,0:T(8,128)(2,1)S(1)}, bf16[528,128]{1,0:T(8,128)(2,1)S(1)}, u32[]{:S(2)}, u32[]{:S(2)}) collective-permute-start(bf16[528,128]{1,0:T(8,128)(2,1)S(1)} %slice_bitcast_fusion), channel_id=1, source_target_pairs={{0,6},{1,7},{2,0},{3,1},{4,2},{5,3},{6,4},{7,5},{8,14},{9,15},{10,... | collective-permute-start | bytes 405512 | tf_op jit(solution)/shard_map/ppermute | solution.py:232
  31.6 5.1 %collective-permute-start.4 = (bf16[528,128]{1,0:T(8,128)(2,1)S(1)}, bf16[528,128]{1,0:T(8,128)(2,1)S(1)}, u32[]{:S(2)}, u32[]{:S(2)}) collective-permute-start(bf16[528,128]{1,0:T(8,128)(2,1)S(1)} %slice_bitcast_fusion.3), channel_id=1, source_target_pairs={{0,2},{1,3},{2,4},{3,5},{4,6},{5,7},{6,0},{7,1},{8,10},{9,11},{10,... | collective-permute-start | bytes 405512 | tf_op jit(solution)/shard_map/ppermute | solution.py:232
  33.3 5.1 %collective-permute-start.5 = (bf16[528,128]{1,0:T(8,128)(2,1)S(1)}, bf16[528,128]{1,0:T(8,128)(2,1)S(1)}, u32[]{:S(2)}, u32[]{:S(2)}) collective-permute-start(bf16[528,128]{1,0:T(8,128)(2,1)S(1)} %slice_bitcast_fusion.2), channel_id=1, source_target_pairs={{0,6},{1,7},{2,0},{3,1},{4,2},{5,3},{6,4},{7,5},{8,14},{9,15},{10,... | collective-permute-start | bytes 405512 | tf_op jit(solution)/shard_map/ppermute | solution.py:232
  39.6 20.9 %copy-start.3 = (bf16[2,256,256]{2,1,0:T(8,128)(2,1)S(1)}, bf16[2,256,256]{2,1,0:T(8,128)(2,1)}, u32[]{:S(2)}) copy-start(bf16[2,256,256]{2,1,0:T(8,128)(2,1)} %constant.67.clone.second_ref) | copy-start | bytes 786436
  39.6 20.9 %copy-start.4 = (bf16[2,256,256]{2,1,0:T(8,128)(2,1)S(1)}, bf16[2,256,256]{2,1,0:T(8,128)(2,1)}, u32[]{:S(2)}) copy-start(bf16[2,256,256]{2,1,0:T(8,128)(2,1)} %constant.68.clone.back_ref) | copy-start | bytes 786436
  39.6 20.9 %copy-start.5 = (f32[2,128,128]{2,1,0:T(8,128)S(1)}, f32[2,128,128]{2,1,0:T(8,128)}, u32[]{:S(2)}) copy-start(f32[2,128,128]{2,1,0:T(8,128)} %constant.66.clone.turn_ref) | copy-start | bytes 393220
  39.6 20.9 %copy-start.6 = (bf16[2,128,256]{2,1,0:T(8,128)(2,1)S(1)}, bf16[2,128,256]{2,1,0:T(8,128)(2,1)}, u32[]{:S(2)}) copy-start(bf16[2,128,256]{2,1,0:T(8,128)(2,1)} %constant.69.clone.last_ref) | copy-start | bytes 393220
  58.9 1.7 %copy-start.2 = (bf16[2,256,256]{2,1,0:T(8,128)(2,1)S(1)}, bf16[2,256,256]{2,1,0:T(8,128)(2,1)}, u32[]{:S(2)}) copy-start(bf16[2,256,256]{2,1,0:T(8,128)(2,1)} %constant.65.clone.first_ref) | copy-start | bytes 786436
  58.9 1.6 %collective-permute-start.12 = (bf16[16,32,128]{2,1,0:T(8,128)(2,1)S(1)}, bf16[16,32,128]{2,1,0:T(8,128)(2,1)S(1)}, u32[]{:S(2)}, u32[]{:S(2)}) collective-permute-start(bf16[16,32,128]{2,1,0:T(8,128)(2,1)S(1)} %slice.24), channel_id=1, source_target_pairs={{0,1},{1,0},{2,3},{3,2},{4,5},{5,4},{6,7},{7,6},{8,9},{9,8},{10,11... | collective-permute-start | bytes 393224 | tf_op jit(solution)/shard_map/ppermute | solution.py:232

commit v4 on v3

--- a/solution.py
+++ b/solution.py
@@ -89,7 +89,7 @@
 
 
 def load_all(unpacked, values):
-    unpacked[...] = values.astype(F32).reshape(CTX * BLOCKS * SHARE, LANES)
+    unpacked[: CTX * BLOCKS * SHARE, :] = values.astype(F32).reshape(CTX * BLOCKS * SHARE, LANES)
     return jnp.concatenate(
         [unpacked[pl.ds(at, LANES, stride=SHARE), :] for at in range(SHARE)], axis=1
     ).astype(BF16)
@@ -128,7 +128,8 @@
     result = mm3_left(last_ref, turned)
     for at in range(SHARE):
         gathered[pl.ds(at, LANES, stride=SHARE), :] = result[:, at * LANES : (at + 1) * LANES]
-    out_ref[...] = gathered[...].reshape(CTX, BLOCKS * SHARE, LANES).astype(BF16)
+    result = gathered[: CTX * BLOCKS * SHARE, :]
+    out_ref[...] = result.reshape(CTX, BLOCKS * SHARE, LANES).astype(BF16)
 
 
 def add_products(d_high, place_ref, piece_refs, w_own_ref, w_other_ref, total, squares):
@@ -299,7 +300,7 @@
     blocks = lax.all_to_all(blocks, "ctx", split_axis=0, concat_axis=0, tiled=True)
     other = tp_shift(blocks[:, BLOCKS * SHARE // 2 : BLOCKS * SHARE, :], 0, 0, 1)
     consts = [jnp.asarray(table[k]) for k in ("first", "turn", "second", "second_back", "last")]
-    unpacked = pltpu.VMEM((CTX * BLOCKS * SHARE, LANES), F32)
+    unpacked = pltpu.VMEM(((CTX * BLOCKS + 1) * SHARE, LANES), F32)
     mixed = call(
         mix_kernel,
         bf16(CTX, BLOCKS * SHARE, LANES),

time: 79 us -> 79 us (level)
  no operation moved by 1% of the time
where the time goes in v4:
time: 79 us; the launch traced here: 78.8 us
  blocking collectives  33.4 us (42%)
  waiting for transfers between devices  18.7 us (24%)
  starting transfers between devices  16.7 us (21%)
  Pallas kernels  6.25 us (8%)
  local copies, waits for them, and re-layouts  2.49 us (3%)
  matrix products  0.83 us (1%)
    all_to_all x1, blocking collectives, on_device(): lax.all_to_all(blocks, 'ctx', split_axis=0, concat_axis=0, tiled=True)  19.2 us
    ppermute x13, waiting for transfers between devices, tp_shift(): return lax.ppermute(value, 'tp', pairs)  18.7 us
    ppermute x13, starting transfers between devices, tp_shift(): return lax.ppermute(value, 'tp', pairs)  16.7 us
    all_to_all x1, blocking collectives, on_device(): lax.all_to_all(mixed, 'ctx', split_axis=0, concat_axis=0, tiled=True)  14.2 us
    pallas_call x4, Pallas kernels, call(): pl.pallas_call(kernel, out_shape=outs, in_specs=[first_spec] + [VMEM] * (...  6.25 us
  transfers between devices with their start and end apart: 13, of which 6 were waited for; matrix products, arithmetic and copies ran while one was open for 1% of the time, Pallas kernels for 1%

profile of v4, /device:TPU:8, one launch (start us, length us, event | category | flops | bytes accessed | tf_op | source)
XLA Modules:
  0.0 78.8 jit_solution(7989814927602183232)
XLA Ops:
  0.0 1.0 %constant_dynamic-slice_fusion.1 = (bf16[512,128]{1,0:T(8,128)(2,1)S(1)}, bf16[512,128]{1,0:T(8,128)(2,1)S(1)}) fusion(bf16[1024,128]{1,0:T(8,128)(2,1)} %param.11, s32[]{:T(128)S(6)} %select_n.26, s32[]{:T(128)S(6)} %select_n.27), kind=kLoop, calls=%fused_computation.22 | loop fusion | bytes 524296 | tf_op jit(solution)/shard_map/dynamic_slice | solution.py:263
  1.1 0.6 copy-done.9
  1.9 7.3 %collective-permute-start.1 = (bf16[528,128]{1,0:T(8,128)(2,1)S(1)}, bf16[528,128]{1,0:T(8,128)(2,1)S(1)}, u32[]{:S(2)}, u32[]{:S(2)}) collective-permute-start(bf16[528,128]{1,0:T(8,128)(2,1)S(1)} %get-tuple-element.13), channel_id=1, source_target_pairs={{0,9},{1,8},{2,11},{3,10},{4,13},{5,12},{6,15},{7,14},{8,1},{9,0},... | collective-permute-start | bytes 405512 | tf_op jit(solution)/shard_map/ppermute | solution.py:233
  10.0 1.7 %collective-permute-start.8 = (bf16[2,528,128]{2,1,0:T(8,128)(2,1)S(1)}, bf16[2,528,128]{2,1,0:T(8,128)(2,1)S(1)}, u32[]{:S(2)}, u32[]{:S(2)}) collective-permute-start(bf16[2,528,128]{2,1,0:T(8,128)(2,1)S(1)} %pad_maximum_fusion.1.refs_0_), channel_id=1, source_target_pairs={{0,2},{1,3},{2,4},{3,5},{4,6},{5,7},{6,0},{7,1},{8,10},{9,11},{10,... | collective-permute-start | bytes 811016 | tf_op jit(solution)/shard_map/ppermute | solution.py:233
  11.7 0.7 copy-done.8
  12.4 0.4 fusion.2.refs_7_
  12.8 0.5 collective-permute-start.9
  13.3 8.8 %collective-permute-done = bf16[528,128]{1,0:T(8,128)(2,1)S(1)} collective-permute-done((bf16[528,128]{1,0:T(8,128)(2,1)S(1)}, bf16[528,128]{1,0:T(8,128)(2,1)S(1)}, u32[]{:S(2)}, u32[]{:S(2)}) %collective-permute-start) | collective-permute-done | bytes 135200 | tf_op jit(solution)/shard_map/ppermute | solution.py:233
  22.1 1.7 %collective-permute-start.2 = (bf16[2,528,128]{2,1,0:T(8,128)(2,1)S(1)}, bf16[2,528,128]{2,1,0:T(8,128)(2,1)S(1)}, u32[]{:S(2)}, u32[]{:S(2)}) collective-permute-start(bf16[2,528,128]{2,1,0:T(8,128)(2,1)S(1)} %pad_maximum_fusion.refs_0_), channel_id=1, source_target_pairs={{0,2},{1,3},{2,4},{3,5},{4,6},{5,7},{6,0},{7,1},{8,10},{9,11},{10,... | collective-permute-start | bytes 811016 | tf_op jit(solution)/shard_map/ppermute | solution.py:233
  23.8 0.4 collective-permute-start.3
  24.3 1.7 %collective-permute-start.10 = (bf16[528,128]{1,0:T(8,128)(2,1)S(1)}, bf16[528,128]{1,0:T(8,128)(2,1)S(1)}, u32[]{:S(2)}, u32[]{:S(2)}) collective-permute-start(bf16[528,128]{1,0:T(8,128)(2,1)S(1)} %slice_bitcast_fusion.1), channel_id=1, source_target_pairs={{0,2},{1,3},{2,4},{3,5},{4,6},{5,7},{6,0},{7,1},{8,10},{9,11},{10,... | collective-permute-start | bytes 405512 | tf_op jit(solution)/shard_map/ppermute | solution.py:233
  25.9 0.5 collective-permute-start.11
  26.5 5.2 %collective-permute-done.2.refs_1_ = bf16[2,528,128]{2,1,0:T(8,128)(2,1)S(1)} collective-permute-done((bf16[2,528,128]{2,1,0:T(8,128)(2,1)S(1)}, bf16[2,528,128]{2,1,0:T(8,128)(2,1)S(1)}, u32[]{:S(2)}, u32[]{:S(2)}) %collective-permute-start.2) | collective-permute-done | bytes 270368 | tf_op jit(solution)/shard_map/ppermute | solution.py:233
  31.6 1.7 %collective-permute-start.4 = (bf16[528,128]{1,0:T(8,128)(2,1)S(1)}, bf16[528,128]{1,0:T(8,128)(2,1)S(1)}, u32[]{:S(2)}, u32[]{:S(2)}) collective-permute-start(bf16[528,128]{1,0:T(8,128)(2,1)S(1)} %slice_bitcast_fusion.3), channel_id=1, source_target_pairs={{0,2},{1,3},{2,4},{3,5},{4,6},{5,7},{6,0},{7,1},{8,10},{9,11},{10,... | collective-permute-start | bytes 405512 | tf_op jit(solution)/shard_map/ppermute | solution.py:233
  33.3 0.5 collective-permute-start.5
  34.3 1.5 %collective-permute-done.11.refs_4_ = bf16[528,128]{1,0:T(8,128)(2,1)S(1)} collective-permute-done((bf16[528,128]{1,0:T(8,128)(2,1)S(1)}, bf16[528,128]{1,0:T(8,128)(2,1)S(1)}, u32[]{:S(2)}, u32[]{:S(2)}) %collective-permute-start.11) | collective-permute-done | bytes 135200 | tf_op jit(solution)/shard_map/ppermute | solution.py:233
  35.8 1.0 %shard_map.109 = (f32[512,256]{1,0:T(8,128)S(1)}, f32[512,128]{1,0:T(8,128)S(1)}) custom-call(s32[4]{0:T(128)S(1)} %pad_add_fusion.place_ref, bf16[2,528,128]{2,1,0:T(8,128)(2,1)S(1)} %pad_maximum_fusion.1.refs_0_, bf16[2,528,128]{2,1,0:T(8,128)(2,1)S(1)} %collective-permute-done.8.refs_1_, bf16[2,528,128]{2,1,0:T(8,128)(2,1)S(1)} %collective-permute-done.9.refs_2_, ...), custom_call_target="tpu_custom_call" | custom-call | flops 268435456 | bytes 2129936 | tf_op jit(solution)/shard_map/pallas_call | solution.py:208
  36.8 1.6 %collective-permute-done.5.refs_4_ = bf16[528,128]{1,0:T(8,128)(2,1)S(1)} collective-permute-done((bf16[528,128]{1,0:T(8,128)(2,1)S(1)}, bf16[528,128]{1,0:T(8,128)(2,1)S(1)}, u32[]{:S(2)}, u32[]{:S(2)}) %collective-permute-start.5) | collective-permute-done | bytes 135200 | tf_op jit(solution)/shard_map/ppermute | solution.py:233
  38.4 1.2 %shard_map.110 = bf16[16,128,128]{2,1,0:T(8,128)(2,1)S(1)} custom-call(s32[4]{0:T(128)S(1)} %pad_add_fusion.place_ref, bf16[2,528,128]{2,1,0:T(8,128)(2,1)S(1)} %pad_maximum_fusion.refs_0_, bf16[2,528,128]{2,1,0:T(8,128)(2,1)S(1)} %collective-permute-done.2.refs_1_, bf16[2,528,128]{2,1,0:T(8,128)(2,1)S(1)} %collective-permute-done.3.refs_2_, ...), custom_call_target="tpu_custom_call" | custom-call | flops 268435456 | bytes 3178512 | tf_op jit(solution)/shard_map/pallas_call | solution.py:208
  39.6 19.2 %all_to_all.10.own_ref = bf16[16,128,128]{2,1,0:T(8,128)(2,1)S(1)} all-to-all(bf16[16,128,128]{2,1,0:T(8,128)(2,1)S(1)} %shard_map.110), channel_id=1, replica_groups=mesh['ctx'=16,'tp'=16] {'ctx'}, dimensions={0} | all-to-all | bytes 1048576 | tf_op jit(solution)/shard_map/all_to_all | solution.py:300
  59.2 1.3 %collective-permute-done.12.other_ref = bf16[16,32,128]{2,1,0:T(8,128)(2,1)S(1)} collective-permute-done((bf16[16,32,128]{2,1,0:T(8,128)(2,1)S(1)}, bf16[16,32,128]{2,1,0:T(8,128)(2,1)S(1)}, u32[]{:S(2)}, u32[]{:S(2)}) %collective-permute-start.12) | collective-permute-done | bytes 131104 | tf_op jit(solution)/shard_map/ppermute | solution.py:233
  60.5 3.2 %shard_map.111 = bf16[16,64,128]{2,1,0:T(8,128)(2,1)S(1)} custom-call(s32[4]{0:T(128)S(1)} %pad_add_fusion.place_ref, bf16[16,128,128]{2,1,0:T(8,128)(2,1)S(1)} %all_to_all.10.own_ref, bf16[16,32,128]{2,1,0:T(8,128)(2,1)S(1)} %collective-permute-done.12.other_ref, bf16[2,256,256]{2,1,0:T(8,128)(2,1)S(1)} %copy-done.2, f32[2,128,128]{2,1,0:T(8,128)S(1)} %copy-done.5, ...), custom_call_target="tpu_custom_call" | custom-call | flops 3000000000 | bytes 1703952 | tf_op jit(solution)/shard_map/pallas_call | solution.py:208
  63.8 14.2 %all_to_all.11.blocks_ref = bf16[16,64,128]{2,1,0:T(8,128)(2,1)S(1)} all-to-all(bf16[16,64,128]{2,1,0:T(8,128)(2,1)S(1)} %shard_map.111), channel_id=1, replica_groups=mesh['ctx'=16,'tp'=16] {'ctx'}, dimensions={0} | all-to-all | bytes 524288 | tf_op jit(solution)/shard_map/all_to_all | solution.py:312
  77.9 0.8 %shard_map.112 = bf16[1024,128]{1,0:T(8,128)(2,1)} custom-call(bf16[16,64,128]{2,1,0:T(8,128)(2,1)S(1)} %all_to_all.11.blocks_ref), custom_call_target="tpu_custom_call" | custom-call | bytes 262144 | tf_op jit(solution)/shard_map/pallas_call | solution.py:208
  (42 shorter events, 1.8 us)
Async XLA Ops:
  0.0 9.6 %copy-start = (f32[24,1024]{1,0:T(8,128)S(1)}, f32[24,1024]{1,0:T(8,128)}, u32[]{:S(2)}) copy-start(f32[24,1024]{1,0:T(8,128)} %param.14) | copy-start | bytes 294916
  0.0 9.2 %copy-start.1 = (bf16[2048,128]{1,0:T(8,128)(2,1)S(1)}, bf16[2048,128]{1,0:T(8,128)(2,1)}, u32[]{:S(2)}) copy-start(bf16[2048,128]{1,0:T(8,128)(2,1)} %refs_5_.3) | copy-start | bytes 1572868
  1.1 0.7 copy-start.9
  1.7 7.8 %copy-start.7 = (bf16[24,128]{1,0:T(8,128)(2,1)S(1)}, bf16[24,128]{1,0:T(8,128)(2,1)}, u32[]{:S(2)}) copy-start(bf16[24,128]{1,0:T(8,128)(2,1)} %param.15) | copy-start | bytes 18436
  1.8 8.2 %collective-permute-start.7 = (bf16[528,128]{1,0:T(8,128)(2,1)S(1)}, bf16[528,128]{1,0:T(8,128)(2,1)S(1)}, u32[]{:S(2)}, u32[]{:S(2)}) collective-permute-start(bf16[528,128]{1,0:T(8,128)(2,1)S(1)} %get-tuple-element.13), channel_id=1, source_target_pairs={{0,1},{1,0},{2,3},{3,2},{4,5},{5,4},{6,7},{7,6},{8,9},{9,8},{10,11... | collective-permute-start | bytes 405512 | tf_op jit(solution)/shard_map/ppermute | solution.py:233
  1.9 20.2 %collective-permute-start.1 = (bf16[528,128]{1,0:T(8,128)(2,1)S(1)}, bf16[528,128]{1,0:T(8,128)(2,1)S(1)}, u32[]{:S(2)}, u32[]{:S(2)}) collective-permute-start(bf16[528,128]{1,0:T(8,128)(2,1)S(1)} %get-tuple-element.13), channel_id=1, source_target_pairs={{0,9},{1,8},{2,11},{3,10},{4,13},{5,12},{6,15},{7,14},{8,1},{9,0},... | collective-permute-start | bytes 405512 | tf_op jit(solution)/shard_map/ppermute | solution.py:233
  9.2 24.7 %collective-permute-start.6 = (bf16[2048,128]{1,0:T(8,128)(2,1)S(1)}, bf16[2048,128]{1,0:T(8,128)(2,1)S(1)}, u32[]{:S(2)}, u32[]{:S(2)}) collective-permute-start(bf16[2048,128]{1,0:T(8,128)(2,1)S(1)} %copy-done.1), channel_id=1, source_target_pairs={{0,1},{1,0},{2,3},{3,2},{4,5},{5,4},{6,7},{7,6},{8,9},{9,8},{10,11... | collective-permute-start | bytes 1572872 | tf_op jit(solution)/shard_map/ppermute | solution.py:233
  9.3 12.8 %collective-permute-start = (bf16[528,128]{1,0:T(8,128)(2,1)S(1)}, bf16[528,128]{1,0:T(8,128)(2,1)S(1)}, u32[]{:S(2)}, u32[]{:S(2)}) collective-permute-start(bf16[528,128]{1,0:T(8,128)(2,1)S(1)} %get-tuple-element.12), channel_id=1, source_target_pairs={{0,8},{1,9},{2,10},{3,11},{4,12},{5,13},{6,14},{7,15},{8,0},{9,1},... | collective-permute-start | bytes 405512 | tf_op jit(solution)/shard_map/ppermute | solution.py:233
  10.0 14.2 %collective-permute-start.8 = (bf16[2,528,128]{2,1,0:T(8,128)(2,1)S(1)}, bf16[2,528,128]{2,1,0:T(8,128)(2,1)S(1)}, u32[]{:S(2)}, u32[]{:S(2)}) collective-permute-start(bf16[2,528,128]{2,1,0:T(8,128)(2,1)S(1)} %pad_maximum_fusion.1.refs_0_), channel_id=1, source_target_pairs={{0,2},{1,3},{2,4},{3,5},{4,6},{5,7},{6,0},{7,1},{8,10},{9,11},{10,... | collective-permute-start | bytes 811016 | tf_op jit(solution)/shard_map/ppermute | solution.py:233
  11.7 0.7 copy-start.8
  12.8 13.1 %collective-permute-start.9 = (bf16[2,528,128]{2,1,0:T(8,128)(2,1)S(1)}, bf16[2,528,128]{2,1,0:T(8,128)(2,1)S(1)}, u32[]{:S(2)}, u32[]{:S(2)}) collective-permute-start(bf16[2,528,128]{2,1,0:T(8,128)(2,1)S(1)} %pad_maximum_fusion.1.refs_0_), channel_id=1, source_target_pairs={{0,6},{1,7},{2,0},{3,1},{4,2},{5,3},{6,4},{7,5},{8,14},{9,15},{10,... | collective-permute-start | bytes 811016 | tf_op jit(solution)/shard_map/ppermute | solution.py:233
  22.1 9.5 %collective-permute-start.2 = (bf16[2,528,128]{2,1,0:T(8,128)(2,1)S(1)}, bf16[2,528,128]{2,1,0:T(8,128)(2,1)S(1)}, u32[]{:S(2)}, u32[]{:S(2)}) collective-permute-start(bf16[2,528,128]{2,1,0:T(8,128)(2,1)S(1)} %pad_maximum_fusion.refs_0_), channel_id=1, source_target_pairs={{0,2},{1,3},{2,4},{3,5},{4,6},{5,7},{6,0},{7,1},{8,10},{9,11},{10,... | collective-permute-start | bytes 811016 | tf_op jit(solution)/shard_map/ppermute | solution.py:233
  23.8 9.5 %collective-permute-start.3 = (bf16[2,528,128]{2,1,0:T(8,128)(2,1)S(1)}, bf16[2,528,128]{2,1,0:T(8,128)(2,1)S(1)}, u32[]{:S(2)}, u32[]{:S(2)}) collective-permute-start(bf16[2,528,128]{2,1,0:T(8,128)(2,1)S(1)} %pad_maximum_fusion.refs_0_), channel_id=1, source_target_pairs={{0,6},{1,7},{2,0},{3,1},{4,2},{5,3},{6,4},{7,5},{8,14},{9,15},{10,... | collective-permute-start | bytes 811016 | tf_op jit(solution)/shard_map/ppermute | solution.py:233
  24.3 10.0 %collective-permute-start.10 = (bf16[528,128]{1,0:T(8,128)(2,1)S(1)}, bf16[528,128]{1,0:T(8,128)(2,1)S(1)}, u32[]{:S(2)}, u32[]{:S(2)}) collective-permute-start(bf16[528,128]{1,0:T(8,128)(2,1)S(1)} %slice_bitcast_fusion.1), channel_id=1, source_target_pairs={{0,2},{1,3},{2,4},{3,5},{4,6},{5,7},{6,0},{7,1},{8,10},{9,11},{10,... | collective-permute-start | bytes 405512 | tf_op jit(solution)/shard_map/ppermute | solution.py:233
  25.9 9.8 %collective-permute-start.11 = (bf16[528,128]{1,0:T(8,128)(2,1)S(1)}, bf16[528,128]{1,0:T(8,128)(2,1)S(1)}, u32[]{:S(2)}, u32[]{:S(2)}) collective-permute-start(bf16[528,128]{1,0:T(8,128)(2,1)S(1)} %slice_bitcast_fusion), channel_id=1, source_target_pairs={{0,6},{1,7},{2,0},{3,1},{4,2},{5,3},{6,4},{7,5},{8,14},{9,15},{10,... | collective-permute-start | bytes 405512 | tf_op jit(solution)/shard_map/ppermute | solution.py:233
  31.6 5.1 %collective-permute-start.4 = (bf16[528,128]{1,0:T(8,128)(2,1)S(1)}, bf16[528,128]{1,0:T(8,128)(2,1)S(1)}, u32[]{:S(2)}, u32[]{:S(2)}) collective-permute-start(bf16[528,128]{1,0:T(8,128)(2,1)S(1)} %slice_bitcast_fusion.3), channel_id=1, source_target_pairs={{0,2},{1,3},{2,4},{3,5},{4,6},{5,7},{6,0},{7,1},{8,10},{9,11},{10,... | collective-permute-start | bytes 405512 | tf_op jit(solution)/shard_map/ppermute | solution.py:233
  33.3 5.1 %collective-permute-start.5 = (bf16[528,128]{1,0:T(8,128)(2,1)S(1)}, bf16[528,128]{1,0:T(8,128)(2,1)S(1)}, u32[]{:S(2)}, u32[]{:S(2)}) collective-permute-start(bf16[528,128]{1,0:T(8,128)(2,1)S(1)} %slice_bitcast_fusion.2), channel_id=1, source_target_pairs={{0,6},{1,7},{2,0},{3,1},{4,2},{5,3},{6,4},{7,5},{8,14},{9,15},{10,... | collective-permute-start | bytes 405512 | tf_op jit(solution)/shard_map/ppermute | solution.py:233
  39.6 20.9 %copy-start.3 = (bf16[2,256,256]{2,1,0:T(8,128)(2,1)S(1)}, bf16[2,256,256]{2,1,0:T(8,128)(2,1)}, u32[]{:S(2)}) copy-start(bf16[2,256,256]{2,1,0:T(8,128)(2,1)} %constant.67.clone.second_ref) | copy-start | bytes 786436
  39.6 20.9 %copy-start.4 = (bf16[2,256,256]{2,1,0:T(8,128)(2,1)S(1)}, bf16[2,256,256]{2,1,0:T(8,128)(2,1)}, u32[]{:S(2)}) copy-start(bf16[2,256,256]{2,1,0:T(8,128)(2,1)} %constant.68.clone.back_ref) | copy-start | bytes 786436
  39.6 20.9 %copy-start.5 = (f32[2,128,128]{2,1,0:T(8,128)S(1)}, f32[2,128,128]{2,1,0:T(8,128)}, u32[]{:S(2)}) copy-start(f32[2,128,128]{2,1,0:T(8,128)} %constant.66.clone.turn_ref) | copy-start | bytes 393220
  39.6 20.9 %copy-start.6 = (bf16[2,128,256]{2,1,0:T(8,128)(2,1)S(1)}, bf16[2,128,256]{2,1,0:T(8,128)(2,1)}, u32[]{:S(2)}) copy-start(bf16[2,128,256]{2,1,0:T(8,128)(2,1)} %constant.69.clone.last_ref) | copy-start | bytes 393220
  58.9 1.7 %copy-start.2 = (bf16[2,256,256]{2,1,0:T(8,128)(2,1)S(1)}, bf16[2,256,256]{2,1,0:T(8,128)(2,1)}, u32[]{:S(2)}) copy-start(bf16[2,256,256]{2,1,0:T(8,128)(2,1)} %constant.65.clone.first_ref) | copy-start | bytes 786436
  58.9 1.6 %collective-permute-start.12 = (bf16[16,32,128]{2,1,0:T(8,128)(2,1)S(1)}, bf16[16,32,128]{2,1,0:T(8,128)(2,1)S(1)}, u32[]{:S(2)}, u32[]{:S(2)}) collective-permute-start(bf16[16,32,128]{2,1,0:T(8,128)(2,1)S(1)} %slice.24), channel_id=1, source_target_pairs={{0,1},{1,0},{2,3},{3,2},{4,5},{5,4},{6,7},{7,6},{8,9},{9,8},{10,11... | collective-permute-start | bytes 393224 | tf_op jit(solution)/shard_map/ppermute | solution.py:233

commit v5 on v4

--- a/solution.py
+++ b/solution.py
@@ -216,6 +216,11 @@
     )(*operands)
 
 
+def half_kernel(value_ref, out_ref):
+    rows = BLOCKS * SHARE // 2
+    out_ref[...] = value_ref[:, rows : 2 * rows, :]
+
+
 def bf16(*shape):
     return jax.ShapeDtypeStruct(shape, BF16)
 
@@ -298,7 +303,7 @@
         flops=flops,
     )
     blocks = lax.all_to_all(blocks, "ctx", split_axis=0, concat_axis=0, tiled=True)
-    other = tp_shift(blocks[:, BLOCKS * SHARE // 2 : BLOCKS * SHARE, :], 0, 0, 1)
+    other = tp_shift(call(half_kernel, bf16(CTX, BLOCKS * SHARE // 2, LANES), [blocks]), 0, 0, 1)
     consts = [jnp.asarray(table[k]) for k in ("first", "turn", "second", "second_back", "last")]
     unpacked = pltpu.VMEM(((CTX * BLOCKS + 1) * SHARE, LANES), F32)
     mixed = call(

time: 79 us -> 79 us (level)
    pallas_call x4 -> x5, Pallas kernels: 6.25 us -> 6.26 us  [call(): pl.pallas_call(kernel, out_shape=outs, in_specs=[first_spec] + [VMEM] * (...]
where the time goes in v5:
time: 79 us; the launch traced here: 78.8 us
  blocking collectives  33.4 us (42%)
  waiting for transfers between devices  18.7 us (24%)
  starting transfers between devices  16.7 us (21%)
  Pallas kernels  6.26 us (8%)
  local copies, waits for them, and re-layouts  2.47 us (3%)
  matrix products  0.83 us (1%)
    all_to_all x1, blocking collectives, on_device(): lax.all_to_all(blocks, 'ctx', split_axis=0, concat_axis=0, tiled=True)  19.2 us
    ppermute x13, waiting for transfers between devices, tp_shift(): return lax.ppermute(value, 'tp', pairs)  18.7 us
    ppermute x13, starting transfers between devices, tp_shift(): return lax.ppermute(value, 'tp', pairs)  16.7 us
    all_to_all x1, blocking collectives, on_device(): lax.all_to_all(mixed, 'ctx', split_axis=0, concat_axis=0, tiled=True)  14.2 us
    pallas_call x5, Pallas kernels, call(): pl.pallas_call(kernel, out_shape=outs, in_specs=[first_spec] + [VMEM] * (...  6.26 us
  transfers between devices with their start and end apart: 13, of which 6 were waited for; matrix products, arithmetic and copies ran while one was open for 1% of the time, Pallas kernels for 1%

profile of v5, /device:TPU:8, one launch (start us, length us, event | category | flops | bytes accessed | tf_op | source)
XLA Modules:
  0.0 78.8 jit_solution(2541292802930894328)
XLA Ops:
  0.0 1.0 %constant_dynamic-slice_fusion.1 = (bf16[512,128]{1,0:T(8,128)(2,1)S(1)}, bf16[512,128]{1,0:T(8,128)(2,1)S(1)}) fusion(bf16[1024,128]{1,0:T(8,128)(2,1)} %param.11, s32[]{:T(128)S(6)} %select_n.26, s32[]{:T(128)S(6)} %select_n.27), kind=kLoop, calls=%fused_computation.22 | loop fusion | bytes 524296 | tf_op jit(solution)/shard_map/dynamic_slice | solution.py:268
  1.1 0.6 copy-done.9
  1.9 7.3 %collective-permute-start.1 = (bf16[528,128]{1,0:T(8,128)(2,1)S(1)}, bf16[528,128]{1,0:T(8,128)(2,1)S(1)}, u32[]{:S(2)}, u32[]{:S(2)}) collective-permute-start(bf16[528,128]{1,0:T(8,128)(2,1)S(1)} %get-tuple-element.13), channel_id=1, source_target_pairs={{0,9},{1,8},{2,11},{3,10},{4,13},{5,12},{6,15},{7,14},{8,1},{9,0},... | collective-permute-start | bytes 405512 | tf_op jit(solution)/shard_map/ppermute | solution.py:238
  10.0 1.7 %collective-permute-start.8 = (bf16[2,528,128]{2,1,0:T(8,128)(2,1)S(1)}, bf16[2,528,128]{2,1,0:T(8,128)(2,1)S(1)}, u32[]{:S(2)}, u32[]{:S(2)}) collective-permute-start(bf16[2,528,128]{2,1,0:T(8,128)(2,1)S(1)} %pad_maximum_fusion.1.refs_0_), channel_id=1, source_target_pairs={{0,2},{1,3},{2,4},{3,5},{4,6},{5,7},{6,0},{7,1},{8,10},{9,11},{10,... | collective-permute-start | bytes 811016 | tf_op jit(solution)/shard_map/ppermute | solution.py:238
  11.7 0.7 copy-done.8
  12.4 0.4 fusion.2.refs_7_
  12.8 0.5 collective-permute-start.9
  13.3 8.8 %collective-permute-done = bf16[528,128]{1,0:T(8,128)(2,1)S(1)} collective-permute-done((bf16[528,128]{1,0:T(8,128)(2,1)S(1)}, bf16[528,128]{1,0:T(8,128)(2,1)S(1)}, u32[]{:S(2)}, u32[]{:S(2)}) %collective-permute-start) | collective-permute-done | bytes 135200 | tf_op jit(solution)/shard_map/ppermute | solution.py:238
  22.1 1.7 %collective-permute-start.2 = (bf16[2,528,128]{2,1,0:T(8,128)(2,1)S(1)}, bf16[2,528,128]{2,1,0:T(8,128)(2,1)S(1)}, u32[]{:S(2)}, u32[]{:S(2)}) collective-permute-start(bf16[2,528,128]{2,1,0:T(8,128)(2,1)S(1)} %pad_maximum_fusion.refs_0_), channel_id=1, source_target_pairs={{0,2},{1,3},{2,4},{3,5},{4,6},{5,7},{6,0},{7,1},{8,10},{9,11},{10,... | collective-permute-start | bytes 811016 | tf_op jit(solution)/shard_map/ppermute | solution.py:238
  23.8 0.4 collective-permute-start.3
  24.3 1.7 %collective-permute-start.10 = (bf16[528,128]{1,0:T(8,128)(2,1)S(1)}, bf16[528,128]{1,0:T(8,128)(2,1)S(1)}, u32[]{:S(2)}, u32[]{:S(2)}) collective-permute-start(bf16[528,128]{1,0:T(8,128)(2,1)S(1)} %slice_bitcast_fusion.1), channel_id=1, source_target_pairs={{0,2},{1,3},{2,4},{3,5},{4,6},{5,7},{6,0},{7,1},{8,10},{9,11},{10,... | collective-permute-start | bytes 405512 | tf_op jit(solution)/shard_map/ppermute | solution.py:238
  25.9 0.5 collective-permute-start.11
  26.5 5.2 %collective-permute-done.2.refs_1_ = bf16[2,528,128]{2,1,0:T(8,128)(2,1)S(1)} collective-permute-done((bf16[2,528,128]{2,1,0:T(8,128)(2,1)S(1)}, bf16[2,528,128]{2,1,0:T(8,128)(2,1)S(1)}, u32[]{:S(2)}, u32[]{:S(2)}) %collective-permute-start.2) | collective-permute-done | bytes 270368 | tf_op jit(solution)/shard_map/ppermute | solution.py:238
  31.6 1.7 %collective-permute-start.4 = (bf16[528,128]{1,0:T(8,128)(2,1)S(1)}, bf16[528,128]{1,0:T(8,128)(2,1)S(1)}, u32[]{:S(2)}, u32[]{:S(2)}) collective-permute-start(bf16[528,128]{1,0:T(8,128)(2,1)S(1)} %slice_bitcast_fusion.3), channel_id=1, source_target_pairs={{0,2},{1,3},{2,4},{3,5},{4,6},{5,7},{6,0},{7,1},{8,10},{9,11},{10,... | collective-permute-start | bytes 405512 | tf_op jit(solution)/shard_map/ppermute | solution.py:238
  33.3 0.5 collective-permute-start.5
  34.3 1.5 %collective-permute-done.11.refs_4_ = bf16[528,128]{1,0:T(8,128)(2,1)S(1)} collective-permute-done((bf16[528,128]{1,0:T(8,128)(2,1)S(1)}, bf16[528,128]{1,0:T(8,128)(2,1)S(1)}, u32[]{:S(2)}, u32[]{:S(2)}) %collective-permute-start.11) | collective-permute-done | bytes 135200 | tf_op jit(solution)/shard_map/ppermute | solution.py:238
  35.8 1.0 %shard_map.109 = (f32[512,256]{1,0:T(8,128)S(1)}, f32[512,128]{1,0:T(8,128)S(1)}) custom-call(s32[4]{0:T(128)S(1)} %pad_add_fusion.place_ref, bf16[2,528,128]{2,1,0:T(8,128)(2,1)S(1)} %pad_maximum_fusion.1.refs_0_, bf16[2,528,128]{2,1,0:T(8,128)(2,1)S(1)} %collective-permute-done.8.refs_1_, bf16[2,528,128]{2,1,0:T(8,128)(2,1)S(1)} %collective-permute-done.9.refs_2_, ...), custom_call_target="tpu_custom_call" | custom-call | flops 268435456 | bytes 2129936 | tf_op jit(solution)/shard_map/pallas_call | solution.py:208
  36.8 1.6 %collective-permute-done.5.refs_4_ = bf16[528,128]{1,0:T(8,128)(2,1)S(1)} collective-permute-done((bf16[528,128]{1,0:T(8,128)(2,1)S(1)}, bf16[528,128]{1,0:T(8,128)(2,1)S(1)}, u32[]{:S(2)}, u32[]{:S(2)}) %collective-permute-start.5) | collective-permute-done | bytes 135200 | tf_op jit(solution)/shard_map/ppermute | solution.py:238
  38.4 1.2 %shard_map.110 = bf16[16,128,128]{2,1,0:T(8,128)(2,1)S(1)} custom-call(s32[4]{0:T(128)S(1)} %pad_add_fusion.place_ref, bf16[2,528,128]{2,1,0:T(8,128)(2,1)S(1)} %pad_maximum_fusion.refs_0_, bf16[2,528,128]{2,1,0:T(8,128)(2,1)S(1)} %collective-permute-done.2.refs_1_, bf16[2,528,128]{2,1,0:T(8,128)(2,1)S(1)} %collective-permute-done.3.refs_2_, ...), custom_call_target="tpu_custom_call" | custom-call | flops 268435456 | bytes 3178512 | tf_op jit(solution)/shard_map/pallas_call | solution.py:208
  39.6 19.2 %all_to_all.10.value_ref.own_ref = bf16[16,128,128]{2,1,0:T(8,128)(2,1)S(1)} all-to-all(bf16[16,128,128]{2,1,0:T(8,128)(2,1)S(1)} %shard_map.110), channel_id=1, replica_groups=mesh['ctx'=16,'tp'=16] {'ctx'}, dimensions={0} | all-to-all | bytes 1048576 | tf_op jit(solution)/shard_map/all_to_all | solution.py:305
  59.2 1.3 %collective-permute-done.12.other_ref = bf16[16,32,128]{2,1,0:T(8,128)(2,1)S(1)} collective-permute-done((bf16[16,32,128]{2,1,0:T(8,128)(2,1)S(1)}, bf16[16,32,128]{2,1,0:T(8,128)(2,1)S(1)}, u32[]{:S(2)}, u32[]{:S(2)}) %collective-permute-start.12) | collective-permute-done | bytes 131104 | tf_op jit(solution)/shard_map/ppermute | solution.py:238
  60.5 3.2 %shard_map.112 = bf16[16,64,128]{2,1,0:T(8,128)(2,1)S(1)} custom-call(s32[4]{0:T(128)S(1)} %pad_add_fusion.place_ref, bf16[16,128,128]{2,1,0:T(8,128)(2,1)S(1)} %all_to_all.10.value_ref.own_ref, bf16[16,32,128]{2,1,0:T(8,128)(2,1)S(1)} %collective-permute-done.12.other_ref, bf16[2,256,256]{2,1,0:T(8,128)(2,1)S(1)} %copy-done.2, ...), custom_call_target="tpu_custom_call" | custom-call | flops 3000000000 | bytes 1703952 | tf_op jit(solution)/shard_map/pallas_call | solution.py:208
  63.7 14.2 %all_to_all.11.blocks_ref = bf16[16,64,128]{2,1,0:T(8,128)(2,1)S(1)} all-to-all(bf16[16,64,128]{2,1,0:T(8,128)(2,1)S(1)} %shard_map.112), channel_id=1, replica_groups=mesh['ctx'=16,'tp'=16] {'ctx'}, dimensions={0} | all-to-all | bytes 524288 | tf_op jit(solution)/shard_map/all_to_all | solution.py:317
  77.9 0.8 %shard_map.113 = bf16[1024,128]{1,0:T(8,128)(2,1)} custom-call(bf16[16,64,128]{2,1,0:T(8,128)(2,1)S(1)} %all_to_all.11.blocks_ref), custom_call_target="tpu_custom_call" | custom-call | bytes 262144 | tf_op jit(solution)/shard_map/pallas_call | solution.py:208
  (42 shorter events, 1.8 us)
Async XLA Ops:
  0.0 9.6 %copy-start = (f32[24,1024]{1,0:T(8,128)S(1)}, f32[24,1024]{1,0:T(8,128)}, u32[]{:S(2)}) copy-start(f32[24,1024]{1,0:T(8,128)} %param.14) | copy-start | bytes 294916
  0.0 9.2 %copy-start.1 = (bf16[2048,128]{1,0:T(8,128)(2,1)S(1)}, bf16[2048,128]{1,0:T(8,128)(2,1)}, u32[]{:S(2)}) copy-start(bf16[2048,128]{1,0:T(8,128)(2,1)} %refs_5_.3) | copy-start | bytes 1572868
  1.1 0.7 copy-start.9
  1.7 7.8 %copy-start.7 = (bf16[24,128]{1,0:T(8,128)(2,1)S(1)}, bf16[24,128]{1,0:T(8,128)(2,1)}, u32[]{:S(2)}) copy-start(bf16[24,128]{1,0:T(8,128)(2,1)} %param.15) | copy-start | bytes 18436
  1.8 8.2 %collective-permute-start.7 = (bf16[528,128]{1,0:T(8,128)(2,1)S(1)}, bf16[528,128]{1,0:T(8,128)(2,1)S(1)}, u32[]{:S(2)}, u32[]{:S(2)}) collective-permute-start(bf16[528,128]{1,0:T(8,128)(2,1)S(1)} %get-tuple-element.13), channel_id=1, source_target_pairs={{0,1},{1,0},{2,3},{3,2},{4,5},{5,4},{6,7},{7,6},{8,9},{9,8},{10,11... | collective-permute-start | bytes 405512 | tf_op jit(solution)/shard_map/ppermute | solution.py:238
  1.9 20.2 %collective-permute-start.1 = (bf16[528,128]{1,0:T(8,128)(2,1)S(1)}, bf16[528,128]{1,0:T(8,128)(2,1)S(1)}, u32[]{:S(2)}, u32[]{:S(2)}) collective-permute-start(bf16[528,128]{1,0:T(8,128)(2,1)S(1)} %get-tuple-element.13), channel_id=1, source_target_pairs={{0,9},{1,8},{2,11},{3,10},{4,13},{5,12},{6,15},{7,14},{8,1},{9,0},... | collective-permute-start | bytes 405512 | tf_op jit(solution)/shard_map/ppermute | solution.py:238
  9.2 24.7 %collective-permute-start.6 = (bf16[2048,128]{1,0:T(8,128)(2,1)S(1)}, bf16[2048,128]{1,0:T(8,128)(2,1)S(1)}, u32[]{:S(2)}, u32[]{:S(2)}) collective-permute-start(bf16[2048,128]{1,0:T(8,128)(2,1)S(1)} %copy-done.1), channel_id=1, source_target_pairs={{0,1},{1,0},{2,3},{3,2},{4,5},{5,4},{6,7},{7,6},{8,9},{9,8},{10,11... | collective-permute-start | bytes 1572872 | tf_op jit(solution)/shard_map/ppermute | solution.py:238
  9.3 12.8 %collective-permute-start = (bf16[528,128]{1,0:T(8,128)(2,1)S(1)}, bf16[528,128]{1,0:T(8,128)(2,1)S(1)}, u32[]{:S(2)}, u32[]{:S(2)}) collective-permute-start(bf16[528,128]{1,0:T(8,128)(2,1)S(1)} %get-tuple-element.12), channel_id=1, source_target_pairs={{0,8},{1,9},{2,10},{3,11},{4,12},{5,13},{6,14},{7,15},{8,0},{9,1},... | collective-permute-start | bytes 405512 | tf_op jit(solution)/shard_map/ppermute | solution.py:238
  10.0 14.2 %collective-permute-start.8 = (bf16[2,528,128]{2,1,0:T(8,128)(2,1)S(1)}, bf16[2,528,128]{2,1,0:T(8,128)(2,1)S(1)}, u32[]{:S(2)}, u32[]{:S(2)}) collective-permute-start(bf16[2,528,128]{2,1,0:T(8,128)(2,1)S(1)} %pad_maximum_fusion.1.refs_0_), channel_id=1, source_target_pairs={{0,2},{1,3},{2,4},{3,5},{4,6},{5,7},{6,0},{7,1},{8,10},{9,11},{10,... | collective-permute-start | bytes 811016 | tf_op jit(solution)/shard_map/ppermute | solution.py:238
  11.7 0.7 copy-start.8
  12.8 13.1 %collective-permute-start.9 = (bf16[2,528,128]{2,1,0:T(8,128)(2,1)S(1)}, bf16[2,528,128]{2,1,0:T(8,128)(2,1)S(1)}, u32[]{:S(2)}, u32[]{:S(2)}) collective-permute-start(bf16[2,528,128]{2,1,0:T(8,128)(2,1)S(1)} %pad_maximum_fusion.1.refs_0_), channel_id=1, source_target_pairs={{0,6},{1,7},{2,0},{3,1},{4,2},{5,3},{6,4},{7,5},{8,14},{9,15},{10,... | collective-permute-start | bytes 811016 | tf_op jit(solution)/shard_map/ppermute | solution.py:238
  22.1 9.5 %collective-permute-start.2 = (bf16[2,528,128]{2,1,0:T(8,128)(2,1)S(1)}, bf16[2,528,128]{2,1,0:T(8,128)(2,1)S(1)}, u32[]{:S(2)}, u32[]{:S(2)}) collective-permute-start(bf16[2,528,128]{2,1,0:T(8,128)(2,1)S(1)} %pad_maximum_fusion.refs_0_), channel_id=1, source_target_pairs={{0,2},{1,3},{2,4},{3,5},{4,6},{5,7},{6,0},{7,1},{8,10},{9,11},{10,... | collective-permute-start | bytes 811016 | tf_op jit(solution)/shard_map/ppermute | solution.py:238
  23.8 9.5 %collective-permute-start.3 = (bf16[2,528,128]{2,1,0:T(8,128)(2,1)S(1)}, bf16[2,528,128]{2,1,0:T(8,128)(2,1)S(1)}, u32[]{:S(2)}, u32[]{:S(2)}) collective-permute-start(bf16[2,528,128]{2,1,0:T(8,128)(2,1)S(1)} %pad_maximum_fusion.refs_0_), channel_id=1, source_target_pairs={{0,6},{1,7},{2,0},{3,1},{4,2},{5,3},{6,4},{7,5},{8,14},{9,15},{10,... | collective-permute-start | bytes 811016 | tf_op jit(solution)/shard_map/ppermute | solution.py:238
  24.3 10.0 %collective-permute-start.10 = (bf16[528,128]{1,0:T(8,128)(2,1)S(1)}, bf16[528,128]{1,0:T(8,128)(2,1)S(1)}, u32[]{:S(2)}, u32[]{:S(2)}) collective-permute-start(bf16[528,128]{1,0:T(8,128)(2,1)S(1)} %slice_bitcast_fusion.1), channel_id=1, source_target_pairs={{0,2},{1,3},{2,4},{3,5},{4,6},{5,7},{6,0},{7,1},{8,10},{9,11},{10,... | collective-permute-start | bytes 405512 | tf_op jit(solution)/shard_map/ppermute | solution.py:238
  25.9 9.8 %collective-permute-start.11 = (bf16[528,128]{1,0:T(8,128)(2,1)S(1)}, bf16[528,128]{1,0:T(8,128)(2,1)S(1)}, u32[]{:S(2)}, u32[]{:S(2)}) collective-permute-start(bf16[528,128]{1,0:T(8,128)(2,1)S(1)} %slice_bitcast_fusion), channel_id=1, source_target_pairs={{0,6},{1,7},{2,0},{3,1},{4,2},{5,3},{6,4},{7,5},{8,14},{9,15},{10,... | collective-permute-start | bytes 405512 | tf_op jit(solution)/shard_map/ppermute | solution.py:238
  31.6 5.1 %collective-permute-start.4 = (bf16[528,128]{1,0:T(8,128)(2,1)S(1)}, bf16[528,128]{1,0:T(8,128)(2,1)S(1)}, u32[]{:S(2)}, u32[]{:S(2)}) collective-permute-start(bf16[528,128]{1,0:T(8,128)(2,1)S(1)} %slice_bitcast_fusion.3), channel_id=1, source_target_pairs={{0,2},{1,3},{2,4},{3,5},{4,6},{5,7},{6,0},{7,1},{8,10},{9,11},{10,... | collective-permute-start | bytes 405512 | tf_op jit(solution)/shard_map/ppermute | solution.py:238
  33.3 5.1 %collective-permute-start.5 = (bf16[528,128]{1,0:T(8,128)(2,1)S(1)}, bf16[528,128]{1,0:T(8,128)(2,1)S(1)}, u32[]{:S(2)}, u32[]{:S(2)}) collective-permute-start(bf16[528,128]{1,0:T(8,128)(2,1)S(1)} %slice_bitcast_fusion.2), channel_id=1, source_target_pairs={{0,6},{1,7},{2,0},{3,1},{4,2},{5,3},{6,4},{7,5},{8,14},{9,15},{10,... | collective-permute-start | bytes 405512 | tf_op jit(solution)/shard_map/ppermute | solution.py:238
  39.6 20.9 %copy-start.4 = (bf16[2,256,256]{2,1,0:T(8,128)(2,1)S(1)}, bf16[2,256,256]{2,1,0:T(8,128)(2,1)}, u32[]{:S(2)}) copy-start(bf16[2,256,256]{2,1,0:T(8,128)(2,1)} %constant.68.clone.back_ref) | copy-start | bytes 786436
  39.6 20.9 %copy-start.6 = (bf16[2,128,256]{2,1,0:T(8,128)(2,1)S(1)}, bf16[2,128,256]{2,1,0:T(8,128)(2,1)}, u32[]{:S(2)}) copy-start(bf16[2,128,256]{2,1,0:T(8,128)(2,1)} %constant.69.clone.last_ref) | copy-start | bytes 393220
  58.9 1.6 %copy-start.2 = (bf16[2,256,256]{2,1,0:T(8,128)(2,1)S(1)}, bf16[2,256,256]{2,1,0:T(8,128)(2,1)}, u32[]{:S(2)}) copy-start(bf16[2,256,256]{2,1,0:T(8,128)(2,1)} %constant.65.clone.first_ref) | copy-start | bytes 786436
  58.9 1.6 %copy-start.3 = (bf16[2,256,256]{2,1,0:T(8,128)(2,1)S(1)}, bf16[2,256,256]{2,1,0:T(8,128)(2,1)}, u32[]{:S(2)}) copy-start(bf16[2,256,256]{2,1,0:T(8,128)(2,1)} %constant.67.clone.second_ref) | copy-start | bytes 786436
  58.9 1.7 %copy-start.5 = (f32[2,128,128]{2,1,0:T(8,128)S(1)}, f32[2,128,128]{2,1,0:T(8,128)}, u32[]{:S(2)}) copy-start(f32[2,128,128]{2,1,0:T(8,128)} %constant.66.clone.turn_ref) | copy-start | bytes 393220
  58.9 1.6 %collective-permute-start.12 = (bf16[16,32,128]{2,1,0:T(8,128)(2,1)S(1)}, bf16[16,32,128]{2,1,0:T(8,128)(2,1)S(1)}, u32[]{:S(2)}, u32[]{:S(2)}) collective-permute-start(bf16[16,32,128]{2,1,0:T(8,128)(2,1)S(1)} %shard_map.111), channel_id=1, source_target_pairs={{0,1},{1,0},{2,3},{3,2},{4,5},{5,4},{6,7},{7,6},{8,9},{9,8},{10,11... | collective-permute-start | bytes 393224 | tf_op jit(solution)/shard_map/ppermute | solution.py:238

commit v6 on v5

--- a/solution.py
+++ b/solution.py
@@ -246,8 +246,10 @@
         return tp_shift(value, 0, YS - 1, 0)
 
     def ring(value):
-        from_left, from_right = left(value), right(value)
-        return [value, from_left, from_right, left(from_left[0]), right(from_right[1])]
+        from_right = right(value)
+        second = right(from_right[1])
+        from_left = left(value)
+        return [value, from_left, from_right, left(from_left[0]), second]
 
     across = [tp_shift(mine, 1, 0, 0), tp_shift(theirs, 1, 0, 1)]
     own = jnp.stack([mine, tp_shift(theirs, 0, 0, 1)])

time: 79 us -> 79 us (level)
  no operation moved by 1% of the time
where the time goes in v6:
time: 79 us; the launch traced here: 78.8 us
  blocking collectives  33.4 us (42%)
  waiting for transfers between devices  18.7 us (24%)
  starting transfers between devices  16.7 us (21%)
  Pallas kernels  6.26 us (8%)
  local copies, waits for them, and re-layouts  2.47 us (3%)
  matrix products  0.83 us (1%)
    all_to_all x1, blocking collectives, on_device(): lax.all_to_all(blocks, 'ctx', split_axis=0, concat_axis=0, tiled=True)  19.2 us
    ppermute x13, waiting for transfers between devices, tp_shift(): return lax.ppermute(value, 'tp', pairs)  18.7 us
    ppermute x13, starting transfers between devices, tp_shift(): return lax.ppermute(value, 'tp', pairs)  16.7 us
    all_to_all x1, blocking collectives, on_device(): lax.all_to_all(mixed, 'ctx', split_axis=0, concat_axis=0, tiled=True)  14.2 us
    pallas_call x5, Pallas kernels, call(): pl.pallas_call(kernel, out_shape=outs, in_specs=[first_spec] + [VMEM] * (...  6.26 us
  transfers between devices with their start and end apart: 13, of which 6 were waited for; matrix products, arithmetic and copies ran while one was open for 1% of the time, Pallas kernels for 1%

profile of v6, /device:TPU:8, one launch (start us, length us, event | category | flops | bytes accessed | tf_op | source)
XLA Modules:
  0.0 78.8 jit_solution(2541292802930894328)
XLA Ops:
  0.0 1.0 %constant_dynamic-slice_fusion.1 = (bf16[512,128]{1,0:T(8,128)(2,1)S(1)}, bf16[512,128]{1,0:T(8,128)(2,1)S(1)}) fusion(bf16[1024,128]{1,0:T(8,128)(2,1)} %param.11, s32[]{:T(128)S(6)} %select_n.26, s32[]{:T(128)S(6)} %select_n.27), kind=kLoop, calls=%fused_computation.22 | loop fusion | bytes 524296 | tf_op jit(solution)/shard_map/dynamic_slice | solution.py:270
  1.1 0.6 copy-done.9
  1.9 7.3 %collective-permute-start.1 = (bf16[528,128]{1,0:T(8,128)(2,1)S(1)}, bf16[528,128]{1,0:T(8,128)(2,1)S(1)}, u32[]{:S(2)}, u32[]{:S(2)}) collective-permute-start(bf16[528,128]{1,0:T(8,128)(2,1)S(1)} %get-tuple-element.13), channel_id=1, source_target_pairs={{0,9},{1,8},{2,11},{3,10},{4,13},{5,12},{6,15},{7,14},{8,1},{9,0},... | collective-permute-start | bytes 405512 | tf_op jit(solution)/shard_map/ppermute | solution.py:238
  10.0 1.7 %collective-permute-start.8 = (bf16[2,528,128]{2,1,0:T(8,128)(2,1)S(1)}, bf16[2,528,128]{2,1,0:T(8,128)(2,1)S(1)}, u32[]{:S(2)}, u32[]{:S(2)}) collective-permute-start(bf16[2,528,128]{2,1,0:T(8,128)(2,1)S(1)} %pad_maximum_fusion.1.refs_0_), channel_id=1, source_target_pairs={{0,2},{1,3},{2,4},{3,5},{4,6},{5,7},{6,0},{7,1},{8,10},{9,11},{10,... | collective-permute-start | bytes 811016 | tf_op jit(solution)/shard_map/ppermute | solution.py:238
  11.7 0.7 copy-done.8
  12.4 0.4 fusion.2.refs_7_
  12.8 0.5 collective-permute-start.9
  13.3 8.8 %collective-permute-done = bf16[528,128]{1,0:T(8,128)(2,1)S(1)} collective-permute-done((bf16[528,128]{1,0:T(8,128)(2,1)S(1)}, bf16[528,128]{1,0:T(8,128)(2,1)S(1)}, u32[]{:S(2)}, u32[]{:S(2)}) %collective-permute-start) | collective-permute-done | bytes 135200 | tf_op jit(solution)/shard_map/ppermute | solution.py:238
  22.1 1.7 %collective-permute-start.2 = (bf16[2,528,128]{2,1,0:T(8,128)(2,1)S(1)}, bf16[2,528,128]{2,1,0:T(8,128)(2,1)S(1)}, u32[]{:S(2)}, u32[]{:S(2)}) collective-permute-start(bf16[2,528,128]{2,1,0:T(8,128)(2,1)S(1)} %pad_maximum_fusion.refs_0_), channel_id=1, source_target_pairs={{0,2},{1,3},{2,4},{3,5},{4,6},{5,7},{6,0},{7,1},{8,10},{9,11},{10,... | collective-permute-start | bytes 811016 | tf_op jit(solution)/shard_map/ppermute | solution.py:238
  23.8 0.4 collective-permute-start.3
  24.3 1.7 %collective-permute-start.10 = (bf16[528,128]{1,0:T(8,128)(2,1)S(1)}, bf16[528,128]{1,0:T(8,128)(2,1)S(1)}, u32[]{:S(2)}, u32[]{:S(2)}) collective-permute-start(bf16[528,128]{1,0:T(8,128)(2,1)S(1)} %slice_bitcast_fusion.1), channel_id=1, source_target_pairs={{0,2},{1,3},{2,4},{3,5},{4,6},{5,7},{6,0},{7,1},{8,10},{9,11},{10,... | collective-permute-start | bytes 405512 | tf_op jit(solution)/shard_map/ppermute | solution.py:238
  25.9 0.5 collective-permute-start.11
  26.5 5.2 %collective-permute-done.2.refs_1_ = bf16[2,528,128]{2,1,0:T(8,128)(2,1)S(1)} collective-permute-done((bf16[2,528,128]{2,1,0:T(8,128)(2,1)S(1)}, bf16[2,528,128]{2,1,0:T(8,128)(2,1)S(1)}, u32[]{:S(2)}, u32[]{:S(2)}) %collective-permute-start.2) | collective-permute-done | bytes 270368 | tf_op jit(solution)/shard_map/ppermute | solution.py:238
  31.6 1.7 %collective-permute-start.4 = (bf16[528,128]{1,0:T(8,128)(2,1)S(1)}, bf16[528,128]{1,0:T(8,128)(2,1)S(1)}, u32[]{:S(2)}, u32[]{:S(2)}) collective-permute-start(bf16[528,128]{1,0:T(8,128)(2,1)S(1)} %slice_bitcast_fusion.3), channel_id=1, source_target_pairs={{0,2},{1,3},{2,4},{3,5},{4,6},{5,7},{6,0},{7,1},{8,10},{9,11},{10,... | collective-permute-start | bytes 405512 | tf_op jit(solution)/shard_map/ppermute | solution.py:238
  33.3 0.5 collective-permute-start.5
  34.3 1.5 %collective-permute-done.11.refs_4_ = bf16[528,128]{1,0:T(8,128)(2,1)S(1)} collective-permute-done((bf16[528,128]{1,0:T(8,128)(2,1)S(1)}, bf16[528,128]{1,0:T(8,128)(2,1)S(1)}, u32[]{:S(2)}, u32[]{:S(2)}) %collective-permute-start.11) | collective-permute-done | bytes 135200 | tf_op jit(solution)/shard_map/ppermute | solution.py:238
  35.8 1.0 %shard_map.109 = (f32[512,256]{1,0:T(8,128)S(1)}, f32[512,128]{1,0:T(8,128)S(1)}) custom-call(s32[4]{0:T(128)S(1)} %pad_add_fusion.place_ref, bf16[2,528,128]{2,1,0:T(8,128)(2,1)S(1)} %pad_maximum_fusion.1.refs_0_, bf16[2,528,128]{2,1,0:T(8,128)(2,1)S(1)} %collective-permute-done.8.refs_1_, bf16[2,528,128]{2,1,0:T(8,128)(2,1)S(1)} %collective-permute-done.9.refs_2_, ...), custom_call_target="tpu_custom_call" | custom-call | flops 268435456 | bytes 2129936 | tf_op jit(solution)/shard_map/pallas_call | solution.py:208
  36.8 1.6 %collective-permute-done.5.refs_4_ = bf16[528,128]{1,0:T(8,128)(2,1)S(1)} collective-permute-done((bf16[528,128]{1,0:T(8,128)(2,1)S(1)}, bf16[528,128]{1,0:T(8,128)(2,1)S(1)}, u32[]{:S(2)}, u32[]{:S(2)}) %collective-permute-start.5) | collective-permute-done | bytes 135200 | tf_op jit(solution)/shard_map/ppermute | solution.py:238
  38.4 1.2 %shard_map.110 = bf16[16,128,128]{2,1,0:T(8,128)(2,1)S(1)} custom-call(s32[4]{0:T(128)S(1)} %pad_add_fusion.place_ref, bf16[2,528,128]{2,1,0:T(8,128)(2,1)S(1)} %pad_maximum_fusion.refs_0_, bf16[2,528,128]{2,1,0:T(8,128)(2,1)S(1)} %collective-permute-done.2.refs_1_, bf16[2,528,128]{2,1,0:T(8,128)(2,1)S(1)} %collective-permute-done.3.refs_2_, ...), custom_call_target="tpu_custom_call" | custom-call | flops 268435456 | bytes 3178512 | tf_op jit(solution)/shard_map/pallas_call | solution.py:208
  39.6 19.2 %all_to_all.10.value_ref.own_ref = bf16[16,128,128]{2,1,0:T(8,128)(2,1)S(1)} all-to-all(bf16[16,128,128]{2,1,0:T(8,128)(2,1)S(1)} %shard_map.110), channel_id=1, replica_groups=mesh['ctx'=16,'tp'=16] {'ctx'}, dimensions={0} | all-to-all | bytes 1048576 | tf_op jit(solution)/shard_map/all_to_all | solution.py:307
  59.2 1.3 %collective-permute-done.12.other_ref = bf16[16,32,128]{2,1,0:T(8,128)(2,1)S(1)} collective-permute-done((bf16[16,32,128]{2,1,0:T(8,128)(2,1)S(1)}, bf16[16,32,128]{2,1,0:T(8,128)(2,1)S(1)}, u32[]{:S(2)}, u32[]{:S(2)}) %collective-permute-start.12) | collective-permute-done | bytes 131104 | tf_op jit(solution)/shard_map/ppermute | solution.py:238
  60.5 3.2 %shard_map.112 = bf16[16,64,128]{2,1,0:T(8,128)(2,1)S(1)} custom-call(s32[4]{0:T(128)S(1)} %pad_add_fusion.place_ref, bf16[16,128,128]{2,1,0:T(8,128)(2,1)S(1)} %all_to_all.10.value_ref.own_ref, bf16[16,32,128]{2,1,0:T(8,128)(2,1)S(1)} %collective-permute-done.12.other_ref, bf16[2,256,256]{2,1,0:T(8,128)(2,1)S(1)} %copy-done.2, ...), custom_call_target="tpu_custom_call" | custom-call | flops 3000000000 | bytes 1703952 | tf_op jit(solution)/shard_map/pallas_call | solution.py:208
  63.7 14.2 %all_to_all.11.blocks_ref = bf16[16,64,128]{2,1,0:T(8,128)(2,1)S(1)} all-to-all(bf16[16,64,128]{2,1,0:T(8,128)(2,1)S(1)} %shard_map.112), channel_id=1, replica_groups=mesh['ctx'=16,'tp'=16] {'ctx'}, dimensions={0} | all-to-all | bytes 524288 | tf_op jit(solution)/shard_map/all_to_all | solution.py:319
  77.9 0.8 %shard_map.113 = bf16[1024,128]{1,0:T(8,128)(2,1)} custom-call(bf16[16,64,128]{2,1,0:T(8,128)(2,1)S(1)} %all_to_all.11.blocks_ref), custom_call_target="tpu_custom_call" | custom-call | bytes 262144 | tf_op jit(solution)/shard_map/pallas_call | solution.py:208
  (42 shorter events, 1.8 us)
Async XLA Ops:
  0.0 9.6 %copy-start = (f32[24,1024]{1,0:T(8,128)S(1)}, f32[24,1024]{1,0:T(8,128)}, u32[]{:S(2)}) copy-start(f32[24,1024]{1,0:T(8,128)} %param.14) | copy-start | bytes 294916
  0.0 9.2 %copy-start.1 = (bf16[2048,128]{1,0:T(8,128)(2,1)S(1)}, bf16[2048,128]{1,0:T(8,128)(2,1)}, u32[]{:S(2)}) copy-start(bf16[2048,128]{1,0:T(8,128)(2,1)} %refs_5_.3) | copy-start | bytes 1572868
  1.1 0.7 copy-start.9
  1.7 7.8 %copy-start.7 = (bf16[24,128]{1,0:T(8,128)(2,1)S(1)}, bf16[24,128]{1,0:T(8,128)(2,1)}, u32[]{:S(2)}) copy-start(bf16[24,128]{1,0:T(8,128)(2,1)} %param.15) | copy-start | bytes 18436
  1.8 8.2 %collective-permute-start.7 = (bf16[528,128]{1,0:T(8,128)(2,1)S(1)}, bf16[528,128]{1,0:T(8,128)(2,1)S(1)}, u32[]{:S(2)}, u32[]{:S(2)}) collective-permute-start(bf16[528,128]{1,0:T(8,128)(2,1)S(1)} %get-tuple-element.13), channel_id=1, source_target_pairs={{0,1},{1,0},{2,3},{3,2},{4,5},{5,4},{6,7},{7,6},{8,9},{9,8},{10,11... | collective-permute-start | bytes 405512 | tf_op jit(solution)/shard_map/ppermute | solution.py:238
  1.9 20.2 %collective-permute-start.1 = (bf16[528,128]{1,0:T(8,128)(2,1)S(1)}, bf16[528,128]{1,0:T(8,128)(2,1)S(1)}, u32[]{:S(2)}, u32[]{:S(2)}) collective-permute-start(bf16[528,128]{1,0:T(8,128)(2,1)S(1)} %get-tuple-element.13), channel_id=1, source_target_pairs={{0,9},{1,8},{2,11},{3,10},{4,13},{5,12},{6,15},{7,14},{8,1},{9,0},... | collective-permute-start | bytes 405512 | tf_op jit(solution)/shard_map/ppermute | solution.py:238
  9.2 24.7 %collective-permute-start.6 = (bf16[2048,128]{1,0:T(8,128)(2,1)S(1)}, bf16[2048,128]{1,0:T(8,128)(2,1)S(1)}, u32[]{:S(2)}, u32[]{:S(2)}) collective-permute-start(bf16[2048,128]{1,0:T(8,128)(2,1)S(1)} %copy-done.1), channel_id=1, source_target_pairs={{0,1},{1,0},{2,3},{3,2},{4,5},{5,4},{6,7},{7,6},{8,9},{9,8},{10,11... | collective-permute-start | bytes 1572872 | tf_op jit(solution)/shard_map/ppermute | solution.py:238
  9.3 12.8 %collective-permute-start = (bf16[528,128]{1,0:T(8,128)(2,1)S(1)}, bf16[528,128]{1,0:T(8,128)(2,1)S(1)}, u32[]{:S(2)}, u32[]{:S(2)}) collective-permute-start(bf16[528,128]{1,0:T(8,128)(2,1)S(1)} %get-tuple-element.12), channel_id=1, source_target_pairs={{0,8},{1,9},{2,10},{3,11},{4,12},{5,13},{6,14},{7,15},{8,0},{9,1},... | collective-permute-start | bytes 405512 | tf_op jit(solution)/shard_map/ppermute | solution.py:238
  10.0 14.2 %collective-permute-start.8 = (bf16[2,528,128]{2,1,0:T(8,128)(2,1)S(1)}, bf16[2,528,128]{2,1,0:T(8,128)(2,1)S(1)}, u32[]{:S(2)}, u32[]{:S(2)}) collective-permute-start(bf16[2,528,128]{2,1,0:T(8,128)(2,1)S(1)} %pad_maximum_fusion.1.refs_0_), channel_id=1, source_target_pairs={{0,2},{1,3},{2,4},{3,5},{4,6},{5,7},{6,0},{7,1},{8,10},{9,11},{10,... | collective-permute-start | bytes 811016 | tf_op jit(solution)/shard_map/ppermute | solution.py:238
  11.7 0.7 copy-start.8
  12.8 13.1 %collective-permute-start.9 = (bf16[2,528,128]{2,1,0:T(8,128)(2,1)S(1)}, bf16[2,528,128]{2,1,0:T(8,128)(2,1)S(1)}, u32[]{:S(2)}, u32[]{:S(2)}) collective-permute-start(bf16[2,528,128]{2,1,0:T(8,128)(2,1)S(1)} %pad_maximum_fusion.1.refs_0_), channel_id=1, source_target_pairs={{0,6},{1,7},{2,0},{3,1},{4,2},{5,3},{6,4},{7,5},{8,14},{9,15},{10,... | collective-permute-start | bytes 811016 | tf_op jit(solution)/shard_map/ppermute | solution.py:238
  22.1 9.5 %collective-permute-start.2 = (bf16[2,528,128]{2,1,0:T(8,128)(2,1)S(1)}, bf16[2,528,128]{2,1,0:T(8,128)(2,1)S(1)}, u32[]{:S(2)}, u32[]{:S(2)}) collective-permute-start(bf16[2,528,128]{2,1,0:T(8,128)(2,1)S(1)} %pad_maximum_fusion.refs_0_), channel_id=1, source_target_pairs={{0,2},{1,3},{2,4},{3,5},{4,6},{5,7},{6,0},{7,1},{8,10},{9,11},{10,... | collective-permute-start | bytes 811016 | tf_op jit(solution)/shard_map/ppermute | solution.py:238
  23.8 9.5 %collective-permute-start.3 = (bf16[2,528,128]{2,1,0:T(8,128)(2,1)S(1)}, bf16[2,528,128]{2,1,0:T(8,128)(2,1)S(1)}, u32[]{:S(2)}, u32[]{:S(2)}) collective-permute-start(bf16[2,528,128]{2,1,0:T(8,128)(2,1)S(1)} %pad_maximum_fusion.refs_0_), channel_id=1, source_target_pairs={{0,6},{1,7},{2,0},{3,1},{4,2},{5,3},{6,4},{7,5},{8,14},{9,15},{10,... | collective-permute-start | bytes 811016 | tf_op jit(solution)/shard_map/ppermute | solution.py:238
  24.3 10.0 %collective-permute-start.10 = (bf16[528,128]{1,0:T(8,128)(2,1)S(1)}, bf16[528,128]{1,0:T(8,128)(2,1)S(1)}, u32[]{:S(2)}, u32[]{:S(2)}) collective-permute-start(bf16[528,128]{1,0:T(8,128)(2,1)S(1)} %slice_bitcast_fusion.1), channel_id=1, source_target_pairs={{0,2},{1,3},{2,4},{3,5},{4,6},{5,7},{6,0},{7,1},{8,10},{9,11},{10,... | collective-permute-start | bytes 405512 | tf_op jit(solution)/shard_map/ppermute | solution.py:238
  25.9 9.8 %collective-permute-start.11 = (bf16[528,128]{1,0:T(8,128)(2,1)S(1)}, bf16[528,128]{1,0:T(8,128)(2,1)S(1)}, u32[]{:S(2)}, u32[]{:S(2)}) collective-permute-start(bf16[528,128]{1,0:T(8,128)(2,1)S(1)} %slice_bitcast_fusion), channel_id=1, source_target_pairs={{0,6},{1,7},{2,0},{3,1},{4,2},{5,3},{6,4},{7,5},{8,14},{9,15},{10,... | collective-permute-start | bytes 405512 | tf_op jit(solution)/shard_map/ppermute | solution.py:238
  31.6 5.1 %collective-permute-start.4 = (bf16[528,128]{1,0:T(8,128)(2,1)S(1)}, bf16[528,128]{1,0:T(8,128)(2,1)S(1)}, u32[]{:S(2)}, u32[]{:S(2)}) collective-permute-start(bf16[528,128]{1,0:T(8,128)(2,1)S(1)} %slice_bitcast_fusion.3), channel_id=1, source_target_pairs={{0,2},{1,3},{2,4},{3,5},{4,6},{5,7},{6,0},{7,1},{8,10},{9,11},{10,... | collective-permute-start | bytes 405512 | tf_op jit(solution)/shard_map/ppermute | solution.py:238
  33.3 5.1 %collective-permute-start.5 = (bf16[528,128]{1,0:T(8,128)(2,1)S(1)}, bf16[528,128]{1,0:T(8,128)(2,1)S(1)}, u32[]{:S(2)}, u32[]{:S(2)}) collective-permute-start(bf16[528,128]{1,0:T(8,128)(2,1)S(1)} %slice_bitcast_fusion.2), channel_id=1, source_target_pairs={{0,6},{1,7},{2,0},{3,1},{4,2},{5,3},{6,4},{7,5},{8,14},{9,15},{10,... | collective-permute-start | bytes 405512 | tf_op jit(solution)/shard_map/ppermute | solution.py:238
  39.6 20.9 %copy-start.4 = (bf16[2,256,256]{2,1,0:T(8,128)(2,1)S(1)}, bf16[2,256,256]{2,1,0:T(8,128)(2,1)}, u32[]{:S(2)}) copy-start(bf16[2,256,256]{2,1,0:T(8,128)(2,1)} %constant.68.clone.back_ref) | copy-start | bytes 786436
  39.6 20.9 %copy-start.6 = (bf16[2,128,256]{2,1,0:T(8,128)(2,1)S(1)}, bf16[2,128,256]{2,1,0:T(8,128)(2,1)}, u32[]{:S(2)}) copy-start(bf16[2,128,256]{2,1,0:T(8,128)(2,1)} %constant.69.clone.last_ref) | copy-start | bytes 393220
  58.9 1.6 %copy-start.2 = (bf16[2,256,256]{2,1,0:T(8,128)(2,1)S(1)}, bf16[2,256,256]{2,1,0:T(8,128)(2,1)}, u32[]{:S(2)}) copy-start(bf16[2,256,256]{2,1,0:T(8,128)(2,1)} %constant.65.clone.first_ref) | copy-start | bytes 786436
  58.9 1.6 %copy-start.3 = (bf16[2,256,256]{2,1,0:T(8,128)(2,1)S(1)}, bf16[2,256,256]{2,1,0:T(8,128)(2,1)}, u32[]{:S(2)}) copy-start(bf16[2,256,256]{2,1,0:T(8,128)(2,1)} %constant.67.clone.second_ref) | copy-start | bytes 786436
  58.9 1.7 %copy-start.5 = (f32[2,128,128]{2,1,0:T(8,128)S(1)}, f32[2,128,128]{2,1,0:T(8,128)}, u32[]{:S(2)}) copy-start(f32[2,128,128]{2,1,0:T(8,128)} %constant.66.clone.turn_ref) | copy-start | bytes 393220
  58.9 1.6 %collective-permute-start.12 = (bf16[16,32,128]{2,1,0:T(8,128)(2,1)S(1)}, bf16[16,32,128]{2,1,0:T(8,128)(2,1)S(1)}, u32[]{:S(2)}, u32[]{:S(2)}) collective-permute-start(bf16[16,32,128]{2,1,0:T(8,128)(2,1)S(1)} %shard_map.111), channel_id=1, source_target_pairs={{0,1},{1,0},{2,3},{3,2},{4,5},{5,4},{6,7},{7,6},{8,9},{9,8},{10,11... | collective-permute-start | bytes 393224 | tf_op jit(solution)/shard_map/ppermute | solution.py:238
